TPU v7x, 32 devices: a whole 2x2x4 slice. The times are simulated.
32 devices in a mesh: stream: 2 (over x), wide: 8 (over z, y), narrow: 2 (over core).
Axes of the slice: x: 2, y: 2, z: 4, core: 2. Of those that a mesh axis runs over, the one named last changes fastest.
Arguments:
- frames: bfloat16 [2, 64, 13, 13, 256], P('stream', ('wide', 'narrow')), may hold values from -6 to 6
- weight3: bfloat16 [2, 2304, 512], P('stream'), may hold values from -0.125 to 0.125
- bias3: bfloat16 [2, 512], P('stream'), may hold values from -3 to 3
- weight4: bfloat16 [2, 4608, 512], P('stream'), may hold values from -0.125 to 0.125
- bias4: bfloat16 [2, 512], P('stream'), may hold values from -3 to 3
- cotangent: bfloat16 [2, 64, 13, 13, 512], P('stream', ('wide', 'narrow')), may hold values from -6 to 6
- clip_counts: int32 [8], replicated, may hold values from 1 to 25, 64 in all
Outputs:
- activations: bfloat16 [2, 64, 13, 13, 512], P('stream', ('wide', 'narrow'))
- frames_grad: bfloat16 [2, 64, 13, 13, 256], P('stream', ('wide', 'narrow'))
- weight3_grad: float32 [2, 2304, 512], P('stream')
- bias3_grad: float32 [2, 512], P('stream')
- weight4_grad: float32 [2, 4608, 512], P('stream')
- bias4_grad: float32 [2, 512], P('stream')
Inputs may be any that keep to these rules, and one draw needn't show every extreme that they name: `clip_counts`: the counts sum to 64; the largest is exactly 25.
All inputs are finite; a program needn't handle non-finite values.
Results may differ from a plain program's by a relative error of at most 0.0062.
Values sent between devices are 32-bit elements; how exact they have to be, the bound alone decides.
No kernel may reach another device: no remote copies, remote signals or barrier semaphores. Data moves between devices by JAX's collectives and lax.ppermute only.
A program may use at most 128 MiB of HBM per device.

v0:
```python
import jax
import jax.numpy as jnp
from jax import lax
from jax.sharding import PartitionSpec as P


def columns(field):
    count, side = (field.shape[0], field.shape[1])
    padded = jnp.pad(field, ((0, 0), (1, 1), (1, 1), (0, 0)))
    pieces = [padded[:, r : r + side, c : c + side, :] for r in range(3) for c in range(3)]
    return jnp.concatenate(pieces, axis=-1).reshape(count * side * side, -1)


def flipped(weight, c_in, c_out):
    kernel = weight.reshape(3, 3, c_in, c_out)[::-1, ::-1]
    return jnp.transpose(kernel, (0, 1, 3, 2)).reshape(9 * c_out, c_in)


def silu_slope(value):
    sigma = jax.nn.sigmoid(value)
    return sigma * (1.0 + value * (1.0 - sigma))


def contract_rows(left, right):
    return lax.dot_general(
        left, right, (((0,), (0,)), ((), ())), preferred_element_type=jnp.float32
    )


def reduce_grads(grads):
    shares = (
        lax.psum_scatter(grads[0], "wide", scatter_dimension=0, tiled=True),
        lax.psum_scatter(grads[1], "wide", scatter_dimension=0, tiled=True),
        lax.psum_scatter(grads[2], "wide", scatter_dimension=0, tiled=True),
        lax.psum_scatter(grads[3], "wide", scatter_dimension=0, tiled=True),
    )
    shares = lax.psum((shares[0], shares[1], shares[2], shares[3]), "narrow")
    return (
        lax.all_gather(shares[0], "wide", axis=0, tiled=True),
        lax.all_gather(shares[1], "wide", axis=0, tiled=True),
        lax.all_gather(shares[2], "wide", axis=0, tiled=True),
        lax.all_gather(shares[3], "wide", axis=0, tiled=True),
    )


def body(frames, weight3, bias3, weight4, bias4, cotangent, clip_counts):
    field = frames[0]
    count, side, c_in = (field.shape[0], field.shape[1], field.shape[3])
    w_three, w_four = (weight3[0], weight4[0])
    c_mid, c_out = (w_three.shape[1], w_four.shape[1])
    rows = count * side * side
    total_frames = count * lax.axis_size("wide") * lax.axis_size("narrow")
    videos = clip_counts.shape[0]
    first = lax.axis_index(("wide", "narrow")) * count
    index = first + jnp.arange(count, dtype=jnp.int32)
    ends = jnp.cumsum(clip_counts)
    starts = ends - clip_counts
    inside = (index[:, None] >= starts[None, :]) & (index[:, None] < ends[None, :])
    owned = jnp.sum(jnp.where(inside, clip_counts[None, :], 0), axis=1)
    scale = total_frames / (videos * owned.astype(jnp.float32))
    cols_three = columns(field)
    pre3 = jnp.dot(cols_three, w_three, preferred_element_type=jnp.float32) + bias3[0].astype(
        jnp.float32
    )
    act3 = jax.nn.silu(pre3).astype(jnp.bfloat16)
    cols_four = columns(act3.reshape(count, side, side, c_mid))
    pre4 = jnp.dot(cols_four, w_four, preferred_element_type=jnp.float32) + bias4[0].astype(
        jnp.float32
    )
    output = jax.nn.silu(pre4).astype(jnp.bfloat16)
    weighted = cotangent[0].astype(jnp.float32) * scale[:, None, None, None]
    delta4 = (weighted.reshape(rows, c_out) * silu_slope(pre4)).astype(jnp.bfloat16)
    grad_w4 = contract_rows(cols_four, delta4)
    grad_b4 = jnp.sum(delta4, axis=0, dtype=jnp.float32)
    spread4 = columns(delta4.reshape(count, side, side, c_out))
    back3 = jnp.dot(spread4, flipped(w_four, c_mid, c_out), preferred_element_type=jnp.float32)
    delta3 = (back3 * silu_slope(pre3)).astype(jnp.bfloat16)
    grad_w3 = contract_rows(cols_three, delta3)
    grad_b3 = jnp.sum(delta3, axis=0, dtype=jnp.float32)
    spread3 = columns(delta3.reshape(count, side, side, c_mid))
    back_in = jnp.dot(spread3, flipped(w_three, c_in, c_mid), preferred_element_type=jnp.float32)
    field_grad = back_in.astype(jnp.bfloat16).reshape(count, side, side, c_in)
    late_w3, late_b3, late_w4, late_b4 = reduce_grads((grad_w3, grad_b3, grad_w4, grad_b4))
    return (
        output.reshape(count, side, side, c_out)[None],
        field_grad[None],
        late_w3[None],
        late_b3[None],
        late_w4[None],
        late_b4[None],
    )


def solution(mesh):
    return jax.shard_map(
        body,
        mesh=mesh,
        in_specs=(
            P("stream", ("wide", "narrow"), None, None, None),
            P("stream", None, None),
            P("stream", None),
            P("stream", None, None),
            P("stream", None),
            P("stream", ("wide", "narrow"), None, None, None),
            P(),
        ),
        out_specs=(
            P("stream", ("wide", "narrow"), None, None, None),
            P("stream", ("wide", "narrow"), None, None, None),
            P("stream", None, None),
            P("stream", None),
            P("stream", None, None),
            P("stream", None),
        ),
        check_vma=False,
    )
```

profile of v0, /device:TPU:0, one launch (start us, length us, event | category | flops | bytes accessed | tf_op | source)
XLA Modules:
  0.0 666.0 jit_solution(11948454283094423143)
XLA Ops:
  10.7 1.9 pad_slice_fusion.24
  23.8 1.8 constant_dynamic-update-slice_fusion.6
  35.3 4.9 multiply_convert_fusion.2
  42.2 6.0 pad_slice_fusion.16
  48.2 2.1 concatenate.92
  50.3 2.1 constant_dynamic-update-slice_fusion.17
  52.4 2.1 concatenate.93
  54.5 2.2 concatenate.94
  56.7 2.1 concatenate.95
  58.9 2.1 constant_dynamic-update-slice_fusion.16
  61.0 2.1 constant_dynamic-update-slice_fusion.15
  63.0 2.0 constant_dynamic-update-slice_fusion.14
  65.0 2.0 constant_dynamic-update-slice_fusion.13
  70.7 2.0 constant_dynamic-update-slice_fusion.11
  74.6 8.9 %convert_reduce_fusion = (f32[512]{0:T(512)S(1)}, bf16[676,512]{1,0:T(8,128)(2,1)S(1)}, bf16[676,512]{1,0:T(8,128)(2,1)}) fusion(f32[676,512]{1,0:T(8,128)S(1)} %copy-done.16, f32[676]{0:T(1024)S(1)} %mul.57, f32[512]{0:T(512)S(1)} %bitcast.51, bf16[676,4608]{1,0:T(8,128)(2,1)} %constant_dynamic-update-slice_fusion.9, bf16[1,4608,512]{2,1,0:T(8,128)(2,1)} %param.10), kind=kOutput, calls=%fused_computation.7 | convolution fusion | flops 3194959360 | bytes 13724304 | tf_op jit(solution)/shard_map/dot_general | solution.py:67
  85.5 6.1 pad_slice_fusion.8
  91.6 2.1 concatenate.101
  93.7 2.0 constant_dynamic-update-slice_fusion.26
  95.7 2.1 concatenate.102
  97.8 2.2 concatenate.103
  100.0 2.1 concatenate.104
  102.2 2.0 constant_dynamic-update-slice_fusion.25
  104.2 2.0 constant_dynamic-update-slice_fusion.24
  106.2 2.0 constant_dynamic-update-slice_fusion.23
  108.2 2.0 constant_dynamic-update-slice_fusion.22
  112.0 4.8 reverse_bitcast_fusion
  116.8 6.8 %copy.66 = bf16[3,3,512,512]{3,2,1,0:T(8,128)(2,1)} copy(bf16[3,3,512,512]{2,3,1,0:T(8,128)(2,1)} %reverse_bitcast_fusion) | data formatting | bytes 9437184 | tf_op jit(solution)/shard_map/transpose | solution.py:16
  127.2 7.0 %convert_reduce_fusion.1 = (f32[512]{0:T(512)S(1)}, bf16[676,512]{1,0:T(8,128)(2,1)S(1)}) fusion(f32[676,512]{1,0:T(8,128)} %get-tuple-element.82, bf16[676,4608]{1,0:T(8,128)(2,1)} %constant_dynamic-update-slice_fusion.18, bf16[4608,512]{1,0:T(8,128)(2,1)S(1)} %bitcast.47), kind=kOutput, calls=%fused_computation.8 | convolution fusion | flops 3193574912 | bytes 13027328 | tf_op jit(solution)/shard_map/dot_general | solution.py:76
  134.2 4.2 fusion.12
  139.6 9.2 %fusion.13 = f32[4608,512]{1,0:T(8,128)} fusion(bf16[676,4608]{1,0:T(8,128)(2,1)} %constant_dynamic-update-slice_fusion.9, bf16[676,512]{1,0:T(8,128)(2,1)S(1)} %copy-done.6), kind=kOutput, calls=%fused_computation.92 | convolution fusion | flops 3189768192 | bytes 16359424 | tf_op jit(solution)/shard_map/dot_general | solution.py:25
  148.9 87.7 %reduce-scatter.3.cloned.1.call-done = f32[288,512]{1,0:T(8,128)} async-done(((f32[2304,512]{1,0:T(8,128)}), f32[288,512]{1,0:T(8,128)}) %reduce-scatter.3.cloned.1.call-update) | async-done | bytes 589840 | tf_op jit(solution)/shard_map/reduce_scatter | solution.py:32
  236.6 167.3 %reduce-scatter.5.cloned.1.call-done = f32[576,512]{1,0:T(8,128)} async-done(((f32[4608,512]{1,0:T(8,128)}), f32[576,512]{1,0:T(8,128)}) %reduce-scatter.5.cloned.1.call-update) | async-done | bytes 1179664 | tf_op jit(solution)/shard_map/reduce_scatter | solution.py:34
  403.9 22.2 %all-reduce.14.cloned.1.call-done = (f32[288,512]{1,0:T(8,128)}, f32[576,512]{1,0:T(8,128)}) async-done(((f32[288,512]{1,0:T(8,128)}, f32[576,512]{1,0:T(8,128)}), (f32[288,512]{1,0:T(8,128)}, f32[576,512]{1,0:T(8,128)})) %all-reduce.14.cloned.1.call-update) | async-done | bytes 1769488 | tf_op jit(solution)/shard_map/psum | solution.py:37
  428.7 3.1 pad_slice_fusion
  431.8 2.3 concatenate.110
  434.0 2.2 concatenate.111
  436.2 2.2 concatenate.112
  438.4 2.2 concatenate.113
  445.0 1.9 reverse_bitcast_fusion.1
  446.9 2.4 copy.67
  454.7 1.8 convolution_convert_fusion
  458.8 22.4 %all-reduce.9 = (f32[512]{0:T(512)S(1)}, f32[512]{0:T(512)S(1)}) all-reduce(f32[512]{0:T(512)S(1)} %get-tuple-element.83, f32[512]{0:T(512)S(1)} %get-tuple-element.44), channel_id=3, replica_groups=mesh['stream'=2,'wide'=8,'narrow'=2] {'wide'}, use_global_device_ids=true, to_apply=%region_5.6.clone | all-reduce | flops 1024 | bytes 8192
  482.0 2.5 all-reduce.10
  484.9 18.0 %all-reduce.8 = (f32[512]{0:T(512)}, f32[512]{0:T(512)}) all-reduce(f32[512]{0:T(512)S(1)} %dynamic-update-slice, f32[512]{0:T(512)S(1)} %dynamic-update-slice.1), channel_id=1, replica_groups=mesh['stream'=2,'wide'=8,'narrow'=2] {'wide'}, use_global_device_ids=true, to_apply=%add.4 | all-reduce | flops 1024 | bytes 8192
  502.9 7.3 %all-gather.3.cloned.1.call-done = f32[2304,512]{1,0:T(8,128)} async-done(((f32[288,512]{1,0:T(8,128)}), f32[2304,512]{1,0:T(8,128)}) %all-gather.3.cloned.1.call-update) | async-done | bytes 4718608 | tf_op jit(solution)/shard_map/all_gather | solution.py:39
  510.2 138.7 %all-gather.5.cloned.1.call-done = f32[4608,512]{1,0:T(8,128)} async-done(((f32[576,512]{1,0:T(8,128)}), f32[4608,512]{1,0:T(8,128)}) %all-gather.5.cloned.1.call-update) | async-done | bytes 9437200 | tf_op jit(solution)/shard_map/all_gather | solution.py:41
  648.9 5.4 copy.108
  655.7 3.7 copy.109
  (139 shorter events, 56.0 us)
Async XLA Ops:
  7.2 2.8 copy-start.24
  7.2 3.4 copy-start.22
  7.2 3.4 copy-start.23
  7.2 3.4 copy-start.18
  7.2 229.4 %reduce-scatter.3.cloned.1.call-start = ((), (), s32[]{:S(2)}) async-start(), calls=%async_computation.2 | async-start | bytes 5308416 | tf_op jit(solution)/shard_map/reduce_scatter | solution.py:32
  18.4 17.0 %copy-start.14 = (bf16[1,2304,512]{2,1,0:T(8,128)(2,1)S(1)}, bf16[1,2304,512]{2,1,0:T(8,128)(2,1)}, u32[]{:S(2)}) copy-start(bf16[1,2304,512]{2,1,0:T(8,128)(2,1)} %param.8) | copy-start | bytes 7077892
  23.0 11.5 %copy-start.17 = (bf16[676,256]{1,0:T(8,128)(2,1)S(1)}, bf16[676,256]{1,0:T(8,128)(2,1)}, u32[]{:S(2)}) copy-start(bf16[676,256]{1,0:T(8,128)(2,1)} %concatenate.90) | copy-start | bytes 1038340
  40.2 0.9 copy-start.7
  68.2 1.6 copy-start.13
  69.8 4.8 copy-start.16
  83.5 0.9 copy-start.5
  116.8 6.8 %copy-start.12 = (bf16[676,512]{1,0:T(8,128)(2,1)S(1)}, bf16[676,512]{1,0:T(8,128)(2,1)}, u32[]{:S(2)}) copy-start(bf16[676,512]{1,0:T(8,128)(2,1)} %concatenate.105) | copy-start | bytes 2076676
  123.6 3.6 copy-start.1
  127.2 7.0 %copy-start.20 = (bf16[676,2304]{1,0:T(8,128)(2,1)S(1)}, bf16[676,2304]{1,0:T(8,128)(2,1)}, u32[]{:S(2)}) copy-start(bf16[676,2304]{1,0:T(8,128)(2,1)} %constant_dynamic-update-slice_fusion) | copy-start | bytes 9345028
  134.2 292.5 %copy-start.3 = (bf16[676,512]{1,0:T(8,128)(2,1)}, bf16[676,512]{1,0:T(8,128)(2,1)S(1)}, u32[]{:S(2)}) copy-start(bf16[676,512]{1,0:T(8,128)(2,1)S(1)} %get-tuple-element.84) | copy-start | bytes 2076676
  138.5 1.1 copy-start.6
  138.5 265.4 %reduce-scatter.5.cloned.1.call-start = ((), (), s32[]{:S(2)}) async-start(), calls=%async_computation.4 | async-start | bytes 10616832 | tf_op jit(solution)/shard_map/reduce_scatter | solution.py:34
  148.8 278.2 %copy-start.19 = (bf16[676,512]{1,0:T(8,128)(2,1)S(1)}, bf16[676,512]{1,0:T(8,128)(2,1)}, u32[]{:S(2)}) copy-start(bf16[676,512]{1,0:T(8,128)(2,1)} %get-tuple-element.46) | copy-start | bytes 2076676
  148.8 277.3 %all-reduce.14.cloned.1.call-start = ((), (), s32[]{:S(2)}) async-start(), calls=%async_computation.6 | async-start | bytes 3538944 | tf_op jit(solution)/shard_map/psum | solution.py:37
  403.9 106.4 %all-gather.3.cloned.1.call-start = ((), (), s32[]{:S(2)}) async-start(), calls=%async_computation.3 | async-start | bytes 5308416 | tf_op jit(solution)/shard_map/all_gather | solution.py:39
  426.1 222.8 %all-gather.5.cloned.1.call-start = ((), (), s32[]{:S(2)}) async-start(), calls=%async_computation.5 | async-start | bytes 10616832 | tf_op jit(solution)/shard_map/all_gather | solution.py:41
  431.8 8.8 %copy-start.2 = (bf16[4,13,13,512]{3,2,1,0:T(8,128)(2,1)S(1)}, bf16[4,13,13,512]{3,2,1,0:T(8,128)(2,1)}, u32[]{:S(2)}) copy-start(bf16[4,13,13,512]{3,2,1,0:T(8,128)(2,1)} %get-tuple-element.51) | copy-start | bytes 2076676
  446.9 7.5 %copy-start.4 = (bf16[676,512]{1,0:T(8,128)(2,1)S(1)}, bf16[676,512]{1,0:T(8,128)(2,1)}, u32[]{:S(2)}) copy-start(bf16[676,512]{1,0:T(8,128)(2,1)} %copy-done.3) | copy-start | bytes 2076676
  449.3 5.1 copy-start.11
  449.3 5.2 copy-start.10
  449.3 5.2 copy-start.8
  450.6 4.0 copy-start.9
  451.9 2.8 copy-start.15
  454.7 2.9 copy-start.21
  648.9 6.8 %copy-start = (f32[4608,512]{1,0:T(8,128)S(1)}, f32[4608,512]{1,0:T(8,128)}, u32[]{:S(2)}) copy-start(f32[4608,512]{1,0:T(8,128)} %all-gather.5.cloned.1.call-done) | copy-start | bytes 28311556
Sparse Core Ops, SparseCore 0:
  138.6 97.9 reduce-scatter.2
  240.7 163.0 reduce-scatter.4
  406.3 19.8 all-reduce.13
  428.4 81.8 all-gather.2
  512.5 136.3 all-gather.4
where the time goes:
time: 668 us; the launch traced here: 666 us
  waiting for transfers between devices  424 us (63%)
  local copies, waits for them, and re-layouts  147 us (22%)
  blocking collectives  42.9 us (6%)
  matrix products  36 us (5%)
  between operations  15.6 us (2%)
    reduce_scatter x1, waiting for transfers between devices, reduce_grads(): lax.psum_scatter(grads[2], 'wide', scatter_dimension=0, tiled=True)  167 us
    all_gather x1, waiting for transfers between devices, reduce_grads(): lax.all_gather(shares[2], 'wide', axis=0, tiled=True)  139 us
    reduce_scatter x1, waiting for transfers between devices, reduce_grads(): lax.psum_scatter(grads[0], 'wide', scatter_dimension=0, tiled=True)  87.7 us
    unnamed x94, local copies, waits for them, and re-layouts  61.1 us
    concatenate x37, local copies, waits for them, and re-layouts, columns(): return jnp.concatenate(pieces, axis=-1).reshape(count * side * side, -1)  43.8 us
    unnamed x2, blocking collectives  40.4 us
    psum x1, waiting for transfers between devices, reduce_grads(): shares = lax.psum((shares[0], shares[1], shares[2], shares[3]), 'narrow')  22.2 us
    slice x12, local copies, waits for them, and re-layouts, columns(): padded[:, r:r + side, c:c + side, :]  20.5 us
  transfers between devices with their start and end apart: 5, of which 5 were waited for; matrix products, arithmetic and copies ran while one was open for 6% of the time, Pallas kernels for 0%

commit v1 on v0

v1 whole, which is shorter than its diff:
```python
import functools

import jax
import jax.numpy as jnp
from jax import lax
from jax.experimental import pallas as pl
from jax.experimental.pallas import tpu as pltpu
from jax.sharding import PartitionSpec as P

BF16 = jnp.bfloat16
F32 = jnp.float32
STEP = 16
MIB = 1024 * 1024
HEAD_MIB, BACK4_MIB, BACK3_MIB = 60, 62, 16
HBM = pl.BlockSpec(memory_space=pltpu.HBM)


def own_place(size):
    core, wide = lax.axis_index("narrow"), lax.axis_index("wide")
    half = lax.div(wide, 2)
    return core, jnp.where(lax.rem(wide, 2) == 0, half, size - 1 - half), 1 - 2 * core


def kernel_call(kernel, outs, scratch, mib, flops, *args, aliases={}):
    return pl.pallas_call(
        kernel,
        out_shape=outs,
        in_specs=[HBM] * len(args),
        out_specs=jax.tree.map(lambda _: HBM, outs),
        scratch_shapes=scratch,
        input_output_aliases=aliases,
        compiler_params=pltpu.CompilerParams(vmem_limit_bytes=mib * MIB),
        cost_estimate=pl.CostEstimate(flops=flops, bytes_accessed=8 * MIB, transcendentals=0),
    )(*args)


def spread(value, cat_ref, count):
    rows, width = value.shape
    edge = count * STEP
    for at, shift in enumerate((count, 0, rows - count)):
        moved = value if shift == 0 else pltpu.roll(value, shift, 0)
        cat_ref[edge : edge + rows, at * width : (at + 1) * width] = moved.astype(BF16)


def clear_edges(cat_ref, count):
    edge = count * STEP
    zeros = jnp.zeros((edge, cat_ref.shape[1]), cat_ref.dtype)
    cat_ref[0:edge, :] = zeros
    cat_ref[cat_ref.shape[0] - edge :, :] = zeros


def convolve_into(acc_ref, cat_ref, w_ref, edge):
    rows, width = acc_ref.shape[0], cat_ref.shape[1]
    for r in range(3):
        part = jnp.dot(
            cat_ref[r * edge : r * edge + rows, :],
            w_ref[r * width : (r + 1) * width, :],
            preferred_element_type=F32,
        )
        if r == 0:
            acc_ref[...] = part
        else:
            acc_ref[...] += part


def back_into(acc_ref, cat_ref, w_ref, edge):
    rows, width = acc_ref.shape[0], w_ref.shape[2]
    for r in range(3):
        for c in range(3):
            part = lax.dot_general(
                cat_ref[(2 - r) * edge : (2 - r) * edge + rows, (2 - c) * width : (3 - c) * width],
                w_ref[3 * r + c],
                (((1,), (1,)), ((), ())),
                preferred_element_type=F32,
            )
            if r + c == 0:
                acc_ref[...] = part
            else:
                acc_ref[...] += part


def silu_slope(value, sigma):
    return sigma * (1.0 + value * (1.0 - sigma))


def head_kernel(
    total, counts_hbm, frames_hbm, w3_hbm, b3_hbm, w4_hbm, b4_hbm, cot_hbm,
    out_hbm, mine_hbm, slope_hbm, field_mine_hbm, send_hbm,
    counts_ref, frames_ref, w3_ref, b3_ref, w4_ref, b4_ref, cot_ref,
    field_ref, act_ref, acc_ref, slope_ref, delta_ref, out_ref, block3_ref, block_ref, cat3_ref, cat4_ref,
    in_sems, out_sems,
):
    sources = (frames_hbm, counts_hbm, w3_hbm, b3_hbm, b4_hbm, w4_hbm, cot_hbm)
    targets = (frames_ref, counts_ref, w3_ref, b3_ref, b4_ref, w4_ref, cot_ref)
    loads = [
        pltpu.make_async_copy(source, target, in_sems.at[at])
        for at, (source, target) in enumerate(zip(sources, targets))
    ]
    for load in loads:
        load.start()
    side, count = frames_ref.shape[0], frames_ref.shape[2]
    edge = count * STEP
    valid = side * count
    videos = counts_ref.shape[0]
    half3, half4 = field_mine_hbm.shape[1], mine_hbm.shape[1]
    c_out = delta_ref.shape[1]
    delta_hbm = send_hbm.at[:, 0:c_out]

    block3_ref[...] = jnp.zeros_like(block3_ref)
    block_ref[...] = jnp.zeros_like(block_ref)
    clear_edges(cat3_ref, count)
    clear_edges(cat4_ref, count)
    for load in loads[:2]:
        load.wait()

    def gather(i, _):
        for j in range(side):
            block3_ref[j * count : (j + 1) * count, :] = frames_ref[i, j].astype(F32)
        field_ref[pl.ds(pl.multiple_of(i * edge, edge), edge), :] = block3_ref[...]
        return 0

    lax.fori_loop(0, side, gather, 0)
    spread(field_ref[...], cat3_ref, count)
    core = lax.axis_index("narrow")
    first = (lax.axis_index("wide") * lax.axis_size("narrow") + core) * count

    def part(at, half):
        return pl.ds(pl.multiple_of(at * half, half), half)

    stores = [
        pltpu.make_async_copy(field_ref.at[:, part(core, half3)], field_mine_hbm, out_sems.at[0]),
        pltpu.make_async_copy(field_ref.at[:, part(1 - core, half3)], send_hbm.at[:, c_out + half4 :], out_sems.at[1]),
    ]

    def owned(f):
        index = first + f

        def look(v, carry):
            start, found = carry
            end = start + counts_ref[v]
            inside = jnp.logical_and(index >= start, index < end)
            return end, jnp.where(inside, counts_ref[v], found)

        return lax.fori_loop(0, videos, look, (jnp.int32(0), jnp.int32(1)))[1]

    row = lax.broadcasted_iota(jnp.int32, (edge, 1), 0)
    held = jnp.zeros((edge, 1), jnp.int32)
    for f in range(count):
        held = jnp.where(lax.rem(row, count) == f, owned(f), held)
    scale = total / (videos * held.astype(F32))
    for load in loads[2:5]:
        load.wait()
    convolve_into(acc_ref, cat3_ref, w3_ref, edge)
    bias3 = b3_ref[...].astype(F32)

    def silu_rows(i, _):
        here = pl.ds(pl.multiple_of(i * edge, edge), edge)
        pre = acc_ref[here, :] + bias3
        sigma = jax.nn.sigmoid(pre)
        slope_ref[here, :] = silu_slope(pre, sigma)
        act = jnp.where(row < valid, pre * sigma, 0.0)
        act_ref[here, :] = act.astype(BF16).astype(F32)
        return 0

    lax.fori_loop(0, side, silu_rows, 0)
    stores += [
        pltpu.make_async_copy(act_ref.at[:, part(1 - core, half4)], send_hbm.at[:, c_out : c_out + half4], out_sems.at[2]),
        pltpu.make_async_copy(act_ref.at[:, part(core, half4)], mine_hbm, out_sems.at[3]),
        pltpu.make_async_copy(slope_ref, slope_hbm, out_sems.at[4]),
    ]
    for store in stores:
        store.start()
    spread(act_ref[...], cat4_ref, count)
    for load in loads[5:]:
        load.wait()
    convolve_into(acc_ref, cat4_ref, w4_ref, edge)
    bias4 = b4_ref[...].astype(F32)

    def last_rows(i, _):
        here = pl.ds(pl.multiple_of(i * edge, edge), edge)
        for j in range(side):
            block_ref[j * count : (j + 1) * count, :] = cot_ref[i, j].astype(F32)
        pre = acc_ref[here, :] + bias4
        sigma = jax.nn.sigmoid(pre)
        delta = block_ref[...] * scale * silu_slope(pre, sigma)
        delta_ref[here, :] = delta.astype(BF16).astype(F32)
        pltpu.make_async_copy(delta_ref.at[here], send_hbm.at[here, 0:c_out], out_sems.at[5]).start()
        out = pre * sigma
        for j in range(side):
            out_ref[i, j] = out[j * count : (j + 1) * count, :].astype(BF16)
        return 0

    lax.fori_loop(0, side, last_rows, 0)
    stores.append(pltpu.make_async_copy(out_ref, out_hbm, out_sems.at[6]))
    stores[-1].start()
    stores.append(pltpu.make_async_copy(delta_ref, delta_hbm, out_sems.at[5]))
    for store in stores:
        store.wait()


def head(total, clip_counts, frames, w3, b3, w4, b4, cot):
    side, count, c_in = frames.shape[1:]
    c_mid, c_out = w3.shape[1], w4.shape[1]
    rows = side * count * STEP
    edges = rows + 2 * count * STEP

    def field(width):
        return jax.ShapeDtypeStruct((rows, width), F32)

    return kernel_call(
        functools.partial(head_kernel, float(total)),
        (
            jax.ShapeDtypeStruct(cot.shape, BF16),
            field(c_mid // 2),
            field(c_mid),
            field(c_in // 2),
            field(c_out + c_mid // 2 + c_in // 2),
        ),
        [
            pltpu.SMEM(clip_counts.shape, jnp.int32),
            pltpu.VMEM(frames.shape, BF16),
            pltpu.VMEM(w3.shape, BF16),
            pltpu.VMEM(b3.shape, BF16),
            pltpu.VMEM(w4.shape, BF16),
            pltpu.VMEM(b4.shape, BF16),
            pltpu.VMEM(cot.shape, BF16),
            pltpu.VMEM((rows, c_in), F32),
            pltpu.VMEM((rows, c_mid), F32),
            pltpu.VMEM((rows, c_mid), F32),
            pltpu.VMEM((rows, c_mid), F32),
            pltpu.VMEM((rows, c_out), F32),
            pltpu.VMEM(cot.shape, BF16),
            pltpu.VMEM((count * STEP, c_in), F32),
            pltpu.VMEM((count * STEP, c_out), F32),
            pltpu.VMEM((edges, 3 * c_in), BF16),
            pltpu.VMEM((edges, 3 * c_mid), BF16),
            pltpu.SemaphoreType.DMA((7,)),
            pltpu.SemaphoreType.DMA((7,)),
        ],
        HEAD_MIB,
        2 * rows * 9 * c_mid * (c_in + c_out),
        clip_counts, frames, w3, b3, w4, b4, cot,
    )


def load_columns(pieces, target, sem):
    copies, at = [], 0
    for piece in pieces:
        width = piece.shape[1]
        copies.append(pltpu.make_async_copy(piece, target.at[:, at : at + width], sem.at[len(copies)]))
        at += width
    for copy in copies:
        copy.start()
    return copies


def back4_kernel(
    count, delta_hbm, slope_hbm, w_hbm, out_hbm, sums_hbm,
    delta_ref, slope_ref, w_ref, cat_ref, acc_ref, out_ref, sums_ref, sems,
):
    edge = count * STEP
    rows = out_ref.shape[0]
    loads = [
        pltpu.make_async_copy(delta_hbm.at[:, 0 : delta_ref.shape[1]], delta_ref, sems.at[0]),
        pltpu.make_async_copy(w_hbm, w_ref, sems.at[1]),
        pltpu.make_async_copy(slope_hbm, slope_ref, sems.at[2]),
    ]
    for load in loads:
        load.start()
    clear_edges(cat_ref, count)
    loads[0].wait()
    spread(delta_ref[...], cat_ref, count)
    loads[1].wait()
    back_into(acc_ref, cat_ref, w_ref, edge)
    loads[2].wait()
    side = rows // edge
    valid = lax.broadcasted_iota(jnp.int32, (edge, 1), 0) < side * count

    def rows_of(i, carry):
        here = pl.ds(pl.multiple_of(i * edge, edge), edge)
        delta = jnp.where(valid, acc_ref[here, :] * slope_ref[here, :], 0.0)
        delta = delta.astype(BF16).astype(F32)
        out_ref[here, :] = delta
        pltpu.make_async_copy(out_ref.at[here], out_hbm.at[here], sems.at[3]).start()
        sum3, sum4 = carry
        return (
            sum3 + jnp.sum(delta, 0, keepdims=True),
            sum4 + jnp.sum(delta_ref[here, :], 0, keepdims=True),
        )

    nothing = (jnp.zeros((1, out_ref.shape[1]), F32), jnp.zeros((1, delta_ref.shape[1]), F32))
    sums_ref[0:1, :], sums_ref[1:2, :] = lax.fori_loop(0, side, rows_of, nothing)
    stores = [
        pltpu.make_async_copy(out_ref, out_hbm, sems.at[3]),
        pltpu.make_async_copy(sums_ref, sums_hbm, sems.at[4]),
    ]
    stores[1].start()
    for store in stores:
        store.wait()


def back4(count, delta, slope, w):
    rows = delta.shape[0]
    taps, c_mid, width = w.shape
    return kernel_call(
        functools.partial(back4_kernel, count),
        (jax.ShapeDtypeStruct((rows, c_mid), F32), jax.ShapeDtypeStruct((2, width), F32)),
        [
            pltpu.VMEM((rows, width), F32),
            pltpu.VMEM((rows, c_mid), F32),
            pltpu.VMEM((taps, c_mid, width), BF16),
            pltpu.VMEM((rows + 2 * count * STEP, 3 * width), BF16),
            pltpu.VMEM((rows, c_mid), F32),
            pltpu.VMEM((rows, c_mid), F32),
            pltpu.VMEM((2, width), F32),
            pltpu.SemaphoreType.DMA((5,)),
        ],
        BACK4_MIB,
        2 * rows * c_mid * width * taps,
        delta, slope, w,
    )


def back3_kernel(count, pieces, *refs):
    deltas, (w_hbm, out_hbm, delta_ref, w_ref, cat_ref, acc_ref, out_ref, sems) = refs[:pieces], refs[pieces:]
    edge = count * STEP
    loads = load_columns(deltas, delta_ref, sems)
    load = pltpu.make_async_copy(w_hbm, w_ref, sems.at[pieces])
    load.start()
    clear_edges(cat_ref, count)
    for copy in loads:
        copy.wait()
    spread(delta_ref[...], cat_ref, count)
    load.wait()
    back_into(acc_ref, cat_ref, w_ref, edge)
    side = out_ref.shape[0]

    def rows_of(i, _):
        block = acc_ref[pl.ds(pl.multiple_of(i * edge, edge), edge), :]
        for j in range(side):
            out_ref[i, j] = block[j * count : (j + 1) * count, :].astype(BF16)
        return 0

    lax.fori_loop(0, side, rows_of, 0)
    store = pltpu.make_async_copy(out_ref, out_hbm, sems.at[pieces + 1])
    store.start()
    store.wait()


def back3(side, count, deltas, w):
    rows = deltas[0].shape[0]
    taps, c_in, width = w.shape
    return kernel_call(
        functools.partial(back3_kernel, count, len(deltas)),
        jax.ShapeDtypeStruct((side, side, count, c_in), BF16),
        [
            pltpu.VMEM((rows, width), F32),
            pltpu.VMEM(w.shape, BF16),
            pltpu.VMEM((rows + 2 * count * STEP, 3 * width), BF16),
            pltpu.VMEM((rows, c_in), F32),
            pltpu.VMEM((side, side, count, c_in), BF16),
            pltpu.SemaphoreType.DMA((len(deltas) + 2,)),
        ],
        BACK3_MIB,
        2 * rows * c_in * width * taps,
        *deltas, w,
    )


def grad_kernel(count, side, lanes, chunks, size, places, tail, *refs):
    sums_hbm, refs = refs[4 : 4 + 2 * tail], refs[:4] + refs[4 + 2 * tail :]
    outs, (*targets, turned_ref, both_ref, acc_ref, sums_ref, in_sems, out_sems) = (
        refs[4 : 4 + 2 * lanes], refs[4 + 2 * lanes :],
    )
    mine_ref, theirs_ref, delta_ref, other_ref = targets
    _, spot, way = own_place(size)
    edge = count * STEP
    wide = 2 * edge
    k = mine_ref.shape[1]
    groups = (0, side // 3, 2 * side // 3, side)
    loads = []
    for group in range(3):
        rows = slice(groups[group] * edge, groups[group + 1] * edge)
        loads.append([])
        for at in range(4):
            columns = slice(places[at], places[at] + targets[at].shape[1])
            copy = pltpu.make_async_copy(
                refs[at].at[rows, columns], targets[at].at[rows], in_sems.at[at, group]
            )
            copy.start()
            loads[-1].append(copy)
    extra = [
        pltpu.make_async_copy(source, sums_ref.at[at], in_sems.at[4, at]) for at, source in enumerate(sums_hbm)
    ]
    for load in extra:
        load.start()
    turned_ref[:, 0:wide] = jnp.zeros((3 * k, wide), BF16)
    turned_ref[:, (side + 1) * wide :] = jnp.zeros((3 * k, wide), BF16)

    def turn(i, carry):
        here = pl.ds(pl.multiple_of(i * edge, edge), edge)
        there = pl.ds(pl.multiple_of((i + 1) * wide, wide), wide)
        turned = jnp.concatenate([mine_ref[here, :], theirs_ref[here, :]], 0).T
        for c, shift in enumerate((count, 0, wide - count)):
            moved = turned if shift == 0 else pltpu.roll(turned, shift, 1)
            turned_ref[c * k : (c + 1) * k, there] = moved.astype(BF16)
        to = pl.multiple_of(i * wide, wide)
        both_ref[pl.ds(to, edge), :] = delta_ref[here, :].astype(BF16)
        both_ref[pl.ds(to + edge, edge), :] = other_ref[here, :].astype(BF16)
        return carry

    for group in range(3):
        for load in loads[group]:
            load.wait()
        lax.fori_loop(groups[group], groups[group + 1], turn, 0)
    blocks = 3 * k // (8 * lanes * chunks)
    if tail:
        for load in extra:
            load.wait()
        acc_ref[0, :, 3 * blocks] = jnp.zeros((chunks,) + acc_ref.shape[3:], F32)
        acc_ref[0, 0, 3 * blocks, 0:2, :] = sums_ref[0] + sums_ref[1]
    stores = []
    for r in range(3):
        part = jnp.dot(
            turned_ref[:, r * wide : (r + side) * wide], both_ref[...], preferred_element_type=F32
        )
        part = part.reshape((3, lanes, chunks, blocks // 3, 8, part.shape[1]))
        for chunk in range(chunks):
            at = lax.rem(way * (spot - chunk) + 2 * size - 1, size) if chunks > 1 else 0
            for lane in range(lanes):
                piece = part[:, lane, chunk].reshape((blocks,) + acc_ref.shape[3:])
                acc_ref[lane, at, r * blocks : (r + 1) * blocks] = piece
        here = slice(r * blocks, (r + 1) * blocks if r < 2 else acc_ref.shape[2])
        for lane in range(lanes):
            first, others = outs[2 * lane : 2 * lane + 2]
            pairs = [(acc_ref.at[lane, 0, here], first.at[here])]
            if chunks > 1:
                pairs.append((acc_ref.at[lane, 1:, here], others.at[:, here]))
            for source, target in pairs:
                copy = pltpu.make_async_copy(source, target, out_sems.at[len(stores)])
                copy.start()
                stores.append(copy)
    for store in stores:
        store.wait()


def grad(mib, side, count, lanes, chunks, size, o, mine, theirs, delta, other, sums=()):
    arrays, places = zip(mine, theirs, delta, other)
    rows, k = arrays[0].shape
    blocks = 9 * k // (8 * lanes * chunks) + (1 if sums else 0)
    first = jax.ShapeDtypeStruct((blocks, 8, o), F32)
    others = jax.ShapeDtypeStruct((max(chunks - 1, 1), blocks, 8, o), F32)
    results = kernel_call(
        functools.partial(grad_kernel, count, side, lanes, chunks, size, places, bool(sums)),
        (first, others) * lanes,
        [
            pltpu.VMEM((rows, k), F32),
            pltpu.VMEM((rows, k), F32),
            pltpu.VMEM((rows, o), F32),
            pltpu.VMEM((rows, o), F32),
            pltpu.VMEM((3 * k, 2 * count * STEP * (side + 2)), BF16),
            pltpu.VMEM((2 * rows, o), BF16),
            pltpu.VMEM((lanes, chunks, blocks, 8, o), F32),
            pltpu.VMEM((2, 2, o), F32),
            pltpu.SemaphoreType.DMA((5, 3)),
            pltpu.SemaphoreType.DMA((6 * lanes,)),
        ],
        mib,
        2 * 2 * rows * 9 * k * o,
        *arrays, *sums,
    )
    return [(results[2 * lane], results[2 * lane + 1]) for lane in range(lanes)]


def lay_kernel(layout, size, inputs, *refs):
    outs, sems = refs[inputs:-1], refs[-1]
    core, spot, way = own_place(size)
    copies = []
    for at, (out, low, stride, back, own) in enumerate(layout):
        rows = refs[at].shape[1]
        chunk = lax.rem(spot - way * (back if own else -back) + 2 * size, size)
        start = low + (core if own else 1 - core) * stride + chunk * rows
        there = outs[out].at[:, pl.ds(pl.multiple_of(start, rows), rows), :]
        copies.append(pltpu.make_async_copy(refs[at], there, sems.at[at]))
    for copy in copies:
        copy.start()
    for copy in copies:
        copy.wait()


def lay(size, pieces, layout, results, shapes):
    kept = [at for at, result in enumerate(results) if result is not None]
    inputs = len(pieces) + len(kept)
    return kernel_call(
        functools.partial(lay_kernel, tuple(layout), size, inputs),
        tuple(jax.ShapeDtypeStruct(shape, F32) for shape in shapes),
        [pltpu.SemaphoreType.DMA((len(pieces),))],
        1,
        0,
        *pieces, *[results[at] for at in kept],
        aliases={len(pieces) + at: out for at, out in enumerate(kept)},
    )


def tally_kernel(size, *refs):
    pieces, (first_hbm, second_hbm, all_ref, total_ref, in_sems, out_sems) = refs[:size], refs[size:]
    _, spot, way = own_place(size)
    loads = []
    for back, piece in enumerate(pieces):
        chunk = lax.rem(spot - way * back + 2 * size, size)
        loads.append(pltpu.make_async_copy(piece.at[piece.shape[0] - 1], all_ref.at[chunk], in_sems.at[back]))
        loads[-1].start()
    for load in loads:
        load.wait()
    total = all_ref[0]
    for chip in range(1, size):
        total = total + all_ref[chip]
    total_ref[0] = total[0:1]
    total_ref[1] = total[1:2]
    stores = [
        pltpu.make_async_copy(total_ref.at[at], out, out_sems.at[at])
        for at, out in enumerate((first_hbm, second_hbm))
    ]
    for store in stores:
        store.start()
    for store in stores:
        store.wait()


def tally(pieces):
    size, width = len(pieces), pieces[0].shape[2]
    out = jax.ShapeDtypeStruct((1, width), F32)
    return kernel_call(
        functools.partial(tally_kernel, size),
        (out, out),
        [
            pltpu.VMEM((size, 8, width), F32),
            pltpu.VMEM((2, 1, width), F32),
            pltpu.SemaphoreType.DMA((size,)),
            pltpu.SemaphoreType.DMA((2,)),
        ],
        2,
        0,
        *pieces,
    )


def swap_cores(value):
    return lax.ppermute(value, "narrow", [(0, 1), (1, 0)])


def pick(array, index, axis=0):
    return lax.dynamic_index_in_dim(array, index, axis, keepdims=False)


class Ring:
    def __init__(self, size):
        self.size = size
        order = list(range(0, size, 2)) + list(range(size - 1, 0, -2))
        self.pairs = []
        for core, way in ((0, 1), (1, -1)):
            for i in range(size):
                self.pairs.append((2 * order[i] + core, 2 * order[(i + way) % size] + core))
        wide = lax.axis_index("wide")
        self.core = lax.axis_index("narrow")
        half = wide // 2
        self.place = jnp.where(wide % 2 == 0, half, size - 1 - half)
        self.way = 1 - 2 * self.core

    def send(self, value):
        return lax.ppermute(value, ("wide", "narrow"), self.pairs)

    def chunk(self, back):
        return lax.rem(self.place - self.way * back + 2 * self.size, self.size)


def collected(grad, core):
    taps, rows, width = grad.shape
    share = lax.psum_scatter(grad.reshape(-1, width), "wide", scatter_dimension=0, tiled=True)
    mine = lax.all_gather(share, "wide", axis=0, tiled=True).reshape(grad.shape)
    theirs = swap_cores(mine)
    lower, upper = jnp.where(core == 0, mine, theirs), jnp.where(core == 0, theirs, mine)
    return jnp.concatenate([lower, upper], 1)


class Lane:
    def __init__(self, parts, ring, low, stride, blocks):
        self.ring, self.low, self.stride, self.blocks = ring, low, stride, blocks
        self.held, self.parts = parts
        self.passed = [self.held]
        self.pieces, self.lows = [], []

    def keep(self, back):
        for piece, own in ((self.held, True), (swap_cores(self.held), False)):
            self.pieces.append(piece.reshape(9, -1, piece.shape[-1]))
            self.lows.append((self.low, self.stride, back, own))

    def step(self, number):
        last = self.ring.size - 1
        if number == last:
            self.keep(0)
        got = self.ring.send(self.held)
        if number < last:
            self.passed.append(got)
            self.held = got + self.parts[number]
            if number == last - 1:
                self.held = self.held[: self.blocks]
        else:
            self.held = got
            self.keep(number - last + 1)


def lay_lanes(lanes, results, shapes):
    pieces, layout = [], []
    for lane, at in lanes:
        pieces += lane.pieces
        layout += [(at,) + low for low in lane.lows]
        size, lane.pieces, lane.lows = lane.ring.size, [], []
    return lay(size, pieces, layout, results, shapes)


def after(value, *others):
    return lax.optimization_barrier((value,) + others)[0]


def body(frames, weight3, bias3, weight4, bias4, cotangent, clip_counts):
    count, side, c_in = frames.shape[1], frames.shape[2], frames.shape[4]
    w_three, w_four = (weight3[0], weight4[0])
    c_mid, c_out = w_three.shape[1], w_four.shape[1]
    taps3, taps4 = w_three.reshape(9, c_in, c_mid), w_four.reshape(9, c_mid, c_out)
    size = lax.axis_size("wide")
    ring = Ring(size)
    core = ring.core
    total_frames = count * size * lax.axis_size("narrow")
    def cells_first(field):
        return jnp.transpose(field, (1, 2, 0, 3))

    def frames_first(field):
        return jnp.transpose(field, (2, 0, 1, 3))

    output, act_mine, slope3, field_mine, send = head(
        total_frames, clip_counts, cells_first(frames[0]), w_three, bias3, w_four, bias4,
        cells_first(cotangent[0]),
    )
    small = size <= 8
    chunks = size if small else 1
    lanes4 = 2 if small else 1
    theirs = swap_cores(send)
    delta3, sums = back4(count, send, slope3, taps4)
    sums_theirs = swap_cores(sums)
    delta3_theirs = swap_cores(delta3)
    grads4 = grad(
        62, side, count, lanes4, chunks, size, c_out,
        (after(act_mine, delta3), 0), (theirs, c_out), (send, 0), (theirs, 0),
    )
    def grad_of_3(mine, sums):
        return grad(
            62, side, count, 1, chunks, size, c_mid,
            (mine, 0), (theirs, c_out + c_mid // 2), (delta3, 0), (delta3_theirs, 0), sums,
        )[0]

    if not small:
        grads3 = grad_of_3(field_mine, ())
        biases = lax.psum(sums + sums_theirs, "wide")
        sum3, sum4 = biases[0:1], biases[1:2]
        grad_w4 = collected(grads4[0][0].reshape(9, -1, c_out), core)
        grad_w3 = collected(grads3[0].reshape(9, -1, c_mid), core)
    else:
        half3, half4, quarter = c_in // 2, c_mid // 2, c_mid // 4
        blocks = 9 * quarter // (8 * size)
        x = Lane(grads4[0], ring, 0, half4, blocks)
        y = Lane(grads4[1], ring, quarter, half4, blocks)
        x.step(0)
        y.step(0)
        grads3 = grad_of_3(field_mine, (sums, sums_theirs))
        z = Lane(grads3, ring, 0, half3, 9 * half3 // (8 * size))
        z.held = after(z.held, x.held, y.held)
        x.held, y.held = after(x.held, z.held), after(y.held, z.held)
        grad_w4 = grad_w3 = None
        shape3, shape4 = (9, c_in, c_mid), (9, c_mid, c_out)
        last = 2 * (size - 1) - 1
        for number in range(last + 1):
            if number in (last - 4, last - 1):
                (grad_w3,) = lay_lanes([(z, 0)], [grad_w3], [shape3])
            if number in (last - 3, last):
                z.held = after(z.held, grad_w3)
            if number in (last - 3, last - 1):
                (grad_w4,) = lay_lanes([(y, 0)], [grad_w4], [shape4])
            if number in (last - 2, last):
                y.held = after(y.held, grad_w4)
                (grad_w4,) = lay_lanes([(x, 0)], [grad_w4], [shape4])
            if number in (last - 1, last):
                x.held = after(x.held, grad_w4)
            z.step(number)
            if number > 0:
                y.step(number)
                x.step(number)
            if number == size - 1:
                sum3, sum4 = tally(z.passed)
            if number == size:
                x.held = after(x.held, sum3)
            if number == 1:
                field_grad = back3(side, count, [after(delta3, z.held)], taps3)
            if number == 3:
                z.held = after(z.held, field_grad)
        grad_w3, grad_w4 = lay_lanes([(z, 0), (x, 1), (y, 1)], [grad_w3, grad_w4], [shape3, shape4])
    if not small:
        field_grad = back3(side, count, [delta3], taps3)
    return (
        frames_first(output)[None],
        frames_first(field_grad)[None],
        grad_w3.reshape(w_three.shape)[None],
        sum3,
        grad_w4.reshape(w_four.shape)[None],
        sum4,
    )


def solution(mesh):
    return jax.shard_map(
        body,
        mesh=mesh,
        in_specs=(
            P("stream", ("wide", "narrow"), None, None, None),
            P("stream", None, None),
            P("stream", None),
            P("stream", None, None),
            P("stream", None),
            P("stream", ("wide", "narrow"), None, None, None),
            P(),
        ),
        out_specs=(
            P("stream", ("wide", "narrow"), None, None, None),
            P("stream", ("wide", "narrow"), None, None, None),
            P("stream", None, None),
            P("stream", None),
            P("stream", None, None),
            P("stream", None),
        ),
        check_vma=False,
    )
```

time: 668 us -> 183 us (0.27)
  waiting for transfers between devices: 424 us -> 54.3 us
  local copies, waits for them, and re-layouts: 147 us -> 0.64 us
  starting transfers between devices: 0.2 us -> 69.5 us
  Pallas kernels: 0 us -> 50.6 us
  blocking collectives: 42.9 us -> 0 us
  matrix products: 36 us -> 0 us
  between operations: 15.6 us -> 1.16 us
    reduce_scatter x2 -> x0, waiting for transfers between devices: 255 us -> none  [the longest x1 167 us: reduce_grads(): lax.psum_scatter(grads[2], 'wide', scatter_dimension=0, tiled=True)]
    all_gather x2 -> x0, waiting for transfers between devices: 146 us -> none  [the longest x1 139 us: reduce_grads(): lax.all_gather(shares[2], 'wide', axis=0, tiled=True)]
    ppermute x0 -> x69, starting transfers between devices: none -> 69.5 us  [the longest x42 66.1 us: send(): return lax.ppermute(value, ('wide', 'narrow'), self.pairs)]
    unnamed x94 -> x16, local copies, waits for them, and re-layouts: 61.1 us -> 0.62 us
    ppermute x0 -> x69, waiting for transfers between devices: none -> 54.3 us  [the longest x42 52.7 us: send(): return lax.ppermute(value, ('wide', 'narrow'), self.pairs)]
    pallas_call x0 -> x13, Pallas kernels: none -> 50.6 us  [kernel_call(): pl.pallas_call(kernel, out_shape=outs, in_specs=[HBM] * len(args), out_sp...]
    concatenate x37 -> x0, local copies, waits for them, and re-layouts: 43.8 us -> none  [columns(): return jnp.concatenate(pieces, axis=-1).reshape(count * side * side, -1)]
    unnamed x2 -> x0, blocking collectives: 40.4 us -> none
  transfers between devices with their start and end apart: 5 -> 69, of which waited for: 5 -> 31; matrix products, arithmetic and copies ran while one was open for 6% -> 3% of each run, Pallas kernels for 0% -> 21%
where the time goes in v1:
time: 183 us
  starting transfers between devices  69.5 us (38%)
  waiting for transfers between devices  54.3 us (30%)
  Pallas kernels  50.6 us (28%)
  other arithmetic  6.85 us (4%)
    ppermute x42, starting transfers between devices, send(): return lax.ppermute(value, ('wide', 'narrow'), self.pairs)  66.1 us
    ppermute x42, waiting for transfers between devices, send(): return lax.ppermute(value, ('wide', 'narrow'), self.pairs)  52.7 us
    pallas_call x13, Pallas kernels, kernel_call(): pl.pallas_call(kernel, out_shape=outs, in_specs=[HBM] * len(args), out_sp...  50.6 us
    add x21, other arithmetic, step(): self.held = got + self.parts[number]  6.85 us
  transfers between devices with their start and end apart: 69, of which 31 were waited for; matrix products, arithmetic and copies ran while one was open for 3% of the time, Pallas kernels for 21%

profile of v1, /device:TPU:0, one launch (start us, length us, event | category | flops | bytes accessed | tf_op | source)
XLA Modules:
  0.0 183.0 jit_solution(15118629911527702875)
XLA Ops:
  0.6 11.1 %shard_map.118 = (bf16[13,13,4,512]{3,2,1,0:T(4,128)(2,1)}, f32[832,256]{1,0:T(8,128)}, f32[832,512]{1,0:T(8,128)}, f32[832,128]{1,0:T(8,128)}, f32[832,896]{1,0:T(8,128)}) custom-call(s32[8]{0:T(128)} %counts_hbm.1, bf16[13,13,4,256]{3,2,1,0:T(4,128)(2,1)} %bitcast.163, bf16[2304,512]{1,0:T(8,128)(2,1)} %bitcast.156, bf16[1,512]{1,0:T(2,128)(2,1)} %b3_hbm.1, ...), custom_call_target="tpu_custom_call" | custom-call | flops 5888802816 | bytes 8388608 | tf_op jit(solution)/shard_map/pallas_call | solution.py:25
  12.3 8.3 %shard_map.119 = (f32[832,512]{1,0:T(8,128)}, f32[2,512]{1,0:T(2,128)}) custom-call(f32[832,896]{1,0:T(8,128)} %get-tuple-element.37.delta_hbm.refs_2_, f32[832,512]{1,0:T(8,128)} %get-tuple-element.38.slope_hbm, bf16[9,512,512]{2,1,0:T(8,128)(2,1)} %bitcast.161), custom_call_target="tpu_custom_call" | custom-call | flops 3925868544 | bytes 8388608 | tf_op jit(solution)/shard_map/pallas_call | solution.py:25
  20.7 10.1 %shard_map.121 = (f32[18,8,512]{2,1,0:T(8,128)}, f32[7,18,8,512]{3,2,1,0:T(8,128)}, f32[18,8,512]{2,1,0:T(8,128)}, f32[7,18,8,512]{3,2,1,0:T(8,128)}) custom-call(f32[832,256]{1,0:T(8,128)} %get-tuple-element.44.refs_0_, f32[832,896]{1,0:T(8,128)} %collective-permute-done.refs_1_.refs_3_, f32[832,896]{1,0:T(8,128)} %get-tuple-element.37.delta_hbm.refs_2_, ...), custom_call_target="tpu_custom_call" | custom-call | flops 3925868544 | bytes 8388608 | tf_op jit(solution)/shard_map/pallas_call | solution.py:25
  30.8 3.1 %collective-permute-start.3 = (f32[18,8,512]{2,1,0:T(8,128)}, f32[18,8,512]{2,1,0:T(8,128)S(1)}, u32[]{:S(2)}, u32[]{:S(2)}) collective-permute-start(f32[18,8,512]{2,1,0:T(8,128)} %get-tuple-element.45), channel_id=1, source_target_pairs={{0,4},{4,8},{8,12},{12,14},{14,10},{10,6},{6,2},{2,0},{1,3},{5,1},... | collective-permute-start | bytes 884744 | tf_op jit(solution)/shard_map/ppermute | solution.py:571
  33.8 1.6 collective-permute-start.4
  36.0 7.0 %shard_map.120 = (f32[19,8,512]{2,1,0:T(8,128)}, f32[7,19,8,512]{3,2,1,0:T(8,128)}) custom-call(f32[832,128]{1,0:T(8,128)} %get-tuple-element.40.refs_0_, f32[832,896]{1,0:T(8,128)} %collective-permute-done.refs_1_.refs_3_, f32[832,512]{1,0:T(8,128)} %get-tuple-element.51.refs_2_.refs_0_, f32[832,512]{1,0:T(8,128)} %collective-permute-done.1.refs_3_, ...), custom_call_target="tpu_custom_call" | custom-call | flops 1962934272 | bytes 8388608 | tf_op jit(solution)/shard_map/pallas_call | solution.py:25
  45.2 1.6 collective-permute-start.27
  49.5 2.5 %collective-permute-done.27 = f32[18,8,512]{2,1,0:T(8,128)S(1)} collective-permute-done((f32[18,8,512]{2,1,0:T(8,128)S(1)}, f32[18,8,512]{2,1,0:T(8,128)S(1)}, u32[]{:S(2)}, u32[]{:S(2)}) %collective-permute-start.27) | collective-permute-done | bytes 294944 | tf_op jit(solution)/shard_map/ppermute | solution.py:571
  53.1 1.6 collective-permute-start.28
  56.2 1.6 collective-permute-start.39
  58.6 1.6 collective-permute-start.6
  62.7 1.6 collective-permute-start.29
  65.8 1.6 collective-permute-start.40
  68.2 1.6 collective-permute-start.7
  69.9 3.8 %shard_map.122 = bf16[13,13,4,256]{3,2,1,0:T(4,128)(2,1)} custom-call(f32[832,512]{1,0:T(8,128)S(1)} %copy-done.2, bf16[9,256,512]{2,1,0:T(8,128)(2,1)S(1)} %bitcast.157), custom_call_target="tpu_custom_call" | custom-call | flops 1962934272 | bytes 8388608 | tf_op jit(solution)/shard_map/pallas_call | solution.py:25
  75.3 2.5 %collective-permute-done.7.refs_3_ = f32[19,8,512]{2,1,0:T(8,128)S(1)} collective-permute-done((f32[19,8,512]{2,1,0:T(8,128)S(1)}, f32[19,8,512]{2,1,0:T(8,128)S(1)}, u32[]{:S(2)}, u32[]{:S(2)}) %collective-permute-start.7) | collective-permute-done | bytes 311328 | tf_op jit(solution)/shard_map/ppermute | solution.py:571
  77.9 1.6 collective-permute-start.8
  82.7 2.2 %collective-permute-done.8.refs_4_ = f32[19,8,512]{2,1,0:T(8,128)S(1)} collective-permute-done((f32[19,8,512]{2,1,0:T(8,128)S(1)}, f32[19,8,512]{2,1,0:T(8,128)S(1)}, u32[]{:S(2)}, u32[]{:S(2)}) %collective-permute-start.8) | collective-permute-done | bytes 311328 | tf_op jit(solution)/shard_map/ppermute | solution.py:571
  84.9 1.6 collective-permute-start.9
  88.0 1.6 collective-permute-start.42
  91.2 1.6 collective-permute-start.32
  92.8 1.6 collective-permute-done.9.refs_5_
  94.5 1.6 collective-permute-start.10
  97.7 1.6 collective-permute-start.43
  100.8 1.6 collective-permute-start.33
  102.5 1.6 collective-permute-done.10.refs_6_
  104.2 1.6 collective-permute-start.11
  107.3 1.6 collective-permute-start.44
  110.5 1.6 collective-permute-start.34
  112.0 4.9 %collective-permute-done.44 = f32[18,8,512]{2,1,0:T(8,128)S(1)} collective-permute-done((f32[18,8,512]{2,1,0:T(8,128)S(1)}, f32[18,8,512]{2,1,0:T(8,128)S(1)}, u32[]{:S(2)}, u32[]{:S(2)}) %collective-permute-start.44) | collective-permute-done | bytes 294944 | tf_op jit(solution)/shard_map/ppermute | solution.py:571
  116.9 1.6 collective-permute-start.45
  120.2 3.5 %collective-permute-done.45 = f32[18,8,512]{2,1,0:T(8,128)S(1)} collective-permute-done((f32[18,8,512]{2,1,0:T(8,128)S(1)}, f32[18,8,512]{2,1,0:T(8,128)S(1)}, u32[]{:S(2)}, u32[]{:S(2)}) %collective-permute-start.45) | collective-permute-done | bytes 294944 | tf_op jit(solution)/shard_map/ppermute | solution.py:571
  123.7 1.6 collective-permute-start.46
  126.8 1.6 collective-permute-start.13
  133.6 3.2 %collective-permute-done.35 = f32[18,8,512]{2,1,0:T(8,128)S(1)} collective-permute-done((f32[18,8,512]{2,1,0:T(8,128)S(1)}, f32[18,8,512]{2,1,0:T(8,128)S(1)}, u32[]{:S(2)}, u32[]{:S(2)}) %collective-permute-start.35) | collective-permute-done | bytes 294944 | tf_op jit(solution)/shard_map/ppermute | solution.py:571
  136.7 1.6 collective-permute-start.14
  141.9 1.6 collective-permute-start.53
  144.8 1.8 collective-permute-done.36
  146.6 1.6 collective-permute-start.18
  149.8 1.6 collective-permute-start.37
  151.4 2.0 %collective-permute-done.18 = f32[18,8,512]{2,1,0:T(8,128)S(1)} collective-permute-done((f32[18,8,512]{2,1,0:T(8,128)S(1)}, f32[18,8,512]{2,1,0:T(8,128)S(1)}, u32[]{:S(2)}, u32[]{:S(2)}) %collective-permute-start.18) | collective-permute-done | bytes 294944 | tf_op jit(solution)/shard_map/ppermute | solution.py:571
  153.3 1.6 collective-permute-start.19
  154.9 1.7 shard_map.127.refs_4_
  161.6 1.7 collective-permute-done.65
  163.4 3.2 %collective-permute-done.60 = f32[18,8,512]{2,1,0:T(8,128)S(1)} collective-permute-done((f32[18,8,512]{2,1,0:T(8,128)S(1)}, f32[18,8,512]{2,1,0:T(8,128)S(1)}, u32[]{:S(2)}, u32[]{:S(2)}) %collective-permute-start.60) | collective-permute-done | bytes 294944 | tf_op jit(solution)/shard_map/ppermute | solution.py:571
  174.3 2.2 %collective-permute-done.25 = f32[18,8,512]{2,1,0:T(8,128)S(1)} collective-permute-done((f32[18,8,512]{2,1,0:T(8,128)S(1)}, f32[18,8,512]{2,1,0:T(8,128)S(1)}, u32[]{:S(2)}, u32[]{:S(2)}) %collective-permute-start.25) | collective-permute-done | bytes 294944 | tf_op jit(solution)/shard_map/ppermute | solution.py:571
  176.4 3.2 %collective-permute-done.63 = f32[18,8,512]{2,1,0:T(8,128)S(1)} collective-permute-done((f32[18,8,512]{2,1,0:T(8,128)S(1)}, f32[18,8,512]{2,1,0:T(8,128)S(1)}, u32[]{:S(2)}, u32[]{:S(2)}) %collective-permute-start.63) | collective-permute-done | bytes 294944 | tf_op jit(solution)/shard_map/ppermute | solution.py:571
  181.2 1.7 shard_map.130
  (141 shorter events, 57.2 us)
Async XLA Ops:
  11.8 8.9 %collective-permute-start = (f32[832,896]{1,0:T(8,128)}, f32[832,896]{1,0:T(8,128)}, u32[]{:S(2)}, u32[]{:S(2)}) collective-permute-start(f32[832,896]{1,0:T(8,128)} %get-tuple-element.37.delta_hbm.refs_2_), channel_id=1, source_target_pairs={{0,1},{1,0},{2,3},{3,2},{4,5},{5,4},{6,7},{7,6},{8,9},{9,8},{10,11... | collective-permute-start | bytes 8945672 | tf_op jit(solution)/shard_map/ppermute | solution.py:549
  20.6 14.9 %collective-permute-start.1 = (f32[832,512]{1,0:T(8,128)}, f32[832,512]{1,0:T(8,128)}, u32[]{:S(2)}, u32[]{:S(2)}) collective-permute-start(f32[832,512]{1,0:T(8,128)} %get-tuple-element.51.refs_2_.refs_0_), channel_id=1, source_target_pairs={{0,1},{1,0},{2,3},{3,2},{4,5},{5,4},{6,7},{7,6},{8,9},{9,8},{10,11... | collective-permute-start | bytes 5111816 | tf_op jit(solution)/shard_map/ppermute | solution.py:549
  30.8 12.3 %collective-permute-start.3 = (f32[18,8,512]{2,1,0:T(8,128)}, f32[18,8,512]{2,1,0:T(8,128)S(1)}, u32[]{:S(2)}, u32[]{:S(2)}) collective-permute-start(f32[18,8,512]{2,1,0:T(8,128)} %get-tuple-element.45), channel_id=1, source_target_pairs={{0,4},{4,8},{8,12},{12,14},{14,10},{10,6},{6,2},{2,0},{1,3},{5,1},... | collective-permute-start | bytes 884744 | tf_op jit(solution)/shard_map/ppermute | solution.py:571
  33.8 10.4 %collective-permute-start.4 = (f32[18,8,512]{2,1,0:T(8,128)}, f32[18,8,512]{2,1,0:T(8,128)S(1)}, u32[]{:S(2)}, u32[]{:S(2)}) collective-permute-start(f32[18,8,512]{2,1,0:T(8,128)} %get-tuple-element.47), channel_id=1, source_target_pairs={{0,4},{4,8},{8,12},{12,14},{14,10},{10,6},{6,2},{2,0},{1,3},{5,1},... | collective-permute-start | bytes 884744 | tf_op jit(solution)/shard_map/ppermute | solution.py:571
  46.9 8.3 %collective-permute-start.38 = (f32[18,8,512]{2,1,0:T(8,128)S(1)}, f32[18,8,512]{2,1,0:T(8,128)S(1)}, u32[]{:S(2)}, u32[]{:S(2)}) collective-permute-start(f32[18,8,512]{2,1,0:T(8,128)S(1)} %bitcast_add_fusion.18), channel_id=1, source_target_pairs={{0,4},{4,8},{8,12},{12,14},{14,10},{10,6},{6,2},{2,0},{1,3},{5,1},... | collective-permute-start | bytes 884744 | tf_op jit(solution)/shard_map/ppermute | solution.py:571
  48.4 10.1 %collective-permute-start.5 = (f32[19,8,512]{2,1,0:T(8,128)}, f32[19,8,512]{2,1,0:T(8,128)S(1)}, u32[]{:S(2)}, u32[]{:S(2)}) collective-permute-start(f32[19,8,512]{2,1,0:T(8,128)} %get-tuple-element.49.refs_0_), channel_id=1, source_target_pairs={{0,4},{4,8},{8,12},{12,14},{14,10},{10,6},{6,2},{2,0},{1,3},{5,1},... | collective-permute-start | bytes 933896 | tf_op jit(solution)/shard_map/ppermute | solution.py:571
  53.1 8.6 %collective-permute-start.28 = (f32[18,8,512]{2,1,0:T(8,128)S(1)}, f32[18,8,512]{2,1,0:T(8,128)S(1)}, u32[]{:S(2)}, u32[]{:S(2)}) collective-permute-start(f32[18,8,512]{2,1,0:T(8,128)S(1)} %bitcast_add_fusion.17), channel_id=1, source_target_pairs={{0,4},{4,8},{8,12},{12,14},{14,10},{10,6},{6,2},{2,0},{1,3},{5,1},... | collective-permute-start | bytes 884744 | tf_op jit(solution)/shard_map/ppermute | solution.py:571
  56.2 8.7 %collective-permute-start.39 = (f32[18,8,512]{2,1,0:T(8,128)S(1)}, f32[18,8,512]{2,1,0:T(8,128)S(1)}, u32[]{:S(2)}, u32[]{:S(2)}) collective-permute-start(f32[18,8,512]{2,1,0:T(8,128)S(1)} %bitcast_add_fusion.11), channel_id=1, source_target_pairs={{0,4},{4,8},{8,12},{12,14},{14,10},{10,6},{6,2},{2,0},{1,3},{5,1},... | collective-permute-start | bytes 884744 | tf_op jit(solution)/shard_map/ppermute | solution.py:571
  58.6 9.6 %collective-permute-start.6 = (f32[19,8,512]{2,1,0:T(8,128)S(1)}, f32[19,8,512]{2,1,0:T(8,128)S(1)}, u32[]{:S(2)}, u32[]{:S(2)}) collective-permute-start(f32[19,8,512]{2,1,0:T(8,128)S(1)} %bitcast_add_fusion.5), channel_id=1, source_target_pairs={{0,4},{4,8},{8,12},{12,14},{14,10},{10,6},{6,2},{2,0},{1,3},{5,1},... | collective-permute-start | bytes 933896 | tf_op jit(solution)/shard_map/ppermute | solution.py:571
  62.7 11.0 %collective-permute-start.29 = (f32[18,8,512]{2,1,0:T(8,128)S(1)}, f32[18,8,512]{2,1,0:T(8,128)S(1)}, u32[]{:S(2)}, u32[]{:S(2)}) collective-permute-start(f32[18,8,512]{2,1,0:T(8,128)S(1)} %bitcast_add_fusion.16), channel_id=1, source_target_pairs={{0,4},{4,8},{8,12},{12,14},{14,10},{10,6},{6,2},{2,0},{1,3},{5,1},... | collective-permute-start | bytes 884744 | tf_op jit(solution)/shard_map/ppermute | solution.py:571
  65.8 13.7 %collective-permute-start.40 = (f32[18,8,512]{2,1,0:T(8,128)S(1)}, f32[18,8,512]{2,1,0:T(8,128)S(1)}, u32[]{:S(2)}, u32[]{:S(2)}) collective-permute-start(f32[18,8,512]{2,1,0:T(8,128)S(1)} %bitcast_add_fusion.10), channel_id=1, source_target_pairs={{0,4},{4,8},{8,12},{12,14},{14,10},{10,6},{6,2},{2,0},{1,3},{5,1},... | collective-permute-start | bytes 884744 | tf_op jit(solution)/shard_map/ppermute | solution.py:571
  68.2 9.6 %collective-permute-start.7 = (f32[19,8,512]{2,1,0:T(8,128)S(1)}, f32[19,8,512]{2,1,0:T(8,128)S(1)}, u32[]{:S(2)}, u32[]{:S(2)}) collective-permute-start(f32[19,8,512]{2,1,0:T(8,128)S(1)} %bitcast_add_fusion.4), channel_id=1, source_target_pairs={{0,4},{4,8},{8,12},{12,14},{14,10},{10,6},{6,2},{2,0},{1,3},{5,1},... | collective-permute-start | bytes 933896 | tf_op jit(solution)/shard_map/ppermute | solution.py:571
  73.8 7.4 %collective-permute-start.30 = (f32[18,8,512]{2,1,0:T(8,128)S(1)}, f32[18,8,512]{2,1,0:T(8,128)S(1)}, u32[]{:S(2)}, u32[]{:S(2)}) collective-permute-start(f32[18,8,512]{2,1,0:T(8,128)S(1)} %bitcast_add_fusion.15), channel_id=1, source_target_pairs={{0,4},{4,8},{8,12},{12,14},{14,10},{10,6},{6,2},{2,0},{1,3},{5,1},... | collective-permute-start | bytes 884744 | tf_op jit(solution)/shard_map/ppermute | solution.py:571
  77.9 7.0 %collective-permute-start.8 = (f32[19,8,512]{2,1,0:T(8,128)S(1)}, f32[19,8,512]{2,1,0:T(8,128)S(1)}, u32[]{:S(2)}, u32[]{:S(2)}) collective-permute-start(f32[19,8,512]{2,1,0:T(8,128)S(1)} %bitcast_add_fusion.3), channel_id=1, source_target_pairs={{0,4},{4,8},{8,12},{12,14},{14,10},{10,6},{6,2},{2,0},{1,3},{5,1},... | collective-permute-start | bytes 933896 | tf_op jit(solution)/shard_map/ppermute | solution.py:571
  79.6 8.4 %collective-permute-start.41 = (f32[18,8,512]{2,1,0:T(8,128)S(1)}, f32[18,8,512]{2,1,0:T(8,128)S(1)}, u32[]{:S(2)}, u32[]{:S(2)}) collective-permute-start(f32[18,8,512]{2,1,0:T(8,128)S(1)} %bitcast_add_fusion.9), channel_id=1, source_target_pairs={{0,4},{4,8},{8,12},{12,14},{14,10},{10,6},{6,2},{2,0},{1,3},{5,1},... | collective-permute-start | bytes 884744 | tf_op jit(solution)/shard_map/ppermute | solution.py:571
  81.2 10.0 %collective-permute-start.31 = (f32[18,8,512]{2,1,0:T(8,128)S(1)}, f32[18,8,512]{2,1,0:T(8,128)S(1)}, u32[]{:S(2)}, u32[]{:S(2)}) collective-permute-start(f32[18,8,512]{2,1,0:T(8,128)S(1)} %bitcast_add_fusion.14), channel_id=1, source_target_pairs={{0,4},{4,8},{8,12},{12,14},{14,10},{10,6},{6,2},{2,0},{1,3},{5,1},... | collective-permute-start | bytes 884744 | tf_op jit(solution)/shard_map/ppermute | solution.py:571
  84.9 9.6 %collective-permute-start.9 = (f32[19,8,512]{2,1,0:T(8,128)S(1)}, f32[19,8,512]{2,1,0:T(8,128)S(1)}, u32[]{:S(2)}, u32[]{:S(2)}) collective-permute-start(f32[19,8,512]{2,1,0:T(8,128)S(1)} %bitcast_add_fusion.2), channel_id=1, source_target_pairs={{0,4},{4,8},{8,12},{12,14},{14,10},{10,6},{6,2},{2,0},{1,3},{5,1},... | collective-permute-start | bytes 933896 | tf_op jit(solution)/shard_map/ppermute | solution.py:571
  88.0 9.6 %collective-permute-start.42 = (f32[18,8,512]{2,1,0:T(8,128)S(1)}, f32[18,8,512]{2,1,0:T(8,128)S(1)}, u32[]{:S(2)}, u32[]{:S(2)}) collective-permute-start(f32[18,8,512]{2,1,0:T(8,128)S(1)} %bitcast_add_fusion.8), channel_id=1, source_target_pairs={{0,4},{4,8},{8,12},{12,14},{14,10},{10,6},{6,2},{2,0},{1,3},{5,1},... | collective-permute-start | bytes 884744 | tf_op jit(solution)/shard_map/ppermute | solution.py:571
  91.2 9.6 %collective-permute-start.32 = (f32[18,8,512]{2,1,0:T(8,128)S(1)}, f32[18,8,512]{2,1,0:T(8,128)S(1)}, u32[]{:S(2)}, u32[]{:S(2)}) collective-permute-start(f32[18,8,512]{2,1,0:T(8,128)S(1)} %bitcast_add_fusion.13), channel_id=1, source_target_pairs={{0,4},{4,8},{8,12},{12,14},{14,10},{10,6},{6,2},{2,0},{1,3},{5,1},... | collective-permute-start | bytes 884744 | tf_op jit(solution)/shard_map/ppermute | solution.py:571
  94.5 9.6 %collective-permute-start.10 = (f32[19,8,512]{2,1,0:T(8,128)S(1)}, f32[19,8,512]{2,1,0:T(8,128)S(1)}, u32[]{:S(2)}, u32[]{:S(2)}) collective-permute-start(f32[19,8,512]{2,1,0:T(8,128)S(1)} %bitcast_add_fusion.1), channel_id=1, source_target_pairs={{0,4},{4,8},{8,12},{12,14},{14,10},{10,6},{6,2},{2,0},{1,3},{5,1},... | collective-permute-start | bytes 933896 | tf_op jit(solution)/shard_map/ppermute | solution.py:571
  97.7 9.6 %collective-permute-start.43 = (f32[18,8,512]{2,1,0:T(8,128)S(1)}, f32[18,8,512]{2,1,0:T(8,128)S(1)}, u32[]{:S(2)}, u32[]{:S(2)}) collective-permute-start(f32[18,8,512]{2,1,0:T(8,128)S(1)} %bitcast_add_fusion.7), channel_id=1, source_target_pairs={{0,4},{4,8},{8,12},{12,14},{14,10},{10,6},{6,2},{2,0},{1,3},{5,1},... | collective-permute-start | bytes 884744 | tf_op jit(solution)/shard_map/ppermute | solution.py:571
  100.8 9.6 %collective-permute-start.33 = (f32[18,8,512]{2,1,0:T(8,128)S(1)}, f32[18,8,512]{2,1,0:T(8,128)S(1)}, u32[]{:S(2)}, u32[]{:S(2)}) collective-permute-start(f32[18,8,512]{2,1,0:T(8,128)S(1)} %bitcast_add_fusion.12), channel_id=1, source_target_pairs={{0,4},{4,8},{8,12},{12,14},{14,10},{10,6},{6,2},{2,0},{1,3},{5,1},... | collective-permute-start | bytes 884744 | tf_op jit(solution)/shard_map/ppermute | solution.py:571
  104.2 14.3 %collective-permute-start.11 = (f32[19,8,512]{2,1,0:T(8,128)S(1)}, f32[19,8,512]{2,1,0:T(8,128)S(1)}, u32[]{:S(2)}, u32[]{:S(2)}) collective-permute-start(f32[19,8,512]{2,1,0:T(8,128)S(1)} %bitcast_add_fusion), channel_id=1, source_target_pairs={{0,4},{4,8},{8,12},{12,14},{14,10},{10,6},{6,2},{2,0},{1,3},{5,1},... | collective-permute-start | bytes 933896 | tf_op jit(solution)/shard_map/ppermute | solution.py:571
  107.3 9.6 %collective-permute-start.44 = (f32[18,8,512]{2,1,0:T(8,128)S(1)}, f32[18,8,512]{2,1,0:T(8,128)S(1)}, u32[]{:S(2)}, u32[]{:S(2)}) collective-permute-start(f32[18,8,512]{2,1,0:T(8,128)S(1)} %bitcast_add_fusion.6), channel_id=1, source_target_pairs={{0,4},{4,8},{8,12},{12,14},{14,10},{10,6},{6,2},{2,0},{1,3},{5,1},... | collective-permute-start | bytes 884744 | tf_op jit(solution)/shard_map/ppermute | solution.py:571
  109.0 11.2 %collective-permute-start.55 = (f32[18,8,512]{2,1,0:T(8,128)S(1)}, f32[18,8,512]{2,1,0:T(8,128)S(1)}, u32[]{:S(2)}, u32[]{:S(2)}) collective-permute-start(f32[18,8,512]{2,1,0:T(8,128)S(1)} %bitcast_add_fusion.12), channel_id=1, source_target_pairs={{0,1},{1,0},{2,3},{3,2},{4,5},{5,4},{6,7},{7,6},{8,9},{9,8},{10,11... | collective-permute-start | bytes 884744 | tf_op jit(solution)/shard_map/ppermute | solution.py:549
  109.0 16.2 %collective-permute-start.49 = (f32[18,8,512]{2,1,0:T(8,128)S(1)}, f32[18,8,512]{2,1,0:T(8,128)S(1)}, u32[]{:S(2)}, u32[]{:S(2)}) collective-permute-start(f32[18,8,512]{2,1,0:T(8,128)S(1)} %bitcast_add_fusion.6), channel_id=1, source_target_pairs={{0,1},{1,0},{2,3},{3,2},{4,5},{5,4},{6,7},{7,6},{8,9},{9,8},{10,11... | collective-permute-start | bytes 884744 | tf_op jit(solution)/shard_map/ppermute | solution.py:549
  110.5 14.8 %collective-permute-start.34 = (f32[18,8,512]{2,1,0:T(8,128)S(1)}, f32[18,8,512]{2,1,0:T(8,128)S(1)}, u32[]{:S(2)}, u32[]{:S(2)}) collective-permute-start(f32[18,8,512]{2,1,0:T(8,128)S(1)} %collective-permute-done.33), channel_id=1, source_target_pairs={{0,4},{4,8},{8,12},{12,14},{14,10},{10,6},{6,2},{2,0},{1,3},{5,1},... | collective-permute-start | bytes 884744 | tf_op jit(solution)/shard_map/ppermute | solution.py:571
  118.6 8.3 %collective-permute-start.12 = (f32[18,8,512]{2,1,0:T(8,128)S(1)}, f32[18,8,512]{2,1,0:T(8,128)S(1)}, u32[]{:S(2)}, u32[]{:S(2)}) collective-permute-start(f32[18,8,512]{2,1,0:T(8,128)S(1)} %slice_add_fusion), channel_id=1, source_target_pairs={{0,4},{4,8},{8,12},{12,14},{14,10},{10,6},{6,2},{2,0},{1,3},{5,1},... | collective-permute-start | bytes 884744 | tf_op jit(solution)/shard_map/ppermute | solution.py:571
  120.2 9.1 %collective-permute-start.50 = (f32[18,8,512]{2,1,0:T(8,128)S(1)}, f32[18,8,512]{2,1,0:T(8,128)S(1)}, u32[]{:S(2)}, u32[]{:S(2)}) collective-permute-start(f32[18,8,512]{2,1,0:T(8,128)S(1)} %collective-permute-done.44), channel_id=1, source_target_pairs={{0,1},{1,0},{2,3},{3,2},{4,5},{5,4},{6,7},{7,6},{8,9},{9,8},{10,11... | collective-permute-start | bytes 884744 | tf_op jit(solution)/shard_map/ppermute | solution.py:549
  123.7 7.2 %collective-permute-start.46 = (f32[18,8,512]{2,1,0:T(8,128)S(1)}, f32[18,8,512]{2,1,0:T(8,128)S(1)}, u32[]{:S(2)}, u32[]{:S(2)}) collective-permute-start(f32[18,8,512]{2,1,0:T(8,128)S(1)} %collective-permute-done.45), channel_id=1, source_target_pairs={{0,4},{4,8},{8,12},{12,14},{14,10},{10,6},{6,2},{2,0},{1,3},{5,1},... | collective-permute-start | bytes 884744 | tf_op jit(solution)/shard_map/ppermute | solution.py:571
  129.3 7.4 %collective-permute-start.35 = (f32[18,8,512]{2,1,0:T(8,128)S(1)}, f32[18,8,512]{2,1,0:T(8,128)S(1)}, u32[]{:S(2)}, u32[]{:S(2)}) collective-permute-start(f32[18,8,512]{2,1,0:T(8,128)S(1)} %collective-permute-done.34), channel_id=1, source_target_pairs={{0,4},{4,8},{8,12},{12,14},{14,10},{10,6},{6,2},{2,0},{1,3},{5,1},... | collective-permute-start | bytes 884744 | tf_op jit(solution)/shard_map/ppermute | solution.py:571
  130.9 7.4 %collective-permute-start.52 = (f32[18,8,512]{2,1,0:T(8,128)S(1)}, f32[18,8,512]{2,1,0:T(8,128)S(1)}, u32[]{:S(2)}, u32[]{:S(2)}) collective-permute-start(f32[18,8,512]{2,1,0:T(8,128)S(1)} %collective-permute-done.46), channel_id=1, source_target_pairs={{0,1},{1,0},{2,3},{3,2},{4,5},{5,4},{6,7},{7,6},{8,9},{9,8},{10,11... | collective-permute-start | bytes 884744 | tf_op jit(solution)/shard_map/ppermute | solution.py:549
  130.9 9.0 %collective-permute-start.47 = (f32[18,8,512]{2,1,0:T(8,128)S(1)}, f32[18,8,512]{2,1,0:T(8,128)S(1)}, u32[]{:S(2)}, u32[]{:S(2)}) collective-permute-start(f32[18,8,512]{2,1,0:T(8,128)S(1)} %collective-permute-done.46), channel_id=1, source_target_pairs={{0,4},{4,8},{8,12},{12,14},{14,10},{10,6},{6,2},{2,0},{1,3},{5,1},... | collective-permute-start | bytes 884744 | tf_op jit(solution)/shard_map/ppermute | solution.py:571
  132.1 9.2 %collective-permute-start.16 = (f32[18,8,512]{2,1,0:T(8,128)S(1)}, f32[18,8,512]{2,1,0:T(8,128)S(1)}, u32[]{:S(2)}, u32[]{:S(2)}) collective-permute-start(f32[18,8,512]{2,1,0:T(8,128)S(1)} %collective-permute-done.12), channel_id=1, source_target_pairs={{0,1},{1,0},{2,3},{3,2},{4,5},{5,4},{6,7},{7,6},{8,9},{9,8},{10,11... | collective-permute-start | bytes 884744 | tf_op jit(solution)/shard_map/ppermute | solution.py:549
  133.6 8.4 %collective-permute-start.17 = (f32[18,8,512]{2,1,0:T(8,128)S(1)}, f32[18,8,512]{2,1,0:T(8,128)S(1)}, u32[]{:S(2)}, u32[]{:S(2)}) collective-permute-start(f32[18,8,512]{2,1,0:T(8,128)S(1)} %collective-permute-done.13), channel_id=1, source_target_pairs={{0,1},{1,0},{2,3},{3,2},{4,5},{5,4},{6,7},{7,6},{8,9},{9,8},{10,11... | collective-permute-start | bytes 884744 | tf_op jit(solution)/shard_map/ppermute | solution.py:549
  138.3 8.3 %collective-permute-start.36 = (f32[18,8,512]{2,1,0:T(8,128)S(1)}, f32[18,8,512]{2,1,0:T(8,128)S(1)}, u32[]{:S(2)}, u32[]{:S(2)}) collective-permute-start(f32[18,8,512]{2,1,0:T(8,128)S(1)} %collective-permute-done.35), channel_id=1, source_target_pairs={{0,4},{4,8},{8,12},{12,14},{14,10},{10,6},{6,2},{2,0},{1,3},{5,1},... | collective-permute-start | bytes 884744 | tf_op jit(solution)/shard_map/ppermute | solution.py:571
  141.9 7.8 %collective-permute-start.53 = (f32[18,8,512]{2,1,0:T(8,128)S(1)}, f32[18,8,512]{2,1,0:T(8,128)S(1)}, u32[]{:S(2)}, u32[]{:S(2)}) collective-permute-start(f32[18,8,512]{2,1,0:T(8,128)S(1)} %collective-permute-done.47), channel_id=1, source_target_pairs={{0,4},{4,8},{8,12},{12,14},{14,10},{10,6},{6,2},{2,0},{1,3},{5,1},... | collective-permute-start | bytes 884744 | tf_op jit(solution)/shard_map/ppermute | solution.py:571
  148.2 8.4 %collective-permute-start.48 = (f32[18,8,512]{2,1,0:T(8,128)S(1)}, f32[18,8,512]{2,1,0:T(8,128)S(1)}, u32[]{:S(2)}, u32[]{:S(2)}) collective-permute-start(f32[18,8,512]{2,1,0:T(8,128)S(1)} %collective-permute-done.47), channel_id=1, source_target_pairs={{0,1},{1,0},{2,3},{3,2},{4,5},{5,4},{6,7},{7,6},{8,9},{9,8},{10,11... | collective-permute-start | bytes 884744 | tf_op jit(solution)/shard_map/ppermute | solution.py:549
  149.8 8.4 %collective-permute-start.54 = (f32[18,8,512]{2,1,0:T(8,128)S(1)}, f32[18,8,512]{2,1,0:T(8,128)S(1)}, u32[]{:S(2)}, u32[]{:S(2)}) collective-permute-start(f32[18,8,512]{2,1,0:T(8,128)S(1)} %collective-permute-done.53), channel_id=1, source_target_pairs={{0,1},{1,0},{2,3},{3,2},{4,5},{5,4},{6,7},{7,6},{8,9},{9,8},{10,11... | collective-permute-start | bytes 884744 | tf_op jit(solution)/shard_map/ppermute | solution.py:549
  149.8 9.5 %collective-permute-start.37 = (f32[18,8,512]{2,1,0:T(8,128)S(1)}, f32[18,8,512]{2,1,0:T(8,128)S(1)}, u32[]{:S(2)}, u32[]{:S(2)}) collective-permute-start(f32[18,8,512]{2,1,0:T(8,128)S(1)} %collective-permute-done.36), channel_id=1, source_target_pairs={{0,4},{4,8},{8,12},{12,14},{14,10},{10,6},{6,2},{2,0},{1,3},{5,1},... | collective-permute-start | bytes 884744 | tf_op jit(solution)/shard_map/ppermute | solution.py:571
  151.3 9.6 %collective-permute-start.22 = (f32[18,8,512]{2,1,0:T(8,128)S(1)}, f32[18,8,512]{2,1,0:T(8,128)S(1)}, u32[]{:S(2)}, u32[]{:S(2)}) collective-permute-start(f32[18,8,512]{2,1,0:T(8,128)S(1)} %collective-permute-done.14), channel_id=1, source_target_pairs={{0,1},{1,0},{2,3},{3,2},{4,5},{5,4},{6,7},{7,6},{8,9},{9,8},{10,11... | collective-permute-start | bytes 884744 | tf_op jit(solution)/shard_map/ppermute | solution.py:549
  153.3 7.1 %collective-permute-start.19 = (f32[18,8,512]{2,1,0:T(8,128)S(1)}, f32[18,8,512]{2,1,0:T(8,128)S(1)}, u32[]{:S(2)}, u32[]{:S(2)}) collective-permute-start(f32[18,8,512]{2,1,0:T(8,128)S(1)} %collective-permute-done.18), channel_id=1, source_target_pairs={{0,4},{4,8},{8,12},{12,14},{14,10},{10,6},{6,2},{2,0},{1,3},{5,1},... | collective-permute-start | bytes 884744 | tf_op jit(solution)/shard_map/ppermute | solution.py:571
  159.2 7.3 %collective-permute-start.60 = (f32[18,8,512]{2,1,0:T(8,128)S(1)}, f32[18,8,512]{2,1,0:T(8,128)S(1)}, u32[]{:S(2)}, u32[]{:S(2)}) collective-permute-start(f32[18,8,512]{2,1,0:T(8,128)S(1)} %collective-permute-done.37), channel_id=1, source_target_pairs={{0,4},{4,8},{8,12},{12,14},{14,10},{10,6},{6,2},{2,0},{1,3},{5,1},... | collective-permute-start | bytes 884744 | tf_op jit(solution)/shard_map/ppermute | solution.py:571
  160.4 7.6 %collective-permute-start.24 = (f32[18,8,512]{2,1,0:T(8,128)S(1)}, f32[18,8,512]{2,1,0:T(8,128)S(1)}, u32[]{:S(2)}, u32[]{:S(2)}) collective-permute-start(f32[18,8,512]{2,1,0:T(8,128)S(1)} %collective-permute-done.19), channel_id=1, source_target_pairs={{0,1},{1,0},{2,3},{3,2},{4,5},{5,4},{6,7},{7,6},{8,9},{9,8},{10,11... | collective-permute-start | bytes 884744 | tf_op jit(solution)/shard_map/ppermute | solution.py:549
  161.0 8.7 %collective-permute-start.20 = (f32[18,8,512]{2,1,0:T(8,128)S(1)}, f32[18,8,512]{2,1,0:T(8,128)S(1)}, u32[]{:S(2)}, u32[]{:S(2)}) collective-permute-start(f32[18,8,512]{2,1,0:T(8,128)S(1)} %collective-permute-done.19), channel_id=1, source_target_pairs={{0,4},{4,8},{8,12},{12,14},{14,10},{10,6},{6,2},{2,0},{1,3},{5,1},... | collective-permute-start | bytes 884744 | tf_op jit(solution)/shard_map/ppermute | solution.py:571
  163.4 7.8 %collective-permute-start.61 = (f32[18,8,512]{2,1,0:T(8,128)S(1)}, f32[18,8,512]{2,1,0:T(8,128)S(1)}, u32[]{:S(2)}, u32[]{:S(2)}) collective-permute-start(f32[18,8,512]{2,1,0:T(8,128)S(1)} %collective-permute-done.37), channel_id=1, source_target_pairs={{0,1},{1,0},{2,3},{3,2},{4,5},{5,4},{6,7},{7,6},{8,9},{9,8},{10,11... | collective-permute-start | bytes 884744 | tf_op jit(solution)/shard_map/ppermute | solution.py:549
  166.5 7.2 %collective-permute-start.67 = (f32[18,8,512]{2,1,0:T(8,128)S(1)}, f32[18,8,512]{2,1,0:T(8,128)S(1)}, u32[]{:S(2)}, u32[]{:S(2)}) collective-permute-start(f32[18,8,512]{2,1,0:T(8,128)S(1)} %collective-permute-done.65), channel_id=1, source_target_pairs={{0,4},{4,8},{8,12},{12,14},{14,10},{10,6},{6,2},{2,0},{1,3},{5,1},... | collective-permute-start | bytes 884744 | tf_op jit(solution)/shard_map/ppermute | solution.py:571
  172.3 7.3 %collective-permute-start.63 = (f32[18,8,512]{2,1,0:T(8,128)S(1)}, f32[18,8,512]{2,1,0:T(8,128)S(1)}, u32[]{:S(2)}, u32[]{:S(2)}) collective-permute-start(f32[18,8,512]{2,1,0:T(8,128)S(1)} %collective-permute-done.60), channel_id=1, source_target_pairs={{0,4},{4,8},{8,12},{12,14},{14,10},{10,6},{6,2},{2,0},{1,3},{5,1},... | collective-permute-start | bytes 884744 | tf_op jit(solution)/shard_map/ppermute | solution.py:571
  (29 other events, 225.5 us)

commit v2 on v1

--- a/solution.py
+++ b/solution.py
@@ -34,12 +34,12 @@
     )(*args)
 
 
-def spread(value, cat_ref, count):
-    rows, width = value.shape
-    edge = count * STEP
-    for at, shift in enumerate((count, 0, rows - count)):
-        moved = value if shift == 0 else pltpu.roll(value, shift, 0)
-        cat_ref[edge : edge + rows, at * width : (at + 1) * width] = moved.astype(BF16)
+def spread_block(block, cat_ref, i, count):
+    edge, width = block.shape
+    here = pl.ds(pl.multiple_of((i + 1) * edge, edge), edge)
+    for at, shift in enumerate((count, 0, edge - count)):
+        moved = block if shift == 0 else pltpu.roll(block, shift, 0)
+        cat_ref[here, at * width : (at + 1) * width] = moved.astype(BF16)
 
 
 def clear_edges(cat_ref, count):
@@ -63,9 +63,10 @@
             acc_ref[...] += part
 
 
-def back_into(acc_ref, cat_ref, w_ref, edge):
+def back_into(acc_ref, cat_ref, w_ref, edge, loads):
     rows, width = acc_ref.shape[0], w_ref.shape[2]
     for r in range(3):
+        loads[r].wait()
         for c in range(3):
             part = lax.dot_general(
                 cat_ref[(2 - r) * edge : (2 - r) * edge + rows, (2 - c) * width : (3 - c) * width],
@@ -85,9 +86,9 @@
 
 def head_kernel(
     total, counts_hbm, frames_hbm, w3_hbm, b3_hbm, w4_hbm, b4_hbm, cot_hbm,
-    out_hbm, mine_hbm, slope_hbm, field_mine_hbm, send_hbm,
+    out_hbm, mine_hbm, slope_hbm, delta_hbm, field_mine_hbm, send_hbm,
     counts_ref, frames_ref, w3_ref, b3_ref, w4_ref, b4_ref, cot_ref,
-    field_ref, act_ref, acc_ref, slope_ref, delta_ref, out_ref, block3_ref, block_ref, cat3_ref, cat4_ref,
+    field_ref, act_ref, acc_ref, slope_ref, delta_ref, short_ref, out_ref, block3_ref, block_ref, cat3_ref, cat4_ref,
     in_sems, out_sems,
 ):
     sources = (frames_hbm, counts_hbm, w3_hbm, b3_hbm, b4_hbm, w4_hbm, cot_hbm)
@@ -100,11 +101,11 @@
         load.start()
     side, count = frames_ref.shape[0], frames_ref.shape[2]
     edge = count * STEP
+    rows = side * edge
     valid = side * count
     videos = counts_ref.shape[0]
     half3, half4 = field_mine_hbm.shape[1], mine_hbm.shape[1]
-    c_out = delta_ref.shape[1]
-    delta_hbm = send_hbm.at[:, 0:c_out]
+    c_mid, c_out = slope_ref.shape[1], delta_ref.shape[1]
 
     block3_ref[...] = jnp.zeros_like(block3_ref)
     block_ref[...] = jnp.zeros_like(block_ref)
@@ -116,20 +117,26 @@
     def gather(i, _):
         for j in range(side):
             block3_ref[j * count : (j + 1) * count, :] = frames_ref[i, j].astype(F32)
-        field_ref[pl.ds(pl.multiple_of(i * edge, edge), edge), :] = block3_ref[...]
+        block = block3_ref[...]
+        field_ref[pl.ds(pl.multiple_of(i * edge, edge), edge), :] = block
+        spread_block(block, cat3_ref, i, count)
         return 0
 
-    lax.fori_loop(0, side, gather, 0)
-    spread(field_ref[...], cat3_ref, count)
+    lax.fori_loop(0, side, gather, 0, unroll=True)
     core = lax.axis_index("narrow")
     first = (lax.axis_index("wide") * lax.axis_size("narrow") + core) * count
 
-    def part(at, half):
-        return pl.ds(pl.multiple_of(at * half, half), half)
-
+    def part(at, half, start=0):
+        return pl.ds(pl.multiple_of(start + at * half, half), half)
+
+    inner = slice(edge, edge + rows)
     stores = [
-        pltpu.make_async_copy(field_ref.at[:, part(core, half3)], field_mine_hbm, out_sems.at[0]),
-        pltpu.make_async_copy(field_ref.at[:, part(1 - core, half3)], send_hbm.at[:, c_out + half4 :], out_sems.at[1]),
+        pltpu.make_async_copy(
+            cat3_ref.at[inner, part(core, half3, 2 * half3)], field_mine_hbm, out_sems.at[0]
+        ),
+        pltpu.make_async_copy(
+            field_ref.at[:, part(1 - core, half3)], send_hbm.at[:, c_out + half4 :], out_sems.at[1]
+        ),
     ]
 
     def owned(f):
@@ -158,19 +165,21 @@
         pre = acc_ref[here, :] + bias3
         sigma = jax.nn.sigmoid(pre)
         slope_ref[here, :] = silu_slope(pre, sigma)
-        act = jnp.where(row < valid, pre * sigma, 0.0)
-        act_ref[here, :] = act.astype(BF16).astype(F32)
+        act = jnp.where(row < valid, pre * sigma, 0.0).astype(BF16).astype(F32)
+        act_ref[here, :] = act
+        spread_block(act, cat4_ref, i, count)
         return 0
 
-    lax.fori_loop(0, side, silu_rows, 0)
+    lax.fori_loop(0, side, silu_rows, 0, unroll=True)
     stores += [
-        pltpu.make_async_copy(act_ref.at[:, part(1 - core, half4)], send_hbm.at[:, c_out : c_out + half4], out_sems.at[2]),
-        pltpu.make_async_copy(act_ref.at[:, part(core, half4)], mine_hbm, out_sems.at[3]),
+        pltpu.make_async_copy(
+            act_ref.at[:, part(1 - core, half4)], send_hbm.at[:, c_out : c_out + half4], out_sems.at[2]
+        ),
+        pltpu.make_async_copy(cat4_ref.at[inner, part(core, half4, c_mid)], mine_hbm, out_sems.at[3]),
         pltpu.make_async_copy(slope_ref, slope_hbm, out_sems.at[4]),
     ]
     for store in stores:
         store.start()
-    spread(act_ref[...], cat4_ref, count)
     for load in loads[5:]:
         load.wait()
     convolve_into(acc_ref, cat4_ref, w4_ref, edge)
@@ -182,19 +191,24 @@
             block_ref[j * count : (j + 1) * count, :] = cot_ref[i, j].astype(F32)
         pre = acc_ref[here, :] + bias4
         sigma = jax.nn.sigmoid(pre)
-        delta = block_ref[...] * scale * silu_slope(pre, sigma)
-        delta_ref[here, :] = delta.astype(BF16).astype(F32)
+        delta = (block_ref[...] * scale * silu_slope(pre, sigma)).astype(BF16)
+        short_ref[here, :] = delta
+        delta_ref[here, :] = delta.astype(F32)
         pltpu.make_async_copy(delta_ref.at[here], send_hbm.at[here, 0:c_out], out_sems.at[5]).start()
         out = pre * sigma
         for j in range(side):
             out_ref[i, j] = out[j * count : (j + 1) * count, :].astype(BF16)
         return 0
 
-    lax.fori_loop(0, side, last_rows, 0)
-    stores.append(pltpu.make_async_copy(out_ref, out_hbm, out_sems.at[6]))
-    stores[-1].start()
-    stores.append(pltpu.make_async_copy(delta_ref, delta_hbm, out_sems.at[5]))
-    for store in stores:
+    lax.fori_loop(0, side, last_rows, 0, unroll=True)
+    late = [
+        pltpu.make_async_copy(short_ref, delta_hbm, out_sems.at[6]),
+        pltpu.make_async_copy(out_ref, out_hbm, out_sems.at[7]),
+    ]
+    for store in late:
+        store.start()
+    stores.append(pltpu.make_async_copy(delta_ref, send_hbm.at[:, 0:c_out], out_sems.at[5]))
+    for store in stores + late:
         store.wait()
 
 
@@ -204,17 +218,18 @@
     rows = side * count * STEP
     edges = rows + 2 * count * STEP
 
-    def field(width):
-        return jax.ShapeDtypeStruct((rows, width), F32)
+    def field(width, dtype):
+        return jax.ShapeDtypeStruct((rows, width), dtype)
 
     return kernel_call(
         functools.partial(head_kernel, float(total)),
         (
             jax.ShapeDtypeStruct(cot.shape, BF16),
-            field(c_mid // 2),
-            field(c_mid),
-            field(c_in // 2),
-            field(c_out + c_mid // 2 + c_in // 2),
+            field(c_mid // 2, BF16),
+            field(c_mid, F32),
+            field(c_out, BF16),
+            field(c_in // 2, BF16),
+            field(c_out + c_mid // 2 + c_in // 2, F32),
         ),
         [
             pltpu.SMEM(clip_counts.shape, jnp.int32),
@@ -229,13 +244,14 @@
             pltpu.VMEM((rows, c_mid), F32),
             pltpu.VMEM((rows, c_mid), F32),
             pltpu.VMEM((rows, c_out), F32),
+            pltpu.VMEM((rows, c_out), BF16),
             pltpu.VMEM(cot.shape, BF16),
             pltpu.VMEM((count * STEP, c_in), F32),
             pltpu.VMEM((count * STEP, c_out), F32),
             pltpu.VMEM((edges, 3 * c_in), BF16),
             pltpu.VMEM((edges, 3 * c_mid), BF16),
             pltpu.SemaphoreType.DMA((7,)),
-            pltpu.SemaphoreType.DMA((7,)),
+            pltpu.SemaphoreType.DMA((8,)),
         ],
         HEAD_MIB,
         2 * rows * 9 * c_mid * (c_in + c_out),
@@ -243,77 +259,97 @@
     )
 
 
-def load_columns(pieces, target, sem):
-    copies, at = [], 0
-    for piece in pieces:
-        width = piece.shape[1]
-        copies.append(pltpu.make_async_copy(piece, target.at[:, at : at + width], sem.at[len(copies)]))
-        at += width
-    for copy in copies:
-        copy.start()
-    return copies
+def spread_delta(side, count, delta_ref, cat_ref):
+    edge = count * STEP
+    clear_edges(cat_ref, count)
+
+    def rows_of(i, _):
+        block = delta_ref[pl.ds(pl.multiple_of(i * edge, edge), edge), :]
+        spread_block(block.astype(F32), cat_ref, i, count)
+        return 0
+
+    return lambda: lax.fori_loop(0, side, rows_of, 0, unroll=True)
 
 
 def back4_kernel(
-    count, delta_hbm, slope_hbm, w_hbm, out_hbm, sums_hbm,
-    delta_ref, slope_ref, w_ref, cat_ref, acc_ref, out_ref, sums_ref, sems,
+    count, delta_hbm, slope_hbm, w_hbm, out_hbm, short_hbm, sums_hbm,
+    delta_ref, slope_ref, w_ref, cat_ref, acc_ref, out_ref, short_ref, sums_ref, sems,
 ):
     edge = count * STEP
     rows = out_ref.shape[0]
-    loads = [
-        pltpu.make_async_copy(delta_hbm.at[:, 0 : delta_ref.shape[1]], delta_ref, sems.at[0]),
-        pltpu.make_async_copy(w_hbm, w_ref, sems.at[1]),
-        pltpu.make_async_copy(slope_hbm, slope_ref, sems.at[2]),
+    side = rows // edge
+    load = pltpu.make_async_copy(delta_hbm, delta_ref, sems.at[0])
+    load_slope = pltpu.make_async_copy(slope_hbm, slope_ref, sems.at[1])
+    load_w = [
+        pltpu.make_async_copy(w_hbm.at[3 * r : 3 * r + 3], w_ref.at[3 * r : 3 * r + 3], sems.at[2 + r])
+        for r in range(3)
     ]
-    for load in loads:
-        load.start()
-    clear_edges(cat_ref, count)
-    loads[0].wait()
-    spread(delta_ref[...], cat_ref, count)
-    loads[1].wait()
-    back_into(acc_ref, cat_ref, w_ref, edge)
-    loads[2].wait()
-    side = rows // edge
+    for copy in [load] + load_w + [load_slope]:
+        copy.start()
+    spread = spread_delta(side, count, delta_ref, cat_ref)
+    load.wait()
+    spread()
+    back_into(acc_ref, cat_ref, w_ref, edge, load_w)
+    load_slope.wait()
     valid = lax.broadcasted_iota(jnp.int32, (edge, 1), 0) < side * count
 
     def rows_of(i, carry):
         here = pl.ds(pl.multiple_of(i * edge, edge), edge)
-        delta = jnp.where(valid, acc_ref[here, :] * slope_ref[here, :], 0.0)
-        delta = delta.astype(BF16).astype(F32)
-        out_ref[here, :] = delta
-        pltpu.make_async_copy(out_ref.at[here], out_hbm.at[here], sems.at[3]).start()
+        delta = jnp.where(valid, acc_ref[here, :] * slope_ref[here, :], 0.0).astype(BF16)
+        short_ref[here, :] = delta
+        long = delta.astype(F32)
+        out_ref[here, :] = long
         sum3, sum4 = carry
         return (
-            sum3 + jnp.sum(delta, 0, keepdims=True),
-            sum4 + jnp.sum(delta_ref[here, :], 0, keepdims=True),
+            sum3 + jnp.sum(long, 0, keepdims=True),
+            sum4 + jnp.sum(delta_ref[here, :].astype(F32), 0, keepdims=True),
         )
 
+    def store(i):
+        here = pl.ds(pl.multiple_of(i * edge, edge), edge)
+        return pltpu.make_async_copy(out_ref.at[here], out_hbm.at[here], sems.at[5])
+
+    def stored_rows(i, carry):
+        carry = rows_of(i, carry)
+        store(i).start()
+        return carry
+
     nothing = (jnp.zeros((1, out_ref.shape[1]), F32), jnp.zeros((1, delta_ref.shape[1]), F32))
-    sums_ref[0:1, :], sums_ref[1:2, :] = lax.fori_loop(0, side, rows_of, nothing)
-    stores = [
-        pltpu.make_async_copy(out_ref, out_hbm, sems.at[3]),
-        pltpu.make_async_copy(sums_ref, sums_hbm, sems.at[4]),
+    sum3, sum4 = rows_of(side - 1, lax.fori_loop(0, side - 1, stored_rows, nothing, unroll=True))
+    sums_ref[0:1, :], sums_ref[1:2, :] = sum3, sum4
+    spare = (side - 1) * edge + (side + 1) * count
+    out_ref[spare : spare + 2, :] = sums_ref[...]
+    store(side - 1).start()
+    late = [
+        pltpu.make_async_copy(short_ref, short_hbm, sems.at[6]),
+        pltpu.make_async_copy(sums_ref, sums_hbm, sems.at[7]),
     ]
-    stores[1].start()
-    for store in stores:
-        store.wait()
+    for copy in late:
+        copy.start()
+    for copy in late + [pltpu.make_async_copy(out_ref, out_hbm, sems.at[5])]:
+        copy.wait()
 
 
 def back4(count, delta, slope, w):
-    rows = delta.shape[0]
-    taps, c_mid, width = w.shape
+    rows, width = delta.shape
+    taps, c_mid, _ = w.shape
     return kernel_call(
         functools.partial(back4_kernel, count),
-        (jax.ShapeDtypeStruct((rows, c_mid), F32), jax.ShapeDtypeStruct((2, width), F32)),
+        (
+            jax.ShapeDtypeStruct((rows, c_mid), F32),
+            jax.ShapeDtypeStruct((rows, c_mid), BF16),
+            jax.ShapeDtypeStruct((2, width), F32),
+        ),
         [
-            pltpu.VMEM((rows, width), F32),
+            pltpu.VMEM((rows, width), BF16),
             pltpu.VMEM((rows, c_mid), F32),
-            pltpu.VMEM((taps, c_mid, width), BF16),
+            pltpu.VMEM(w.shape, BF16),
             pltpu.VMEM((rows + 2 * count * STEP, 3 * width), BF16),
             pltpu.VMEM((rows, c_mid), F32),
             pltpu.VMEM((rows, c_mid), F32),
+            pltpu.VMEM((rows, c_mid), BF16),
             pltpu.VMEM((2, width), F32),
-            pltpu.SemaphoreType.DMA((5,)),
+            pltpu.SemaphoreType.DMA((8,)),
         ],
         BACK4_MIB,
         2 * rows * c_mid * width * taps,
@@ -321,19 +357,20 @@
     )
 
 
-def back3_kernel(count, pieces, *refs):
-    deltas, (w_hbm, out_hbm, delta_ref, w_ref, cat_ref, acc_ref, out_ref, sems) = refs[:pieces], refs[pieces:]
+def back3_kernel(count, delta_hbm, w_hbm, out_hbm, delta_ref, w_ref, cat_ref, acc_ref, out_ref, sems):
     edge = count * STEP
-    loads = load_columns(deltas, delta_ref, sems)
-    load = pltpu.make_async_copy(w_hbm, w_ref, sems.at[pieces])
-    load.start()
-    clear_edges(cat_ref, count)
-    for copy in loads:
-        copy.wait()
-    spread(delta_ref[...], cat_ref, count)
+    side = out_ref.shape[0]
+    load = pltpu.make_async_copy(delta_hbm, delta_ref, sems.at[0])
+    load_w = [
+        pltpu.make_async_copy(w_hbm.at[3 * r : 3 * r + 3], w_ref.at[3 * r : 3 * r + 3], sems.at[1 + r])
+        for r in range(3)
+    ]
+    for copy in [load] + load_w:
+        copy.start()
+    spread = spread_delta(side, count, delta_ref, cat_ref)
     load.wait()
-    back_into(acc_ref, cat_ref, w_ref, edge)
-    side = out_ref.shape[0]
+    spread()
+    back_into(acc_ref, cat_ref, w_ref, edge, load_w)
 
     def rows_of(i, _):
         block = acc_ref[pl.ds(pl.multiple_of(i * edge, edge), edge), :]
@@ -341,38 +378,38 @@
             out_ref[i, j] = block[j * count : (j + 1) * count, :].astype(BF16)
         return 0
 
-    lax.fori_loop(0, side, rows_of, 0)
-    store = pltpu.make_async_copy(out_ref, out_hbm, sems.at[pieces + 1])
+    lax.fori_loop(0, side, rows_of, 0, unroll=True)
+    store = pltpu.make_async_copy(out_ref, out_hbm, sems.at[4])
     store.start()
     store.wait()
 
 
-def back3(side, count, deltas, w):
-    rows = deltas[0].shape[0]
-    taps, c_in, width = w.shape
+def back3(side, count, delta, w):
+    rows, width = delta.shape
+    taps, c_in, _ = w.shape
     return kernel_call(
-        functools.partial(back3_kernel, count, len(deltas)),
+        functools.partial(back3_kernel, count),
         jax.ShapeDtypeStruct((side, side, count, c_in), BF16),
         [
-            pltpu.VMEM((rows, width), F32),
+            pltpu.VMEM((rows, width), BF16),
             pltpu.VMEM(w.shape, BF16),
             pltpu.VMEM((rows + 2 * count * STEP, 3 * width), BF16),
             pltpu.VMEM((rows, c_in), F32),
             pltpu.VMEM((side, side, count, c_in), BF16),
-            pltpu.SemaphoreType.DMA((len(deltas) + 2,)),
+            pltpu.SemaphoreType.DMA((5,)),
         ],
         BACK3_MIB,
         2 * rows * c_in * width * taps,
-        *deltas, w,
+        delta, w,
     )
 
 
 def grad_kernel(count, side, lanes, chunks, size, places, tail, *refs):
-    sums_hbm, refs = refs[4 : 4 + 2 * tail], refs[:4] + refs[4 + 2 * tail :]
+    sums_hbm, refs = refs[4 : 4 + tail], refs[:4] + refs[4 + tail :]
     outs, (*targets, turned_ref, both_ref, acc_ref, sums_ref, in_sems, out_sems) = (
         refs[4 : 4 + 2 * lanes], refs[4 + 2 * lanes :],
     )
-    mine_ref, theirs_ref, delta_ref, other_ref = targets
+    mine_ref, theirs_ref, other_ref = targets
     _, spot, way = own_place(size)
     edge = count * STEP
     wide = 2 * edge
@@ -380,18 +417,21 @@
     groups = (0, side // 3, 2 * side // 3, side)
     loads = []
     for group in range(3):
+        steps = slice(groups[group], groups[group + 1])
         rows = slice(groups[group] * edge, groups[group + 1] * edge)
         loads.append([])
-        for at in range(4):
-            columns = slice(places[at], places[at] + targets[at].shape[1])
-            copy = pltpu.make_async_copy(
-                refs[at].at[rows, columns], targets[at].at[rows], in_sems.at[at, group]
-            )
+        for at, source in enumerate(refs[:4]):
+            if at == 2:
+                target = both_ref.at[steps, 0:edge]
+                source = source.at[steps]
+            else:
+                target = targets[min(at, 2)]
+                source = source.at[rows, places[at] : places[at] + target.shape[1]]
+                target = target.at[rows]
+            copy = pltpu.make_async_copy(source, target, in_sems.at[at, group])
             copy.start()
             loads[-1].append(copy)
-    extra = [
-        pltpu.make_async_copy(source, sums_ref.at[at], in_sems.at[4, at]) for at, source in enumerate(sums_hbm)
-    ]
+    extra = [pltpu.make_async_copy(source, sums_ref, in_sems.at[4, 0]) for source in sums_hbm]
     for load in extra:
         load.start()
     turned_ref[:, 0:wide] = jnp.zeros((3 * k, wide), BF16)
@@ -400,29 +440,30 @@
     def turn(i, carry):
         here = pl.ds(pl.multiple_of(i * edge, edge), edge)
         there = pl.ds(pl.multiple_of((i + 1) * wide, wide), wide)
-        turned = jnp.concatenate([mine_ref[here, :], theirs_ref[here, :]], 0).T
+        turned = jnp.concatenate([mine_ref[here, :].astype(F32), theirs_ref[here, :]], 0).T
         for c, shift in enumerate((count, 0, wide - count)):
             moved = turned if shift == 0 else pltpu.roll(turned, shift, 1)
             turned_ref[c * k : (c + 1) * k, there] = moved.astype(BF16)
-        to = pl.multiple_of(i * wide, wide)
-        both_ref[pl.ds(to, edge), :] = delta_ref[here, :].astype(BF16)
-        both_ref[pl.ds(to + edge, edge), :] = other_ref[here, :].astype(BF16)
+        both_ref[i, edge:wide, :] = other_ref[here, :].astype(BF16)
         return carry
 
     for group in range(3):
         for load in loads[group]:
             load.wait()
-        lax.fori_loop(groups[group], groups[group + 1], turn, 0)
+        lax.fori_loop(groups[group], groups[group + 1], turn, 0, unroll=True)
     blocks = 3 * k // (8 * lanes * chunks)
     if tail:
         for load in extra:
             load.wait()
         acc_ref[0, :, 3 * blocks] = jnp.zeros((chunks,) + acc_ref.shape[3:], F32)
-        acc_ref[0, 0, 3 * blocks, 0:2, :] = sums_ref[0] + sums_ref[1]
+        spare = (side - 1) * edge + (side + 1) * count
+        acc_ref[0, 0, 3 * blocks, 0:2, :] = sums_ref[...] + other_ref[spare : spare + 2, :]
     stores = []
     for r in range(3):
         part = jnp.dot(
-            turned_ref[:, r * wide : (r + side) * wide], both_ref[...], preferred_element_type=F32
+            turned_ref[:, r * wide : (r + side) * wide],
+            both_ref[...].reshape(side * wide, both_ref.shape[2]),
+            preferred_element_type=F32,
         )
         part = part.reshape((3, lanes, chunks, blocks // 3, 8, part.shape[1]))
         for chunk in range(chunks):
@@ -447,6 +488,7 @@
 def grad(mib, side, count, lanes, chunks, size, o, mine, theirs, delta, other, sums=()):
     arrays, places = zip(mine, theirs, delta, other)
     rows, k = arrays[0].shape
+    arrays = arrays[:2] + (arrays[2].reshape(side, count * STEP, o),) + arrays[3:]
     blocks = 9 * k // (8 * lanes * chunks) + (1 if sums else 0)
     first = jax.ShapeDtypeStruct((blocks, 8, o), F32)
     others = jax.ShapeDtypeStruct((max(chunks - 1, 1), blocks, 8, o), F32)
@@ -454,14 +496,13 @@
         functools.partial(grad_kernel, count, side, lanes, chunks, size, places, bool(sums)),
         (first, others) * lanes,
         [
-            pltpu.VMEM((rows, k), F32),
+            pltpu.VMEM((rows, k), BF16),
             pltpu.VMEM((rows, k), F32),
             pltpu.VMEM((rows, o), F32),
-            pltpu.VMEM((rows, o), F32),
             pltpu.VMEM((3 * k, 2 * count * STEP * (side + 2)), BF16),
-            pltpu.VMEM((2 * rows, o), BF16),
+            pltpu.VMEM((side, 2 * count * STEP, o), BF16),
             pltpu.VMEM((lanes, chunks, blocks, 8, o), F32),
-            pltpu.VMEM((2, 2, o), F32),
+            pltpu.VMEM((2, o), F32),
             pltpu.SemaphoreType.DMA((5, 3)),
             pltpu.SemaphoreType.DMA((6 * lanes,)),
         ],
@@ -554,7 +595,7 @@
 
 
 class Ring:
-    def __init__(self, size):
+    def __init__(self, size, zero):
         self.size = size
         order = list(range(0, size, 2)) + list(range(size - 1, 0, -2))
         self.pairs = []
@@ -566,6 +607,7 @@
         half = wide // 2
         self.place = jnp.where(wide % 2 == 0, half, size - 1 - half)
         self.way = 1 - 2 * self.core
+        self.zero = zero
 
     def send(self, value):
         return lax.ppermute(value, ("wide", "narrow"), self.pairs)
@@ -599,14 +641,15 @@
         last = self.ring.size - 1
         if number == last:
             self.keep(0)
-        got = self.ring.send(self.held)
+        got = self.got = self.ring.send(self.held)
         if number < last:
             self.passed.append(got)
-            self.held = got + self.parts[number]
-            if number == last - 1:
-                self.held = self.held[: self.blocks]
+            if number < last - 1:
+                self.held = got + self.parts[number]
+            else:
+                self.held = got[: self.blocks] + self.parts[number, : self.blocks]
         else:
-            self.held = got
+            self.held = got + self.ring.zero
             self.keep(number - last + 1)
 
 
@@ -629,7 +672,7 @@
     c_mid, c_out = w_three.shape[1], w_four.shape[1]
     taps3, taps4 = w_three.reshape(9, c_in, c_mid), w_four.reshape(9, c_mid, c_out)
     size = lax.axis_size("wide")
-    ring = Ring(size)
+    ring = Ring(size, jnp.minimum(clip_counts[0], 0).astype(F32))
     core = ring.core
     total_frames = count * size * lax.axis_size("narrow")
     def cells_first(field):
@@ -638,7 +681,7 @@
     def frames_first(field):
         return jnp.transpose(field, (2, 0, 1, 3))
 
-    output, act_mine, slope3, field_mine, send = head(
+    output, act_mine, slope3, delta4, field_mine, send = head(
         total_frames, clip_counts, cells_first(frames[0]), w_three, bias3, w_four, bias4,
         cells_first(cotangent[0]),
     )
@@ -646,22 +689,21 @@
     chunks = size if small else 1
     lanes4 = 2 if small else 1
     theirs = swap_cores(send)
-    delta3, sums = back4(count, send, slope3, taps4)
-    sums_theirs = swap_cores(sums)
-    delta3_theirs = swap_cores(delta3)
+    delta3_sums, delta3, sums = back4(count, delta4, slope3, taps4)
+    delta3_theirs = swap_cores(delta3_sums)
     grads4 = grad(
         62, side, count, lanes4, chunks, size, c_out,
-        (after(act_mine, delta3), 0), (theirs, c_out), (send, 0), (theirs, 0),
+        (after(act_mine, delta3), 0), (theirs, c_out), (delta4, 0), (theirs, 0),
     )
     def grad_of_3(mine, sums):
         return grad(
-            62, side, count, 1, chunks, size, c_mid,
+            24, side, count, 1, chunks, size, c_mid,
             (mine, 0), (theirs, c_out + c_mid // 2), (delta3, 0), (delta3_theirs, 0), sums,
         )[0]
 
     if not small:
         grads3 = grad_of_3(field_mine, ())
-        biases = lax.psum(sums + sums_theirs, "wide")
+        biases = lax.psum(sums, ("wide", "narrow"))
         sum3, sum4 = biases[0:1], biases[1:2]
         grad_w4 = collected(grads4[0][0].reshape(9, -1, c_out), core)
         grad_w3 = collected(grads3[0].reshape(9, -1, c_mid), core)
@@ -672,9 +714,9 @@
         y = Lane(grads4[1], ring, quarter, half4, blocks)
         x.step(0)
         y.step(0)
-        grads3 = grad_of_3(field_mine, (sums, sums_theirs))
+        grads3 = grad_of_3(field_mine, (sums,))
         z = Lane(grads3, ring, 0, half3, 9 * half3 // (8 * size))
-        z.held = after(z.held, x.held, y.held)
+        z.held = after(z.held, x.got, y.got)
         x.held, y.held = after(x.held, z.held), after(y.held, z.held)
         grad_w4 = grad_w3 = None
         shape3, shape4 = (9, c_in, c_mid), (9, c_mid, c_out)
@@ -700,12 +742,13 @@
             if number == size:
                 x.held = after(x.held, sum3)
             if number == 1:
-                field_grad = back3(side, count, [after(delta3, z.held)], taps3)
+                field_grad = back3(side, count, after(delta3, z.held), taps3)
             if number == 3:
                 z.held = after(z.held, field_grad)
-        grad_w3, grad_w4 = lay_lanes([(z, 0), (x, 1), (y, 1)], [grad_w3, grad_w4], [shape3, shape4])
+        grad_w3, grad_w4 = lay_lanes([(z, 0), (y, 1)], [grad_w3, grad_w4], [shape3, shape4])
+        (grad_w4,) = lay_lanes([(x, 0)], [grad_w4], [shape4])
     if not small:
-        field_grad = back3(side, count, [delta3], taps3)
+        field_grad = back3(side, count, delta3, taps3)
     return (
         frames_first(output)[None],
         frames_first(field_grad)[None],

time: 183 us -> 179 us (0.978)
  other arithmetic: 6.85 us -> 1.42 us
  starting transfers between devices: 69.5 us -> 74.5 us
  Pallas kernels: 50.6 us -> 47.8 us
  waiting for transfers between devices: 54.3 us -> 52 us
    add x21 -> x18, other arithmetic: 6.85 us -> 0.81 us  [step(): self.held = got + self.parts[number]]
    ppermute x42, starting transfers between devices: 66.1 us -> 70.1 us  [send(): return lax.ppermute(value, ('wide', 'narrow'), self.pairs)]
    pallas_call x13 -> x14, Pallas kernels: 50.6 us -> 47.8 us  [kernel_call(): pl.pallas_call(kernel, out_shape=outs, in_specs=[HBM] * len(args), out_sp...]
    ppermute x27 -> x26, starting transfers between devices: 3.36 us -> 4.4 us  [swap_cores(): return lax.ppermute(value, 'narrow', [(0, 1), (1, 0)])]
  transfers between devices with their start and end apart: 69 -> 68, of which waited for: 31 -> 33; matrix products, arithmetic and copies ran while one was open for 3% -> 1% of each run, Pallas kernels for 21% -> 20%
where the time goes in v2:
time: 179 us; the launch traced here: 178 us
  starting transfers between devices  74.5 us (42%)
  waiting for transfers between devices  52 us (29%)
  Pallas kernels  47.8 us (27%)
    ppermute x42, starting transfers between devices, send(): return lax.ppermute(value, ('wide', 'narrow'), self.pairs)  70.1 us
    ppermute x42, waiting for transfers between devices, send(): return lax.ppermute(value, ('wide', 'narrow'), self.pairs)  51.9 us
    pallas_call x14, Pallas kernels, kernel_call(): pl.pallas_call(kernel, out_shape=outs, in_specs=[HBM] * len(args), out_sp...  47.8 us
    ppermute x26, starting transfers between devices, swap_cores(): return lax.ppermute(value, 'narrow', [(0, 1), (1, 0)])  4.4 us
  transfers between devices with their start and end apart: 68, of which 33 were waited for; matrix products, arithmetic and copies ran while one was open for 1% of the time, Pallas kernels for 20%

profile of v2, /device:TPU:0, one launch (start us, length us, event | category | flops | bytes accessed | tf_op | source)
XLA Modules:
  0.0 178.3 jit_solution(15784022570112706796)
XLA Ops:
  0.6 10.6 %shard_map.118 = (bf16[13,13,4,512]{3,2,1,0:T(4,128)(2,1)}, bf16[832,256]{1,0:T(8,128)(2,1)}, f32[832,512]{1,0:T(8,128)}, bf16[832,512]{1,0:T(8,128)(2,1)}, bf16...) custom-call(s32[8]{0:T(128)} %counts_hbm.1, bf16[13,13,4,256]{3,2,1,0:T(4,128)(2,1)} %bitcast.168, bf16[2304,512]{1,0:T(8,128)(2,1)} %bitcast.160, ...), custom_call_target="tpu_custom_call" | custom-call | flops 5888802816 | bytes 8388608 | tf_op jit(solution)/shard_map/pallas_call | solution.py:25
  11.8 7.5 %shard_map.119 = (f32[832,512]{1,0:T(8,128)}, bf16[832,512]{1,0:T(8,128)(2,1)}, f32[2,512]{1,0:T(2,128)}) custom-call(bf16[832,512]{1,0:T(8,128)(2,1)} %get-tuple-element.39.delta_hbm, f32[832,512]{1,0:T(8,128)} %get-tuple-element.40.slope_hbm, bf16[9,512,512]{2,1,0:T(8,128)(2,1)} %bitcast.166), custom_call_target="tpu_custom_call" | custom-call | flops 3925868544 | bytes 8388608 | tf_op jit(solution)/shard_map/pallas_call | solution.py:25
  19.5 8.1 %shard_map.121 = (f32[18,8,512]{2,1,0:T(8,128)}, f32[7,18,8,512]{3,2,1,0:T(8,128)}, f32[18,8,512]{2,1,0:T(8,128)}, f32[7,18,8,512]{3,2,1,0:T(8,128)}) custom-call(bf16[832,256]{1,0:T(8,128)(2,1)} %get-tuple-element.48.refs_0_, f32[832,896]{1,0:T(8,128)} %collective-permute-done.refs_1_.refs_3_, bf16[13,64,512]{2,1,0:T(8,128)(2,1)} %bitcast.170, ...), custom_call_target="tpu_custom_call" | custom-call | flops 3925868544 | bytes 8388608 | tf_op jit(solution)/shard_map/pallas_call | solution.py:25
  27.6 3.1 %collective-permute-start.2 = (f32[18,8,512]{2,1,0:T(8,128)}, f32[18,8,512]{2,1,0:T(8,128)S(1)}, u32[]{:S(2)}, u32[]{:S(2)}) collective-permute-start(f32[18,8,512]{2,1,0:T(8,128)} %get-tuple-element.49), channel_id=1, source_target_pairs={{0,4},{4,8},{8,12},{12,14},{14,10},{10,6},{6,2},{2,0},{1,3},{5,1},... | collective-permute-start | bytes 884744 | tf_op jit(solution)/shard_map/ppermute | solution.py:613
  33.4 5.6 %shard_map.120 = (f32[19,8,512]{2,1,0:T(8,128)S(1)}, f32[7,19,8,512]{3,2,1,0:T(8,128)S(1)}) custom-call(bf16[832,128]{1,0:T(8,128)(2,1)S(1)} %copy-done.2, f32[832,896]{1,0:T(8,128)} %collective-permute-done.refs_1_.refs_3_, bf16[13,64,512]{2,1,0:T(8,128)(2,1)S(1)} %bitcast.162, f32[832,512]{1,0:T(8,128)S(1)} %collective-permute-done.1.refs_3_, ...), custom_call_target="tpu_custom_call" | custom-call | flops 1962934272 | bytes 8388608 | tf_op jit(solution)/shard_map/pallas_call | solution.py:25
  39.1 1.8 collective-permute-start.26
  40.9 1.6 collective-permute-start.45
  42.5 1.6 collective-permute-start.4
  44.2 1.7 collective-permute-done.26
  45.9 1.8 collective-permute-start.27
  49.0 1.8 collective-permute-start.46
  52.4 1.8 collective-permute-start.5
  55.5 1.8 collective-permute-start.28
  58.7 1.8 collective-permute-start.47
  62.0 1.8 collective-permute-start.6
  63.8 5.0 %shard_map.122 = bf16[13,13,4,256]{3,2,1,0:T(4,128)(2,1)} custom-call(bf16[832,512]{1,0:T(8,128)(2,1)S(1)} %copy-done.1, bf16[9,256,512]{2,1,0:T(8,128)(2,1)S(1)} %bitcast.161), custom_call_target="tpu_custom_call" | custom-call | flops 1962934272 | bytes 8388608 | tf_op jit(solution)/shard_map/pallas_call | solution.py:25
  68.8 1.6 collective-permute-start.29
  71.7 1.8 collective-permute-start.7
  73.5 1.6 collective-permute-start.48
  75.7 1.6 collective-permute-start.30
  77.3 1.6 collective-permute-done.7.refs_4_
  79.0 1.6 collective-permute-start.8
  82.2 1.6 collective-permute-start.49
  85.3 1.6 collective-permute-start.31
  86.9 1.6 collective-permute-done.8.refs_5_
  88.6 1.6 collective-permute-start.9
  91.8 1.6 collective-permute-start.50
  95.0 1.6 collective-permute-start.32
  96.6 1.6 collective-permute-done.9.refs_6_
  98.3 1.6 collective-permute-start.10
  101.5 1.6 collective-permute-start.52
  104.6 1.6 collective-permute-start.33
  106.2 1.7 collective-permute-done.10.refs_7_
  108.0 1.6 collective-permute-start.11
  111.1 1.6 collective-permute-start.54
  114.3 1.6 collective-permute-start.34
  117.4 3.1 %collective-permute-done.54 = f32[18,8,512]{2,1,0:T(8,128)S(1)} collective-permute-done((f32[18,8,512]{2,1,0:T(8,128)S(1)}, f32[18,8,512]{2,1,0:T(8,128)S(1)}, u32[]{:S(2)}, u32[]{:S(2)}) %collective-permute-start.54) | collective-permute-done | bytes 294944 | tf_op jit(solution)/shard_map/ppermute | solution.py:613
  120.5 1.6 collective-permute-start.12
  123.7 1.6 collective-permute-start.56
  125.3 1.6 collective-permute-start.35
  127.9 2.5 %collective-permute-done.56 = f32[18,8,512]{2,1,0:T(8,128)S(1)} collective-permute-done((f32[18,8,512]{2,1,0:T(8,128)S(1)}, f32[18,8,512]{2,1,0:T(8,128)S(1)}, u32[]{:S(2)}, u32[]{:S(2)}) %collective-permute-start.56) | collective-permute-done | bytes 294944 | tf_op jit(solution)/shard_map/ppermute | solution.py:613
  130.4 1.6 collective-permute-start.13
  133.6 1.6 collective-permute-start.58
  149.1 1.6 collective-permute-done.62
  152.4 1.7 shard_map.127.refs_4_
  158.9 3.6 %collective-permute-done.64 = f32[18,8,512]{2,1,0:T(8,128)S(1)} collective-permute-done((f32[18,8,512]{2,1,0:T(8,128)S(1)}, f32[18,8,512]{2,1,0:T(8,128)S(1)}, u32[]{:S(2)}, u32[]{:S(2)}) %collective-permute-start.64) | collective-permute-done | bytes 294944 | tf_op jit(solution)/shard_map/ppermute | solution.py:613
  170.5 2.0 %collective-permute-done.24 = f32[18,8,512]{2,1,0:T(8,128)S(1)} collective-permute-done((f32[18,8,512]{2,1,0:T(8,128)S(1)}, f32[18,8,512]{2,1,0:T(8,128)S(1)}, u32[]{:S(2)}, u32[]{:S(2)}) %collective-permute-start.24) | collective-permute-done | bytes 294944 | tf_op jit(solution)/shard_map/ppermute | solution.py:613
  172.6 3.1 %collective-permute-done.66 = f32[18,8,512]{2,1,0:T(8,128)S(1)} collective-permute-done((f32[18,8,512]{2,1,0:T(8,128)S(1)}, f32[18,8,512]{2,1,0:T(8,128)S(1)}, u32[]{:S(2)}, u32[]{:S(2)}) %collective-permute-start.66) | collective-permute-done | bytes 294944 | tf_op jit(solution)/shard_map/ppermute | solution.py:613
  (158 shorter events, 61.2 us)
Async XLA Ops:
  11.3 8.2 %collective-permute-start = (f32[832,896]{1,0:T(8,128)}, f32[832,896]{1,0:T(8,128)}, u32[]{:S(2)}, u32[]{:S(2)}) collective-permute-start(f32[832,896]{1,0:T(8,128)} %get-tuple-element.43), channel_id=1, source_target_pairs={{0,1},{1,0},{2,3},{3,2},{4,5},{5,4},{6,7},{7,6},{8,9},{9,8},{10,11... | collective-permute-start | bytes 8945672 | tf_op jit(solution)/shard_map/ppermute | solution.py:590
  19.3 12.9 %collective-permute-start.1 = (f32[832,512]{1,0:T(8,128)}, f32[832,512]{1,0:T(8,128)S(1)}, u32[]{:S(2)}, u32[]{:S(2)}) collective-permute-start(f32[832,512]{1,0:T(8,128)} %get-tuple-element.44), channel_id=1, source_target_pairs={{0,1},{1,0},{2,3},{3,2},{4,5},{5,4},{6,7},{7,6},{8,9},{9,8},{10,11... | collective-permute-start | bytes 5111816 | tf_op jit(solution)/shard_map/ppermute | solution.py:590
  27.6 11.4 %collective-permute-start.2 = (f32[18,8,512]{2,1,0:T(8,128)}, f32[18,8,512]{2,1,0:T(8,128)S(1)}, u32[]{:S(2)}, u32[]{:S(2)}) collective-permute-start(f32[18,8,512]{2,1,0:T(8,128)} %get-tuple-element.49), channel_id=1, source_target_pairs={{0,4},{4,8},{8,12},{12,14},{14,10},{10,6},{6,2},{2,0},{1,3},{5,1},... | collective-permute-start | bytes 884744 | tf_op jit(solution)/shard_map/ppermute | solution.py:613
  30.6 8.4 %collective-permute-start.3 = (f32[18,8,512]{2,1,0:T(8,128)}, f32[18,8,512]{2,1,0:T(8,128)S(1)}, u32[]{:S(2)}, u32[]{:S(2)}) collective-permute-start(f32[18,8,512]{2,1,0:T(8,128)} %get-tuple-element.50), channel_id=1, source_target_pairs={{0,4},{4,8},{8,12},{12,14},{14,10},{10,6},{6,2},{2,0},{1,3},{5,1},... | collective-permute-start | bytes 884744 | tf_op jit(solution)/shard_map/ppermute | solution.py:613
  39.1 6.8 %collective-permute-start.26 = (f32[18,8,512]{2,1,0:T(8,128)S(1)}, f32[18,8,512]{2,1,0:T(8,128)S(1)}, u32[]{:S(2)}, u32[]{:S(2)}) collective-permute-start(f32[18,8,512]{2,1,0:T(8,128)S(1)} %bitcast_add_fusion.19), channel_id=1, source_target_pairs={{0,4},{4,8},{8,12},{12,14},{14,10},{10,6},{6,2},{2,0},{1,3},{5,1},... | collective-permute-start | bytes 884744 | tf_op jit(solution)/shard_map/ppermute | solution.py:613
  40.9 8.1 %collective-permute-start.45 = (f32[18,8,512]{2,1,0:T(8,128)S(1)}, f32[18,8,512]{2,1,0:T(8,128)S(1)}, u32[]{:S(2)}, u32[]{:S(2)}) collective-permute-start(f32[18,8,512]{2,1,0:T(8,128)S(1)} %bitcast_add_fusion.12), channel_id=1, source_target_pairs={{0,4},{4,8},{8,12},{12,14},{14,10},{10,6},{6,2},{2,0},{1,3},{5,1},... | collective-permute-start | bytes 884744 | tf_op jit(solution)/shard_map/ppermute | solution.py:613
  42.5 9.8 %collective-permute-start.4 = (f32[19,8,512]{2,1,0:T(8,128)S(1)}, f32[19,8,512]{2,1,0:T(8,128)S(1)}, u32[]{:S(2)}, u32[]{:S(2)}) collective-permute-start(f32[19,8,512]{2,1,0:T(8,128)S(1)} %get-tuple-element.51.refs_0_), channel_id=1, source_target_pairs={{0,4},{4,8},{8,12},{12,14},{14,10},{10,6},{6,2},{2,0},{1,3},{5,1},... | collective-permute-start | bytes 933896 | tf_op jit(solution)/shard_map/ppermute | solution.py:613
  45.9 9.6 %collective-permute-start.27 = (f32[18,8,512]{2,1,0:T(8,128)S(1)}, f32[18,8,512]{2,1,0:T(8,128)S(1)}, u32[]{:S(2)}, u32[]{:S(2)}) collective-permute-start(f32[18,8,512]{2,1,0:T(8,128)S(1)} %bitcast_add_fusion.18), channel_id=1, source_target_pairs={{0,4},{4,8},{8,12},{12,14},{14,10},{10,6},{6,2},{2,0},{1,3},{5,1},... | collective-permute-start | bytes 884744 | tf_op jit(solution)/shard_map/ppermute | solution.py:613
  49.0 9.6 %collective-permute-start.46 = (f32[18,8,512]{2,1,0:T(8,128)S(1)}, f32[18,8,512]{2,1,0:T(8,128)S(1)}, u32[]{:S(2)}, u32[]{:S(2)}) collective-permute-start(f32[18,8,512]{2,1,0:T(8,128)S(1)} %bitcast_add_fusion.11), channel_id=1, source_target_pairs={{0,4},{4,8},{8,12},{12,14},{14,10},{10,6},{6,2},{2,0},{1,3},{5,1},... | collective-permute-start | bytes 884744 | tf_op jit(solution)/shard_map/ppermute | solution.py:613
  52.4 9.6 %collective-permute-start.5 = (f32[19,8,512]{2,1,0:T(8,128)S(1)}, f32[19,8,512]{2,1,0:T(8,128)S(1)}, u32[]{:S(2)}, u32[]{:S(2)}) collective-permute-start(f32[19,8,512]{2,1,0:T(8,128)S(1)} %bitcast_add_fusion.5), channel_id=1, source_target_pairs={{0,4},{4,8},{8,12},{12,14},{14,10},{10,6},{6,2},{2,0},{1,3},{5,1},... | collective-permute-start | bytes 933896 | tf_op jit(solution)/shard_map/ppermute | solution.py:613
  55.5 13.2 %collective-permute-start.28 = (f32[18,8,512]{2,1,0:T(8,128)S(1)}, f32[18,8,512]{2,1,0:T(8,128)S(1)}, u32[]{:S(2)}, u32[]{:S(2)}) collective-permute-start(f32[18,8,512]{2,1,0:T(8,128)S(1)} %bitcast_add_fusion.17), channel_id=1, source_target_pairs={{0,4},{4,8},{8,12},{12,14},{14,10},{10,6},{6,2},{2,0},{1,3},{5,1},... | collective-permute-start | bytes 884744 | tf_op jit(solution)/shard_map/ppermute | solution.py:613
  58.7 14.8 %collective-permute-start.47 = (f32[18,8,512]{2,1,0:T(8,128)S(1)}, f32[18,8,512]{2,1,0:T(8,128)S(1)}, u32[]{:S(2)}, u32[]{:S(2)}) collective-permute-start(f32[18,8,512]{2,1,0:T(8,128)S(1)} %bitcast_add_fusion.10), channel_id=1, source_target_pairs={{0,4},{4,8},{8,12},{12,14},{14,10},{10,6},{6,2},{2,0},{1,3},{5,1},... | collective-permute-start | bytes 884744 | tf_op jit(solution)/shard_map/ppermute | solution.py:613
  62.0 9.6 %collective-permute-start.6 = (f32[19,8,512]{2,1,0:T(8,128)S(1)}, f32[19,8,512]{2,1,0:T(8,128)S(1)}, u32[]{:S(2)}, u32[]{:S(2)}) collective-permute-start(f32[19,8,512]{2,1,0:T(8,128)S(1)} %bitcast_add_fusion.4), channel_id=1, source_target_pairs={{0,4},{4,8},{8,12},{12,14},{14,10},{10,6},{6,2},{2,0},{1,3},{5,1},... | collective-permute-start | bytes 933896 | tf_op jit(solution)/shard_map/ppermute | solution.py:613
  71.7 7.3 %collective-permute-start.7 = (f32[19,8,512]{2,1,0:T(8,128)S(1)}, f32[19,8,512]{2,1,0:T(8,128)S(1)}, u32[]{:S(2)}, u32[]{:S(2)}) collective-permute-start(f32[19,8,512]{2,1,0:T(8,128)S(1)} %bitcast_add_fusion.3), channel_id=1, source_target_pairs={{0,4},{4,8},{8,12},{12,14},{14,10},{10,6},{6,2},{2,0},{1,3},{5,1},... | collective-permute-start | bytes 933896 | tf_op jit(solution)/shard_map/ppermute | solution.py:613
  73.5 8.6 %collective-permute-start.48 = (f32[18,8,512]{2,1,0:T(8,128)S(1)}, f32[18,8,512]{2,1,0:T(8,128)S(1)}, u32[]{:S(2)}, u32[]{:S(2)}) collective-permute-start(f32[18,8,512]{2,1,0:T(8,128)S(1)} %bitcast_add_fusion.9), channel_id=1, source_target_pairs={{0,4},{4,8},{8,12},{12,14},{14,10},{10,6},{6,2},{2,0},{1,3},{5,1},... | collective-permute-start | bytes 884744 | tf_op jit(solution)/shard_map/ppermute | solution.py:613
  75.7 9.6 %collective-permute-start.30 = (f32[18,8,512]{2,1,0:T(8,128)S(1)}, f32[18,8,512]{2,1,0:T(8,128)S(1)}, u32[]{:S(2)}, u32[]{:S(2)}) collective-permute-start(f32[18,8,512]{2,1,0:T(8,128)S(1)} %bitcast_add_fusion.15), channel_id=1, source_target_pairs={{0,4},{4,8},{8,12},{12,14},{14,10},{10,6},{6,2},{2,0},{1,3},{5,1},... | collective-permute-start | bytes 884744 | tf_op jit(solution)/shard_map/ppermute | solution.py:613
  79.0 9.6 %collective-permute-start.8 = (f32[19,8,512]{2,1,0:T(8,128)S(1)}, f32[19,8,512]{2,1,0:T(8,128)S(1)}, u32[]{:S(2)}, u32[]{:S(2)}) collective-permute-start(f32[19,8,512]{2,1,0:T(8,128)S(1)} %bitcast_add_fusion.2), channel_id=1, source_target_pairs={{0,4},{4,8},{8,12},{12,14},{14,10},{10,6},{6,2},{2,0},{1,3},{5,1},... | collective-permute-start | bytes 933896 | tf_op jit(solution)/shard_map/ppermute | solution.py:613
  82.2 9.6 %collective-permute-start.49 = (f32[18,8,512]{2,1,0:T(8,128)S(1)}, f32[18,8,512]{2,1,0:T(8,128)S(1)}, u32[]{:S(2)}, u32[]{:S(2)}) collective-permute-start(f32[18,8,512]{2,1,0:T(8,128)S(1)} %bitcast_add_fusion.8), channel_id=1, source_target_pairs={{0,4},{4,8},{8,12},{12,14},{14,10},{10,6},{6,2},{2,0},{1,3},{5,1},... | collective-permute-start | bytes 884744 | tf_op jit(solution)/shard_map/ppermute | solution.py:613
  85.3 9.6 %collective-permute-start.31 = (f32[18,8,512]{2,1,0:T(8,128)S(1)}, f32[18,8,512]{2,1,0:T(8,128)S(1)}, u32[]{:S(2)}, u32[]{:S(2)}) collective-permute-start(f32[18,8,512]{2,1,0:T(8,128)S(1)} %bitcast_add_fusion.14), channel_id=1, source_target_pairs={{0,4},{4,8},{8,12},{12,14},{14,10},{10,6},{6,2},{2,0},{1,3},{5,1},... | collective-permute-start | bytes 884744 | tf_op jit(solution)/shard_map/ppermute | solution.py:613
  88.6 9.6 %collective-permute-start.9 = (f32[19,8,512]{2,1,0:T(8,128)S(1)}, f32[19,8,512]{2,1,0:T(8,128)S(1)}, u32[]{:S(2)}, u32[]{:S(2)}) collective-permute-start(f32[19,8,512]{2,1,0:T(8,128)S(1)} %bitcast_add_fusion.1), channel_id=1, source_target_pairs={{0,4},{4,8},{8,12},{12,14},{14,10},{10,6},{6,2},{2,0},{1,3},{5,1},... | collective-permute-start | bytes 933896 | tf_op jit(solution)/shard_map/ppermute | solution.py:613
  91.8 9.6 %collective-permute-start.50 = (f32[18,8,512]{2,1,0:T(8,128)S(1)}, f32[18,8,512]{2,1,0:T(8,128)S(1)}, u32[]{:S(2)}, u32[]{:S(2)}) collective-permute-start(f32[18,8,512]{2,1,0:T(8,128)S(1)} %bitcast_add_fusion.7), channel_id=1, source_target_pairs={{0,4},{4,8},{8,12},{12,14},{14,10},{10,6},{6,2},{2,0},{1,3},{5,1},... | collective-permute-start | bytes 884744 | tf_op jit(solution)/shard_map/ppermute | solution.py:613
  95.0 9.6 %collective-permute-start.32 = (f32[18,8,512]{2,1,0:T(8,128)S(1)}, f32[18,8,512]{2,1,0:T(8,128)S(1)}, u32[]{:S(2)}, u32[]{:S(2)}) collective-permute-start(f32[18,8,512]{2,1,0:T(8,128)S(1)} %bitcast_add_fusion.13), channel_id=1, source_target_pairs={{0,4},{4,8},{8,12},{12,14},{14,10},{10,6},{6,2},{2,0},{1,3},{5,1},... | collective-permute-start | bytes 884744 | tf_op jit(solution)/shard_map/ppermute | solution.py:613
  96.6 28.7 %collective-permute-start.36 = (f32[18,8,512]{2,1,0:T(8,128)S(1)}, f32[18,8,512]{2,1,0:T(8,128)S(1)}, u32[]{:S(2)}, u32[]{:S(2)}) collective-permute-start(f32[18,8,512]{2,1,0:T(8,128)S(1)} %bitcast_add_fusion.13), channel_id=1, source_target_pairs={{0,1},{1,0},{2,3},{3,2},{4,5},{5,4},{6,7},{7,6},{8,9},{9,8},{10,11... | collective-permute-start | bytes 884744 | tf_op jit(solution)/shard_map/ppermute | solution.py:590
  98.3 9.6 %collective-permute-start.10 = (f32[19,8,512]{2,1,0:T(8,128)S(1)}, f32[19,8,512]{2,1,0:T(8,128)S(1)}, u32[]{:S(2)}, u32[]{:S(2)}) collective-permute-start(f32[19,8,512]{2,1,0:T(8,128)S(1)} %bitcast_add_fusion), channel_id=1, source_target_pairs={{0,4},{4,8},{8,12},{12,14},{14,10},{10,6},{6,2},{2,0},{1,3},{5,1},... | collective-permute-start | bytes 933896 | tf_op jit(solution)/shard_map/ppermute | solution.py:613
  101.5 9.6 %collective-permute-start.52 = (f32[18,8,512]{2,1,0:T(8,128)S(1)}, f32[18,8,512]{2,1,0:T(8,128)S(1)}, u32[]{:S(2)}, u32[]{:S(2)}) collective-permute-start(f32[18,8,512]{2,1,0:T(8,128)S(1)} %bitcast_add_fusion.6), channel_id=1, source_target_pairs={{0,4},{4,8},{8,12},{12,14},{14,10},{10,6},{6,2},{2,0},{1,3},{5,1},... | collective-permute-start | bytes 884744 | tf_op jit(solution)/shard_map/ppermute | solution.py:613
  104.6 9.6 %collective-permute-start.33 = (f32[18,8,512]{2,1,0:T(8,128)S(1)}, f32[18,8,512]{2,1,0:T(8,128)S(1)}, u32[]{:S(2)}, u32[]{:S(2)}) collective-permute-start(f32[18,8,512]{2,1,0:T(8,128)S(1)} %broadcast_add_fusion.13), channel_id=1, source_target_pairs={{0,4},{4,8},{8,12},{12,14},{14,10},{10,6},{6,2},{2,0},{1,3},{5,1},... | collective-permute-start | bytes 884744 | tf_op jit(solution)/shard_map/ppermute | solution.py:613
  106.2 21.1 %collective-permute-start.37 = (f32[18,8,512]{2,1,0:T(8,128)S(1)}, f32[18,8,512]{2,1,0:T(8,128)S(1)}, u32[]{:S(2)}, u32[]{:S(2)}) collective-permute-start(f32[18,8,512]{2,1,0:T(8,128)S(1)} %broadcast_add_fusion.13), channel_id=1, source_target_pairs={{0,1},{1,0},{2,3},{3,2},{4,5},{5,4},{6,7},{7,6},{8,9},{9,8},{10,11... | collective-permute-start | bytes 884744 | tf_op jit(solution)/shard_map/ppermute | solution.py:590
  108.0 9.4 %collective-permute-start.11 = (f32[18,8,512]{2,1,0:T(8,128)S(1)}, f32[18,8,512]{2,1,0:T(8,128)S(1)}, u32[]{:S(2)}, u32[]{:S(2)}) collective-permute-start(f32[18,8,512]{2,1,0:T(8,128)S(1)} %slice_add_fusion), channel_id=1, source_target_pairs={{0,4},{4,8},{8,12},{12,14},{14,10},{10,6},{6,2},{2,0},{1,3},{5,1},... | collective-permute-start | bytes 884744 | tf_op jit(solution)/shard_map/ppermute | solution.py:613
  111.1 9.5 %collective-permute-start.54 = (f32[18,8,512]{2,1,0:T(8,128)S(1)}, f32[18,8,512]{2,1,0:T(8,128)S(1)}, u32[]{:S(2)}, u32[]{:S(2)}) collective-permute-start(f32[18,8,512]{2,1,0:T(8,128)S(1)} %broadcast_add_fusion.7), channel_id=1, source_target_pairs={{0,4},{4,8},{8,12},{12,14},{14,10},{10,6},{6,2},{2,0},{1,3},{5,1},... | collective-permute-start | bytes 884744 | tf_op jit(solution)/shard_map/ppermute | solution.py:613
  114.3 9.5 %collective-permute-start.34 = (f32[18,8,512]{2,1,0:T(8,128)S(1)}, f32[18,8,512]{2,1,0:T(8,128)S(1)}, u32[]{:S(2)}, u32[]{:S(2)}) collective-permute-start(f32[18,8,512]{2,1,0:T(8,128)S(1)} %broadcast_add_fusion.12), channel_id=1, source_target_pairs={{0,4},{4,8},{8,12},{12,14},{14,10},{10,6},{6,2},{2,0},{1,3},{5,1},... | collective-permute-start | bytes 884744 | tf_op jit(solution)/shard_map/ppermute | solution.py:613
  117.4 14.7 %collective-permute-start.38 = (f32[18,8,512]{2,1,0:T(8,128)S(1)}, f32[18,8,512]{2,1,0:T(8,128)S(1)}, u32[]{:S(2)}, u32[]{:S(2)}) collective-permute-start(f32[18,8,512]{2,1,0:T(8,128)S(1)} %broadcast_add_fusion.12), channel_id=1, source_target_pairs={{0,1},{1,0},{2,3},{3,2},{4,5},{5,4},{6,7},{7,6},{8,9},{9,8},{10,11... | collective-permute-start | bytes 884744 | tf_op jit(solution)/shard_map/ppermute | solution.py:590
  125.3 8.3 %collective-permute-start.35 = (f32[18,8,512]{2,1,0:T(8,128)S(1)}, f32[18,8,512]{2,1,0:T(8,128)S(1)}, u32[]{:S(2)}, u32[]{:S(2)}) collective-permute-start(f32[18,8,512]{2,1,0:T(8,128)S(1)} %broadcast_add_fusion.11), channel_id=1, source_target_pairs={{0,4},{4,8},{8,12},{12,14},{14,10},{10,6},{6,2},{2,0},{1,3},{5,1},... | collective-permute-start | bytes 884744 | tf_op jit(solution)/shard_map/ppermute | solution.py:613
  127.3 7.9 %collective-permute-start.39 = (f32[18,8,512]{2,1,0:T(8,128)S(1)}, f32[18,8,512]{2,1,0:T(8,128)S(1)}, u32[]{:S(2)}, u32[]{:S(2)}) collective-permute-start(f32[18,8,512]{2,1,0:T(8,128)S(1)} %broadcast_add_fusion.11), channel_id=1, source_target_pairs={{0,1},{1,0},{2,3},{3,2},{4,5},{5,4},{6,7},{7,6},{8,9},{9,8},{10,11... | collective-permute-start | bytes 884744 | tf_op jit(solution)/shard_map/ppermute | solution.py:590
  127.3 9.4 %collective-permute-start.14 = (f32[18,8,512]{2,1,0:T(8,128)S(1)}, f32[18,8,512]{2,1,0:T(8,128)S(1)}, u32[]{:S(2)}, u32[]{:S(2)}) collective-permute-start(f32[18,8,512]{2,1,0:T(8,128)S(1)} %slice_add_fusion), channel_id=1, source_target_pairs={{0,1},{1,0},{2,3},{3,2},{4,5},{5,4},{6,7},{7,6},{8,9},{9,8},{10,11... | collective-permute-start | bytes 884744 | tf_op jit(solution)/shard_map/ppermute | solution.py:590
  130.4 6.9 %collective-permute-start.13 = (f32[18,8,512]{2,1,0:T(8,128)S(1)}, f32[18,8,512]{2,1,0:T(8,128)S(1)}, u32[]{:S(2)}, u32[]{:S(2)}) collective-permute-start(f32[18,8,512]{2,1,0:T(8,128)S(1)} %broadcast_add_fusion.19), channel_id=1, source_target_pairs={{0,4},{4,8},{8,12},{12,14},{14,10},{10,6},{6,2},{2,0},{1,3},{5,1},... | collective-permute-start | bytes 884744 | tf_op jit(solution)/shard_map/ppermute | solution.py:613
  132.0 6.8 %collective-permute-start.15 = (f32[18,8,512]{2,1,0:T(8,128)S(1)}, f32[18,8,512]{2,1,0:T(8,128)S(1)}, u32[]{:S(2)}, u32[]{:S(2)}) collective-permute-start(f32[18,8,512]{2,1,0:T(8,128)S(1)} %broadcast_add_fusion.20), channel_id=1, source_target_pairs={{0,1},{1,0},{2,3},{3,2},{4,5},{5,4},{6,7},{7,6},{8,9},{9,8},{10,11... | collective-permute-start | bytes 884744 | tf_op jit(solution)/shard_map/ppermute | solution.py:590
  133.6 7.1 %collective-permute-start.58 = (f32[18,8,512]{2,1,0:T(8,128)S(1)}, f32[18,8,512]{2,1,0:T(8,128)S(1)}, u32[]{:S(2)}, u32[]{:S(2)}) collective-permute-start(f32[18,8,512]{2,1,0:T(8,128)S(1)} %broadcast_add_fusion.5), channel_id=1, source_target_pairs={{0,4},{4,8},{8,12},{12,14},{14,10},{10,6},{6,2},{2,0},{1,3},{5,1},... | collective-permute-start | bytes 884744 | tf_op jit(solution)/shard_map/ppermute | solution.py:613
  145.6 8.5 %collective-permute-start.43 = (f32[18,8,512]{2,1,0:T(8,128)S(1)}, f32[18,8,512]{2,1,0:T(8,128)S(1)}, u32[]{:S(2)}, u32[]{:S(2)}) collective-permute-start(f32[18,8,512]{2,1,0:T(8,128)S(1)} %broadcast_add_fusion.10), channel_id=1, source_target_pairs={{0,1},{1,0},{2,3},{3,2},{4,5},{5,4},{6,7},{7,6},{8,9},{9,8},{10,11... | collective-permute-start | bytes 884744 | tf_op jit(solution)/shard_map/ppermute | solution.py:590
  147.5 7.2 %collective-permute-start.44 = (f32[18,8,512]{2,1,0:T(8,128)S(1)}, f32[18,8,512]{2,1,0:T(8,128)S(1)}, u32[]{:S(2)}, u32[]{:S(2)}) collective-permute-start(f32[18,8,512]{2,1,0:T(8,128)S(1)} %broadcast_add_fusion.9), channel_id=1, source_target_pairs={{0,1},{1,0},{2,3},{3,2},{4,5},{5,4},{6,7},{7,6},{8,9},{9,8},{10,11... | collective-permute-start | bytes 884744 | tf_op jit(solution)/shard_map/ppermute | solution.py:590
  147.6 9.7 %collective-permute-start.18 = (f32[18,8,512]{2,1,0:T(8,128)S(1)}, f32[18,8,512]{2,1,0:T(8,128)S(1)}, u32[]{:S(2)}, u32[]{:S(2)}) collective-permute-start(f32[18,8,512]{2,1,0:T(8,128)S(1)} %broadcast_add_fusion.17), channel_id=1, source_target_pairs={{0,4},{4,8},{8,12},{12,14},{14,10},{10,6},{6,2},{2,0},{1,3},{5,1},... | collective-permute-start | bytes 884744 | tf_op jit(solution)/shard_map/ppermute | solution.py:613
  150.7 8.1 %collective-permute-start.41 = (f32[18,8,512]{2,1,0:T(8,128)S(1)}, f32[18,8,512]{2,1,0:T(8,128)S(1)}, u32[]{:S(2)}, u32[]{:S(2)}) collective-permute-start(f32[18,8,512]{2,1,0:T(8,128)S(1)} %broadcast_add_fusion.9), channel_id=1, source_target_pairs={{0,4},{4,8},{8,12},{12,14},{14,10},{10,6},{6,2},{2,0},{1,3},{5,1},... | collective-permute-start | bytes 884744 | tf_op jit(solution)/shard_map/ppermute | solution.py:613
  152.3 10.2 %collective-permute-start.21 = (f32[18,8,512]{2,1,0:T(8,128)S(1)}, f32[18,8,512]{2,1,0:T(8,128)S(1)}, u32[]{:S(2)}, u32[]{:S(2)}) collective-permute-start(f32[18,8,512]{2,1,0:T(8,128)S(1)} %broadcast_add_fusion.18), channel_id=1, source_target_pairs={{0,1},{1,0},{2,3},{3,2},{4,5},{5,4},{6,7},{7,6},{8,9},{9,8},{10,11... | collective-permute-start | bytes 884744 | tf_op jit(solution)/shard_map/ppermute | solution.py:590
  154.1 10.0 %collective-permute-start.22 = (f32[18,8,512]{2,1,0:T(8,128)S(1)}, f32[18,8,512]{2,1,0:T(8,128)S(1)}, u32[]{:S(2)}, u32[]{:S(2)}) collective-permute-start(f32[18,8,512]{2,1,0:T(8,128)S(1)} %broadcast_add_fusion.17), channel_id=1, source_target_pairs={{0,1},{1,0},{2,3},{3,2},{4,5},{5,4},{6,7},{7,6},{8,9},{9,8},{10,11... | collective-permute-start | bytes 884744 | tf_op jit(solution)/shard_map/ppermute | solution.py:590
  157.3 8.3 %collective-permute-start.19 = (f32[18,8,512]{2,1,0:T(8,128)S(1)}, f32[18,8,512]{2,1,0:T(8,128)S(1)}, u32[]{:S(2)}, u32[]{:S(2)}) collective-permute-start(f32[18,8,512]{2,1,0:T(8,128)S(1)} %broadcast_add_fusion.16), channel_id=1, source_target_pairs={{0,4},{4,8},{8,12},{12,14},{14,10},{10,6},{6,2},{2,0},{1,3},{5,1},... | collective-permute-start | bytes 884744 | tf_op jit(solution)/shard_map/ppermute | solution.py:613
  162.5 7.3 %collective-permute-start.60 = (f32[18,8,512]{2,1,0:T(8,128)S(1)}, f32[18,8,512]{2,1,0:T(8,128)S(1)}, u32[]{:S(2)}, u32[]{:S(2)}) collective-permute-start(f32[18,8,512]{2,1,0:T(8,128)S(1)} %broadcast_add_fusion.8), channel_id=1, source_target_pairs={{0,4},{4,8},{8,12},{12,14},{14,10},{10,6},{6,2},{2,0},{1,3},{5,1},... | collective-permute-start | bytes 884744 | tf_op jit(solution)/shard_map/ppermute | solution.py:613
  165.7 6.8 %collective-permute-start.24 = (f32[18,8,512]{2,1,0:T(8,128)S(1)}, f32[18,8,512]{2,1,0:T(8,128)S(1)}, u32[]{:S(2)}, u32[]{:S(2)}) collective-permute-start(f32[18,8,512]{2,1,0:T(8,128)S(1)} %broadcast_add_fusion.15), channel_id=1, source_target_pairs={{0,4},{4,8},{8,12},{12,14},{14,10},{10,6},{6,2},{2,0},{1,3},{5,1},... | collective-permute-start | bytes 884744 | tf_op jit(solution)/shard_map/ppermute | solution.py:613
  167.3 8.5 %collective-permute-start.42 = (f32[18,8,512]{2,1,0:T(8,128)S(1)}, f32[18,8,512]{2,1,0:T(8,128)S(1)}, u32[]{:S(2)}, u32[]{:S(2)}) collective-permute-start(f32[18,8,512]{2,1,0:T(8,128)S(1)} %broadcast_add_fusion.8), channel_id=1, source_target_pairs={{0,1},{1,0},{2,3},{3,2},{4,5},{5,4},{6,7},{7,6},{8,9},{9,8},{10,11... | collective-permute-start | bytes 884744 | tf_op jit(solution)/shard_map/ppermute | solution.py:590
  168.3 7.3 %collective-permute-start.66 = (f32[18,8,512]{2,1,0:T(8,128)S(1)}, f32[18,8,512]{2,1,0:T(8,128)S(1)}, u32[]{:S(2)}, u32[]{:S(2)}) collective-permute-start(f32[18,8,512]{2,1,0:T(8,128)S(1)} %broadcast_add_fusion.1), channel_id=1, source_target_pairs={{0,4},{4,8},{8,12},{12,14},{14,10},{10,6},{6,2},{2,0},{1,3},{5,1},... | collective-permute-start | bytes 884744 | tf_op jit(solution)/shard_map/ppermute | solution.py:613
  (27 other events, 178.5 us)

commit v3 on v2

--- a/solution.py
+++ b/solution.py
@@ -36,7 +36,7 @@
 
 def spread_block(block, cat_ref, i, count):
     edge, width = block.shape
-    here = pl.ds(pl.multiple_of((i + 1) * edge, edge), edge)
+    here = slice((i + 1) * edge, (i + 2) * edge)
     for at, shift in enumerate((count, 0, edge - count)):
         moved = block if shift == 0 else pltpu.roll(block, shift, 0)
         cat_ref[here, at * width : (at + 1) * width] = moved.astype(BF16)
@@ -114,15 +114,15 @@
     for load in loads[:2]:
         load.wait()
 
-    def gather(i, _):
+    def gather(i):
         for j in range(side):
             block3_ref[j * count : (j + 1) * count, :] = frames_ref[i, j].astype(F32)
         block = block3_ref[...]
-        field_ref[pl.ds(pl.multiple_of(i * edge, edge), edge), :] = block
+        field_ref[slice(i * edge, (i + 1) * edge), :] = block
         spread_block(block, cat3_ref, i, count)
-        return 0
-
-    lax.fori_loop(0, side, gather, 0, unroll=True)
+
+    for i in range(side):
+        gather(i)
     core = lax.axis_index("narrow")
     first = (lax.axis_index("wide") * lax.axis_size("narrow") + core) * count
 
@@ -132,10 +132,10 @@
     inner = slice(edge, edge + rows)
     stores = [
         pltpu.make_async_copy(
-            cat3_ref.at[inner, part(core, half3, 2 * half3)], field_mine_hbm, out_sems.at[0]
+            cat3_ref.at[inner, part(core, half3, 2 * half3)], field_mine_hbm, out_sems.at[0, 0]
         ),
         pltpu.make_async_copy(
-            field_ref.at[:, part(1 - core, half3)], send_hbm.at[:, c_out + half4 :], out_sems.at[1]
+            field_ref.at[:, part(1 - core, half3)], send_hbm.at[:, c_out + half4 :], out_sems.at[1, 0]
         ),
     ]
 
@@ -160,23 +160,23 @@
     convolve_into(acc_ref, cat3_ref, w3_ref, edge)
     bias3 = b3_ref[...].astype(F32)
 
-    def silu_rows(i, _):
-        here = pl.ds(pl.multiple_of(i * edge, edge), edge)
+    def silu_rows(i):
+        here = slice(i * edge, (i + 1) * edge)
         pre = acc_ref[here, :] + bias3
         sigma = jax.nn.sigmoid(pre)
         slope_ref[here, :] = silu_slope(pre, sigma)
         act = jnp.where(row < valid, pre * sigma, 0.0).astype(BF16).astype(F32)
         act_ref[here, :] = act
         spread_block(act, cat4_ref, i, count)
-        return 0
-
-    lax.fori_loop(0, side, silu_rows, 0, unroll=True)
+
+    for i in range(side):
+        silu_rows(i)
     stores += [
         pltpu.make_async_copy(
-            act_ref.at[:, part(1 - core, half4)], send_hbm.at[:, c_out : c_out + half4], out_sems.at[2]
+            act_ref.at[:, part(1 - core, half4)], send_hbm.at[:, c_out : c_out + half4], out_sems.at[2, 0]
         ),
-        pltpu.make_async_copy(cat4_ref.at[inner, part(core, half4, c_mid)], mine_hbm, out_sems.at[3]),
-        pltpu.make_async_copy(slope_ref, slope_hbm, out_sems.at[4]),
+        pltpu.make_async_copy(cat4_ref.at[inner, part(core, half4, c_mid)], mine_hbm, out_sems.at[3, 0]),
+        pltpu.make_async_copy(slope_ref, slope_hbm, out_sems.at[4, 0]),
     ]
     for store in stores:
         store.start()
@@ -185,8 +185,8 @@
     convolve_into(acc_ref, cat4_ref, w4_ref, edge)
     bias4 = b4_ref[...].astype(F32)
 
-    def last_rows(i, _):
-        here = pl.ds(pl.multiple_of(i * edge, edge), edge)
+    def last_rows(i):
+        here = slice(i * edge, (i + 1) * edge)
         for j in range(side):
             block_ref[j * count : (j + 1) * count, :] = cot_ref[i, j].astype(F32)
         pre = acc_ref[here, :] + bias4
@@ -194,21 +194,25 @@
         delta = (block_ref[...] * scale * silu_slope(pre, sigma)).astype(BF16)
         short_ref[here, :] = delta
         delta_ref[here, :] = delta.astype(F32)
-        pltpu.make_async_copy(delta_ref.at[here], send_hbm.at[here, 0:c_out], out_sems.at[5]).start()
         out = pre * sigma
         for j in range(side):
             out_ref[i, j] = out[j * count : (j + 1) * count, :].astype(BF16)
-        return 0
-
-    lax.fori_loop(0, side, last_rows, 0, unroll=True)
-    late = [
-        pltpu.make_async_copy(short_ref, delta_hbm, out_sems.at[6]),
-        pltpu.make_async_copy(out_ref, out_hbm, out_sems.at[7]),
-    ]
-    for store in late:
-        store.start()
-    stores.append(pltpu.make_async_copy(delta_ref, send_hbm.at[:, 0:c_out], out_sems.at[5]))
-    for store in stores + late:
+
+    parts = [side * at // 4 for at in range(5)]
+    for at in range(4):
+        for i in range(parts[at], parts[at + 1]):
+            last_rows(i)
+        steps = slice(parts[at], parts[at + 1])
+        here = slice(parts[at] * edge, parts[at + 1] * edge)
+        late = [
+            pltpu.make_async_copy(delta_ref.at[here], send_hbm.at[here, 0:c_out], out_sems.at[5, at]),
+            pltpu.make_async_copy(short_ref.at[here], delta_hbm.at[here], out_sems.at[6, at]),
+            pltpu.make_async_copy(out_ref.at[steps], out_hbm.at[steps], out_sems.at[7, at]),
+        ]
+        for store in late:
+            store.start()
+        stores += late
+    for store in stores:
         store.wait()
 
 
@@ -251,7 +255,7 @@
             pltpu.VMEM((edges, 3 * c_in), BF16),
             pltpu.VMEM((edges, 3 * c_mid), BF16),
             pltpu.SemaphoreType.DMA((7,)),
-            pltpu.SemaphoreType.DMA((8,)),
+            pltpu.SemaphoreType.DMA((8, 4)),
         ],
         HEAD_MIB,
         2 * rows * 9 * c_mid * (c_in + c_out),
@@ -263,12 +267,12 @@
     edge = count * STEP
     clear_edges(cat_ref, count)
 
-    def rows_of(i, _):
-        block = delta_ref[pl.ds(pl.multiple_of(i * edge, edge), edge), :]
-        spread_block(block.astype(F32), cat_ref, i, count)
-        return 0
-
-    return lambda: lax.fori_loop(0, side, rows_of, 0, unroll=True)
+    def spread():
+        for i in range(side):
+            block = delta_ref[i * edge : (i + 1) * edge, :]
+            spread_block(block.astype(F32), cat_ref, i, count)
+
+    return spread
 
 
 def back4_kernel(
@@ -293,41 +297,37 @@
     load_slope.wait()
     valid = lax.broadcasted_iota(jnp.int32, (edge, 1), 0) < side * count
 
-    def rows_of(i, carry):
-        here = pl.ds(pl.multiple_of(i * edge, edge), edge)
+    def rows_of(i):
+        here = slice(i * edge, (i + 1) * edge)
         delta = jnp.where(valid, acc_ref[here, :] * slope_ref[here, :], 0.0).astype(BF16)
         short_ref[here, :] = delta
         long = delta.astype(F32)
         out_ref[here, :] = long
-        sum3, sum4 = carry
         return (
-            sum3 + jnp.sum(long, 0, keepdims=True),
-            sum4 + jnp.sum(delta_ref[here, :].astype(F32), 0, keepdims=True),
+            jnp.sum(long, 0, keepdims=True),
+            jnp.sum(delta_ref[here, :].astype(F32), 0, keepdims=True),
         )
 
-    def store(i):
-        here = pl.ds(pl.multiple_of(i * edge, edge), edge)
-        return pltpu.make_async_copy(out_ref.at[here], out_hbm.at[here], sems.at[5])
-
-    def stored_rows(i, carry):
-        carry = rows_of(i, carry)
-        store(i).start()
-        return carry
-
-    nothing = (jnp.zeros((1, out_ref.shape[1]), F32), jnp.zeros((1, delta_ref.shape[1]), F32))
-    sum3, sum4 = rows_of(side - 1, lax.fori_loop(0, side - 1, stored_rows, nothing, unroll=True))
-    sums_ref[0:1, :], sums_ref[1:2, :] = sum3, sum4
-    spare = (side - 1) * edge + (side + 1) * count
-    out_ref[spare : spare + 2, :] = sums_ref[...]
-    store(side - 1).start()
-    late = [
-        pltpu.make_async_copy(short_ref, short_hbm, sems.at[6]),
-        pltpu.make_async_copy(sums_ref, sums_hbm, sems.at[7]),
-    ]
-    for copy in late:
-        copy.start()
-    for copy in late + [pltpu.make_async_copy(out_ref, out_hbm, sems.at[5])]:
-        copy.wait()
+    sum3, sum4 = rows_of(0)
+    stores = []
+    parts = [side * at // 4 for at in range(5)]
+    for at in range(4):
+        for i in range(max(parts[at], 1), parts[at + 1]):
+            more3, more4 = rows_of(i)
+            sum3, sum4 = sum3 + more3, sum4 + more4
+        if at == 3:
+            sums_ref[0:1, :], sums_ref[1:2, :] = sum3, sum4
+            spare = (side - 1) * edge + (side + 1) * count
+            out_ref[spare : spare + 2, :] = sums_ref[...]
+        here = slice(parts[at] * edge, parts[at + 1] * edge)
+        stores.append(pltpu.make_async_copy(out_ref.at[here], out_hbm.at[here], sems.at[5 + at]))
+        stores.append(pltpu.make_async_copy(short_ref.at[here], short_hbm.at[here], sems.at[9 + at]))
+        for store in stores[-2:]:
+            store.start()
+    stores.append(pltpu.make_async_copy(sums_ref, sums_hbm, sems.at[13]))
+    stores[-1].start()
+    for store in stores:
+        store.wait()
 
 
 def back4(count, delta, slope, w):
@@ -349,7 +349,7 @@
             pltpu.VMEM((rows, c_mid), F32),
             pltpu.VMEM((rows, c_mid), BF16),
             pltpu.VMEM((2, width), F32),
-            pltpu.SemaphoreType.DMA((8,)),
+            pltpu.SemaphoreType.DMA((14,)),
         ],
         BACK4_MIB,
         2 * rows * c_mid * width * taps,
@@ -372,13 +372,10 @@
     spread()
     back_into(acc_ref, cat_ref, w_ref, edge, load_w)
 
-    def rows_of(i, _):
-        block = acc_ref[pl.ds(pl.multiple_of(i * edge, edge), edge), :]
+    for i in range(side):
+        block = acc_ref[i * edge : (i + 1) * edge, :]
         for j in range(side):
             out_ref[i, j] = block[j * count : (j + 1) * count, :].astype(BF16)
-        return 0
-
-    lax.fori_loop(0, side, rows_of, 0, unroll=True)
     store = pltpu.make_async_copy(out_ref, out_hbm, sems.at[4])
     store.start()
     store.wait()
@@ -437,20 +434,20 @@
     turned_ref[:, 0:wide] = jnp.zeros((3 * k, wide), BF16)
     turned_ref[:, (side + 1) * wide :] = jnp.zeros((3 * k, wide), BF16)
 
-    def turn(i, carry):
-        here = pl.ds(pl.multiple_of(i * edge, edge), edge)
-        there = pl.ds(pl.multiple_of((i + 1) * wide, wide), wide)
+    def turn(i):
+        here = slice(i * edge, (i + 1) * edge)
+        there = slice((i + 1) * wide, (i + 2) * wide)
         turned = jnp.concatenate([mine_ref[here, :].astype(F32), theirs_ref[here, :]], 0).T
         for c, shift in enumerate((count, 0, wide - count)):
             moved = turned if shift == 0 else pltpu.roll(turned, shift, 1)
             turned_ref[c * k : (c + 1) * k, there] = moved.astype(BF16)
         both_ref[i, edge:wide, :] = other_ref[here, :].astype(BF16)
-        return carry
 
     for group in range(3):
         for load in loads[group]:
             load.wait()
-        lax.fori_loop(groups[group], groups[group + 1], turn, 0, unroll=True)
+        for i in range(groups[group], groups[group + 1]):
+            turn(i)
     blocks = 3 * k // (8 * lanes * chunks)
     if tail:
         for load in extra:
@@ -595,7 +592,7 @@
 
 
 class Ring:
-    def __init__(self, size, zero):
+    def __init__(self, size):
         self.size = size
         order = list(range(0, size, 2)) + list(range(size - 1, 0, -2))
         self.pairs = []
@@ -607,7 +604,6 @@
         half = wide // 2
         self.place = jnp.where(wide % 2 == 0, half, size - 1 - half)
         self.way = 1 - 2 * self.core
-        self.zero = zero
 
     def send(self, value):
         return lax.ppermute(value, ("wide", "narrow"), self.pairs)
@@ -649,7 +645,7 @@
             else:
                 self.held = got[: self.blocks] + self.parts[number, : self.blocks]
         else:
-            self.held = got + self.ring.zero
+            self.held = got
             self.keep(number - last + 1)
 
 
@@ -672,7 +668,7 @@
     c_mid, c_out = w_three.shape[1], w_four.shape[1]
     taps3, taps4 = w_three.reshape(9, c_in, c_mid), w_four.reshape(9, c_mid, c_out)
     size = lax.axis_size("wide")
-    ring = Ring(size, jnp.minimum(clip_counts[0], 0).astype(F32))
+    ring = Ring(size)
     core = ring.core
     total_frames = count * size * lax.axis_size("narrow")
     def cells_first(field):
@@ -722,16 +718,20 @@
         shape3, shape4 = (9, c_in, c_mid), (9, c_mid, c_out)
         last = 2 * (size - 1) - 1
         for number in range(last + 1):
-            if number in (last - 4, last - 1):
+            if number == last - 4:
                 (grad_w3,) = lay_lanes([(z, 0)], [grad_w3], [shape3])
-            if number in (last - 3, last):
-                z.held = after(z.held, grad_w3)
-            if number in (last - 3, last - 1):
+            if number == last - 3:
+                y.held = after(y.held, grad_w3)
                 (grad_w4,) = lay_lanes([(y, 0)], [grad_w4], [shape4])
-            if number in (last - 2, last):
-                y.held = after(y.held, grad_w4)
+            if number == last - 2:
+                x.held = after(x.held, grad_w4)
                 (grad_w4,) = lay_lanes([(x, 0)], [grad_w4], [shape4])
-            if number in (last - 1, last):
+            if number == last - 1:
+                z.held = after(z.held, grad_w4)
+                (grad_w3,) = lay_lanes([(z, 0)], [grad_w3], [shape3])
+                (grad_w4,) = lay_lanes([(y, 0)], [grad_w4], [shape4])
+            if number == last:
+                y.held = after(y.held, grad_w3)
                 x.held = after(x.held, grad_w4)
             z.step(number)
             if number > 0:
@@ -741,9 +741,9 @@
                 sum3, sum4 = tally(z.passed)
             if number == size:
                 x.held = after(x.held, sum3)
-            if number == 1:
+            if number == 3:
                 field_grad = back3(side, count, after(delta3, z.held), taps3)
-            if number == 3:
+            if number == 5:
                 z.held = after(z.held, field_grad)
         grad_w3, grad_w4 = lay_lanes([(z, 0), (y, 1)], [grad_w3, grad_w4], [shape3, shape4])
         (grad_w4,) = lay_lanes([(x, 0)], [grad_w4], [shape4])

time: 179 us -> 176 us (0.983)
    pallas_call x14 -> x13, Pallas kernels: 47.8 us -> 47.1 us  [kernel_call(): pl.pallas_call(kernel, out_shape=outs, in_specs=[HBM] * len(args), out_sp...]
  transfers between devices with their start and end apart: 68 -> 68, of which waited for: 33 -> 34; matrix products, arithmetic and copies ran while one was open for 1% -> 1% of each run, Pallas kernels for 20% -> 20%
where the time goes in v3:
time: 176 us; the launch traced here: 175 us
  starting transfers between devices  74.4 us (42%)
  waiting for transfers between devices  50.5 us (29%)
  Pallas kernels  47.1 us (27%)
    ppermute x42, starting transfers between devices, send(): return lax.ppermute(value, ('wide', 'narrow'), self.pairs)  70.9 us
    ppermute x42, waiting for transfers between devices, send(): return lax.ppermute(value, ('wide', 'narrow'), self.pairs)  50.4 us
    pallas_call x13, Pallas kernels, kernel_call(): pl.pallas_call(kernel, out_shape=outs, in_specs=[HBM] * len(args), out_sp...  47.1 us
    ppermute x26, starting transfers between devices, swap_cores(): return lax.ppermute(value, 'narrow', [(0, 1), (1, 0)])  3.55 us
  transfers between devices with their start and end apart: 68, of which 34 were waited for; matrix products, arithmetic and copies ran while one was open for 1% of the time, Pallas kernels for 20%

profile of v3, /device:TPU:0, one launch (start us, length us, event | category | flops | bytes accessed | tf_op | source)
XLA Modules:
  0.0 175.4 jit_solution(5116894893705568369)
XLA Ops:
  0.6 10.6 %shard_map.118 = (bf16[13,13,4,512]{3,2,1,0:T(4,128)(2,1)}, bf16[832,256]{1,0:T(8,128)(2,1)}, f32[832,512]{1,0:T(8,128)}, bf16[832,512]{1,0:T(8,128)(2,1)}, bf16...) custom-call(s32[8]{0:T(128)} %counts_hbm.1, bf16[13,13,4,256]{3,2,1,0:T(4,128)(2,1)} %bitcast.166, bf16[2304,512]{1,0:T(8,128)(2,1)} %bitcast.158, ...), custom_call_target="tpu_custom_call" | custom-call | flops 5888802816 | bytes 8388608 | tf_op jit(solution)/shard_map/pallas_call | solution.py:25
  11.7 7.7 %shard_map.119 = (f32[832,512]{1,0:T(8,128)}, bf16[832,512]{1,0:T(8,128)(2,1)}, f32[2,512]{1,0:T(2,128)}) custom-call(bf16[832,512]{1,0:T(8,128)(2,1)} %get-tuple-element.38.delta_hbm, f32[832,512]{1,0:T(8,128)} %get-tuple-element.39.slope_hbm, bf16[9,512,512]{2,1,0:T(8,128)(2,1)} %bitcast.164), custom_call_target="tpu_custom_call" | custom-call | flops 3925868544 | bytes 8388608 | tf_op jit(solution)/shard_map/pallas_call | solution.py:25
  19.5 8.1 %shard_map.121 = (f32[18,8,512]{2,1,0:T(8,128)}, f32[7,18,8,512]{3,2,1,0:T(8,128)}, f32[18,8,512]{2,1,0:T(8,128)}, f32[7,18,8,512]{3,2,1,0:T(8,128)}) custom-call(bf16[832,256]{1,0:T(8,128)(2,1)} %get-tuple-element.47.refs_0_, f32[832,896]{1,0:T(8,128)} %collective-permute-done.refs_1_.refs_3_, bf16[13,64,512]{2,1,0:T(8,128)(2,1)} %bitcast.167, ...), custom_call_target="tpu_custom_call" | custom-call | flops 3925868544 | bytes 8388608 | tf_op jit(solution)/shard_map/pallas_call | solution.py:25
  27.6 3.1 %collective-permute-start.2 = (f32[18,8,512]{2,1,0:T(8,128)}, f32[18,8,512]{2,1,0:T(8,128)S(1)}, u32[]{:S(2)}, u32[]{:S(2)}) collective-permute-start(f32[18,8,512]{2,1,0:T(8,128)} %get-tuple-element.48), channel_id=1, source_target_pairs={{0,4},{4,8},{8,12},{12,14},{14,10},{10,6},{6,2},{2,0},{1,3},{5,1},... | collective-permute-start | bytes 884744 | tf_op jit(solution)/shard_map/ppermute | solution.py:609
  33.4 5.6 %shard_map.120 = (f32[19,8,512]{2,1,0:T(8,128)S(1)}, f32[7,19,8,512]{3,2,1,0:T(8,128)S(1)}) custom-call(bf16[832,128]{1,0:T(8,128)(2,1)S(1)} %copy-done.2, f32[832,896]{1,0:T(8,128)} %collective-permute-done.refs_1_.refs_3_, bf16[13,64,512]{2,1,0:T(8,128)(2,1)S(1)} %bitcast.160, f32[832,512]{1,0:T(8,128)S(1)} %collective-permute-done.1.refs_3_, ...), custom_call_target="tpu_custom_call" | custom-call | flops 1962934272 | bytes 8388608 | tf_op jit(solution)/shard_map/pallas_call | solution.py:25
  39.1 1.8 %collective-permute-start.16 = (f32[18,8,512]{2,1,0:T(8,128)S(1)}, f32[18,8,512]{2,1,0:T(8,128)S(1)}, u32[]{:S(2)}, u32[]{:S(2)}) collective-permute-start(f32[18,8,512]{2,1,0:T(8,128)S(1)} %bitcast_add_fusion.19), channel_id=1, source_target_pairs={{0,4},{4,8},{8,12},{12,14},{14,10},{10,6},{6,2},{2,0},{1,3},{5,1},... | collective-permute-start | bytes 884744 | tf_op jit(solution)/shard_map/ppermute | solution.py:609
  42.5 1.6 collective-permute-start.31
  44.1 1.7 collective-permute-done.16
  45.9 1.8 %collective-permute-start.17 = (f32[18,8,512]{2,1,0:T(8,128)S(1)}, f32[18,8,512]{2,1,0:T(8,128)S(1)}, u32[]{:S(2)}, u32[]{:S(2)}) collective-permute-start(f32[18,8,512]{2,1,0:T(8,128)S(1)} %bitcast_add_fusion.18), channel_id=1, source_target_pairs={{0,4},{4,8},{8,12},{12,14},{14,10},{10,6},{6,2},{2,0},{1,3},{5,1},... | collective-permute-start | bytes 884744 | tf_op jit(solution)/shard_map/ppermute | solution.py:609
  49.3 1.8 %collective-permute-start.5 = (f32[19,8,512]{2,1,0:T(8,128)S(1)}, f32[19,8,512]{2,1,0:T(8,128)S(1)}, u32[]{:S(2)}, u32[]{:S(2)}) collective-permute-start(f32[19,8,512]{2,1,0:T(8,128)S(1)} %bitcast_add_fusion.5), channel_id=1, source_target_pairs={{0,4},{4,8},{8,12},{12,14},{14,10},{10,6},{6,2},{2,0},{1,3},{5,1},... | collective-permute-start | bytes 933896 | tf_op jit(solution)/shard_map/ppermute | solution.py:609
  52.4 1.8 %collective-permute-start.32 = (f32[18,8,512]{2,1,0:T(8,128)S(1)}, f32[18,8,512]{2,1,0:T(8,128)S(1)}, u32[]{:S(2)}, u32[]{:S(2)}) collective-permute-start(f32[18,8,512]{2,1,0:T(8,128)S(1)} %bitcast_add_fusion.11), channel_id=1, source_target_pairs={{0,4},{4,8},{8,12},{12,14},{14,10},{10,6},{6,2},{2,0},{1,3},{5,1},... | collective-permute-start | bytes 884744 | tf_op jit(solution)/shard_map/ppermute | solution.py:609
  55.6 1.8 %collective-permute-start.18 = (f32[18,8,512]{2,1,0:T(8,128)S(1)}, f32[18,8,512]{2,1,0:T(8,128)S(1)}, u32[]{:S(2)}, u32[]{:S(2)}) collective-permute-start(f32[18,8,512]{2,1,0:T(8,128)S(1)} %bitcast_add_fusion.17), channel_id=1, source_target_pairs={{0,4},{4,8},{8,12},{12,14},{14,10},{10,6},{6,2},{2,0},{1,3},{5,1},... | collective-permute-start | bytes 884744 | tf_op jit(solution)/shard_map/ppermute | solution.py:609
  58.9 1.8 %collective-permute-start.6 = (f32[19,8,512]{2,1,0:T(8,128)S(1)}, f32[19,8,512]{2,1,0:T(8,128)S(1)}, u32[]{:S(2)}, u32[]{:S(2)}) collective-permute-start(f32[19,8,512]{2,1,0:T(8,128)S(1)} %bitcast_add_fusion.4), channel_id=1, source_target_pairs={{0,4},{4,8},{8,12},{12,14},{14,10},{10,6},{6,2},{2,0},{1,3},{5,1},... | collective-permute-start | bytes 933896 | tf_op jit(solution)/shard_map/ppermute | solution.py:609
  62.1 1.8 %collective-permute-start.33 = (f32[18,8,512]{2,1,0:T(8,128)S(1)}, f32[18,8,512]{2,1,0:T(8,128)S(1)}, u32[]{:S(2)}, u32[]{:S(2)}) collective-permute-start(f32[18,8,512]{2,1,0:T(8,128)S(1)} %bitcast_add_fusion.10), channel_id=1, source_target_pairs={{0,4},{4,8},{8,12},{12,14},{14,10},{10,6},{6,2},{2,0},{1,3},{5,1},... | collective-permute-start | bytes 884744 | tf_op jit(solution)/shard_map/ppermute | solution.py:609
  65.2 1.8 %collective-permute-start.19 = (f32[18,8,512]{2,1,0:T(8,128)S(1)}, f32[18,8,512]{2,1,0:T(8,128)S(1)}, u32[]{:S(2)}, u32[]{:S(2)}) collective-permute-start(f32[18,8,512]{2,1,0:T(8,128)S(1)} %bitcast_add_fusion.16), channel_id=1, source_target_pairs={{0,4},{4,8},{8,12},{12,14},{14,10},{10,6},{6,2},{2,0},{1,3},{5,1},... | collective-permute-start | bytes 884744 | tf_op jit(solution)/shard_map/ppermute | solution.py:609
  68.6 1.8 %collective-permute-start.7 = (f32[19,8,512]{2,1,0:T(8,128)S(1)}, f32[19,8,512]{2,1,0:T(8,128)S(1)}, u32[]{:S(2)}, u32[]{:S(2)}) collective-permute-start(f32[19,8,512]{2,1,0:T(8,128)S(1)} %bitcast_add_fusion.3), channel_id=1, source_target_pairs={{0,4},{4,8},{8,12},{12,14},{14,10},{10,6},{6,2},{2,0},{1,3},{5,1},... | collective-permute-start | bytes 933896 | tf_op jit(solution)/shard_map/ppermute | solution.py:609
  71.7 1.8 %collective-permute-start.34 = (f32[18,8,512]{2,1,0:T(8,128)S(1)}, f32[18,8,512]{2,1,0:T(8,128)S(1)}, u32[]{:S(2)}, u32[]{:S(2)}) collective-permute-start(f32[18,8,512]{2,1,0:T(8,128)S(1)} %bitcast_add_fusion.9), channel_id=1, source_target_pairs={{0,4},{4,8},{8,12},{12,14},{14,10},{10,6},{6,2},{2,0},{1,3},{5,1},... | collective-permute-start | bytes 884744 | tf_op jit(solution)/shard_map/ppermute | solution.py:609
  74.9 1.8 %collective-permute-start.20 = (f32[18,8,512]{2,1,0:T(8,128)S(1)}, f32[18,8,512]{2,1,0:T(8,128)S(1)}, u32[]{:S(2)}, u32[]{:S(2)}) collective-permute-start(f32[18,8,512]{2,1,0:T(8,128)S(1)} %bitcast_add_fusion.15), channel_id=1, source_target_pairs={{0,4},{4,8},{8,12},{12,14},{14,10},{10,6},{6,2},{2,0},{1,3},{5,1},... | collective-permute-start | bytes 884744 | tf_op jit(solution)/shard_map/ppermute | solution.py:609
  78.2 1.8 %collective-permute-start.8 = (f32[19,8,512]{2,1,0:T(8,128)S(1)}, f32[19,8,512]{2,1,0:T(8,128)S(1)}, u32[]{:S(2)}, u32[]{:S(2)}) collective-permute-start(f32[19,8,512]{2,1,0:T(8,128)S(1)} %bitcast_add_fusion.2), channel_id=1, source_target_pairs={{0,4},{4,8},{8,12},{12,14},{14,10},{10,6},{6,2},{2,0},{1,3},{5,1},... | collective-permute-start | bytes 933896 | tf_op jit(solution)/shard_map/ppermute | solution.py:609
  81.4 1.8 %collective-permute-start.35 = (f32[18,8,512]{2,1,0:T(8,128)S(1)}, f32[18,8,512]{2,1,0:T(8,128)S(1)}, u32[]{:S(2)}, u32[]{:S(2)}) collective-permute-start(f32[18,8,512]{2,1,0:T(8,128)S(1)} %bitcast_add_fusion.8), channel_id=1, source_target_pairs={{0,4},{4,8},{8,12},{12,14},{14,10},{10,6},{6,2},{2,0},{1,3},{5,1},... | collective-permute-start | bytes 884744 | tf_op jit(solution)/shard_map/ppermute | solution.py:609
  83.2 5.0 %shard_map.122 = bf16[13,13,4,256]{3,2,1,0:T(4,128)(2,1)} custom-call(bf16[832,512]{1,0:T(8,128)(2,1)S(1)} %copy-done.1, bf16[9,256,512]{2,1,0:T(8,128)(2,1)S(1)} %bitcast.159), custom_call_target="tpu_custom_call" | custom-call | flops 1962934272 | bytes 8388608 | tf_op jit(solution)/shard_map/pallas_call | solution.py:25
  88.2 1.6 collective-permute-start.9
  89.9 1.6 collective-permute-start.21
  93.1 2.0 %collective-permute-done.9.refs_6_ = f32[19,8,512]{2,1,0:T(8,128)S(1)} collective-permute-done((f32[19,8,512]{2,1,0:T(8,128)S(1)}, f32[19,8,512]{2,1,0:T(8,128)S(1)}, u32[]{:S(2)}, u32[]{:S(2)}) %collective-permute-start.9) | collective-permute-done | bytes 311328 | tf_op jit(solution)/shard_map/ppermute | solution.py:609
  95.2 1.6 collective-permute-start.10
  98.4 1.6 collective-permute-start.23
  101.6 1.6 collective-permute-start.38
  104.9 1.6 collective-permute-start.11
  108.0 1.6 collective-permute-start.25
  111.1 1.6 collective-permute-start.40
  114.3 1.6 collective-permute-start.12
  115.9 1.6 collective-permute-done.25
  118.3 1.6 collective-permute-start.27
  120.6 1.6 collective-permute-start.42
  123.8 1.6 collective-permute-start.13
  126.9 3.2 %collective-permute-done.42 = f32[18,8,512]{2,1,0:T(8,128)S(1)} collective-permute-done((f32[18,8,512]{2,1,0:T(8,128)S(1)}, f32[18,8,512]{2,1,0:T(8,128)S(1)}, u32[]{:S(2)}, u32[]{:S(2)}) %collective-permute-start.42) | collective-permute-done | bytes 294944 | tf_op jit(solution)/shard_map/ppermute | solution.py:609
  130.1 1.6 collective-permute-start.29
  133.3 1.6 collective-permute-start.14
  136.1 1.6 collective-permute-start.51
  138.3 1.7 collective-permute-done.14
  140.0 1.6 collective-permute-start.15
  143.1 1.6 collective-permute-start.52
  146.9 1.7 shard_map.125.refs_4_
  149.9 1.6 collective-permute-start.53
  151.4 1.6 collective-permute-done.62
  153.0 1.6 collective-permute-start.44
  164.5 4.7 %collective-permute-done.46 = f32[18,8,512]{2,1,0:T(8,128)S(1)} collective-permute-done((f32[18,8,512]{2,1,0:T(8,128)S(1)}, f32[18,8,512]{2,1,0:T(8,128)S(1)}, u32[]{:S(2)}, u32[]{:S(2)}) %collective-permute-start.46) | collective-permute-done | bytes 294944 | tf_op jit(solution)/shard_map/ppermute | solution.py:609
  170.3 2.1 %collective-permute-done.66 = f32[18,8,512]{2,1,0:T(8,128)S(1)} collective-permute-done((f32[18,8,512]{2,1,0:T(8,128)S(1)}, f32[18,8,512]{2,1,0:T(8,128)S(1)}, u32[]{:S(2)}, u32[]{:S(2)}) %collective-permute-start.66) | collective-permute-done | bytes 294944 | tf_op jit(solution)/shard_map/ppermute | solution.py:609
  (134 shorter events, 58.9 us)
Async XLA Ops:
  11.2 8.3 %collective-permute-start = (f32[832,896]{1,0:T(8,128)}, f32[832,896]{1,0:T(8,128)}, u32[]{:S(2)}, u32[]{:S(2)}) collective-permute-start(f32[832,896]{1,0:T(8,128)} %get-tuple-element.42), channel_id=1, source_target_pairs={{0,1},{1,0},{2,3},{3,2},{4,5},{5,4},{6,7},{7,6},{8,9},{9,8},{10,11... | collective-permute-start | bytes 8945672 | tf_op jit(solution)/shard_map/ppermute | solution.py:587
  19.4 12.9 %collective-permute-start.1 = (f32[832,512]{1,0:T(8,128)}, f32[832,512]{1,0:T(8,128)S(1)}, u32[]{:S(2)}, u32[]{:S(2)}) collective-permute-start(f32[832,512]{1,0:T(8,128)} %get-tuple-element.43), channel_id=1, source_target_pairs={{0,1},{1,0},{2,3},{3,2},{4,5},{5,4},{6,7},{7,6},{8,9},{9,8},{10,11... | collective-permute-start | bytes 5111816 | tf_op jit(solution)/shard_map/ppermute | solution.py:587
  27.6 11.4 %collective-permute-start.2 = (f32[18,8,512]{2,1,0:T(8,128)}, f32[18,8,512]{2,1,0:T(8,128)S(1)}, u32[]{:S(2)}, u32[]{:S(2)}) collective-permute-start(f32[18,8,512]{2,1,0:T(8,128)} %get-tuple-element.48), channel_id=1, source_target_pairs={{0,4},{4,8},{8,12},{12,14},{14,10},{10,6},{6,2},{2,0},{1,3},{5,1},... | collective-permute-start | bytes 884744 | tf_op jit(solution)/shard_map/ppermute | solution.py:609
  30.7 8.3 %collective-permute-start.3 = (f32[18,8,512]{2,1,0:T(8,128)}, f32[18,8,512]{2,1,0:T(8,128)S(1)}, u32[]{:S(2)}, u32[]{:S(2)}) collective-permute-start(f32[18,8,512]{2,1,0:T(8,128)} %get-tuple-element.49), channel_id=1, source_target_pairs={{0,4},{4,8},{8,12},{12,14},{14,10},{10,6},{6,2},{2,0},{1,3},{5,1},... | collective-permute-start | bytes 884744 | tf_op jit(solution)/shard_map/ppermute | solution.py:609
  40.9 8.3 %collective-permute-start.4 = (f32[19,8,512]{2,1,0:T(8,128)S(1)}, f32[19,8,512]{2,1,0:T(8,128)S(1)}, u32[]{:S(2)}, u32[]{:S(2)}) collective-permute-start(f32[19,8,512]{2,1,0:T(8,128)S(1)} %get-tuple-element.50.refs_0_), channel_id=1, source_target_pairs={{0,4},{4,8},{8,12},{12,14},{14,10},{10,6},{6,2},{2,0},{1,3},{5,1},... | collective-permute-start | bytes 933896 | tf_op jit(solution)/shard_map/ppermute | solution.py:609
  42.5 9.9 %collective-permute-start.31 = (f32[18,8,512]{2,1,0:T(8,128)S(1)}, f32[18,8,512]{2,1,0:T(8,128)S(1)}, u32[]{:S(2)}, u32[]{:S(2)}) collective-permute-start(f32[18,8,512]{2,1,0:T(8,128)S(1)} %bitcast_add_fusion.12), channel_id=1, source_target_pairs={{0,4},{4,8},{8,12},{12,14},{14,10},{10,6},{6,2},{2,0},{1,3},{5,1},... | collective-permute-start | bytes 884744 | tf_op jit(solution)/shard_map/ppermute | solution.py:609
  45.9 9.6 %collective-permute-start.17 = (f32[18,8,512]{2,1,0:T(8,128)S(1)}, f32[18,8,512]{2,1,0:T(8,128)S(1)}, u32[]{:S(2)}, u32[]{:S(2)}) collective-permute-start(f32[18,8,512]{2,1,0:T(8,128)S(1)} %bitcast_add_fusion.18), channel_id=1, source_target_pairs={{0,4},{4,8},{8,12},{12,14},{14,10},{10,6},{6,2},{2,0},{1,3},{5,1},... | collective-permute-start | bytes 884744 | tf_op jit(solution)/shard_map/ppermute | solution.py:609
  49.3 9.6 %collective-permute-start.5 = (f32[19,8,512]{2,1,0:T(8,128)S(1)}, f32[19,8,512]{2,1,0:T(8,128)S(1)}, u32[]{:S(2)}, u32[]{:S(2)}) collective-permute-start(f32[19,8,512]{2,1,0:T(8,128)S(1)} %bitcast_add_fusion.5), channel_id=1, source_target_pairs={{0,4},{4,8},{8,12},{12,14},{14,10},{10,6},{6,2},{2,0},{1,3},{5,1},... | collective-permute-start | bytes 933896 | tf_op jit(solution)/shard_map/ppermute | solution.py:609
  52.4 9.6 %collective-permute-start.32 = (f32[18,8,512]{2,1,0:T(8,128)S(1)}, f32[18,8,512]{2,1,0:T(8,128)S(1)}, u32[]{:S(2)}, u32[]{:S(2)}) collective-permute-start(f32[18,8,512]{2,1,0:T(8,128)S(1)} %bitcast_add_fusion.11), channel_id=1, source_target_pairs={{0,4},{4,8},{8,12},{12,14},{14,10},{10,6},{6,2},{2,0},{1,3},{5,1},... | collective-permute-start | bytes 884744 | tf_op jit(solution)/shard_map/ppermute | solution.py:609
  55.6 9.6 %collective-permute-start.18 = (f32[18,8,512]{2,1,0:T(8,128)S(1)}, f32[18,8,512]{2,1,0:T(8,128)S(1)}, u32[]{:S(2)}, u32[]{:S(2)}) collective-permute-start(f32[18,8,512]{2,1,0:T(8,128)S(1)} %bitcast_add_fusion.17), channel_id=1, source_target_pairs={{0,4},{4,8},{8,12},{12,14},{14,10},{10,6},{6,2},{2,0},{1,3},{5,1},... | collective-permute-start | bytes 884744 | tf_op jit(solution)/shard_map/ppermute | solution.py:609
  58.9 9.6 %collective-permute-start.6 = (f32[19,8,512]{2,1,0:T(8,128)S(1)}, f32[19,8,512]{2,1,0:T(8,128)S(1)}, u32[]{:S(2)}, u32[]{:S(2)}) collective-permute-start(f32[19,8,512]{2,1,0:T(8,128)S(1)} %bitcast_add_fusion.4), channel_id=1, source_target_pairs={{0,4},{4,8},{8,12},{12,14},{14,10},{10,6},{6,2},{2,0},{1,3},{5,1},... | collective-permute-start | bytes 933896 | tf_op jit(solution)/shard_map/ppermute | solution.py:609
  62.1 9.6 %collective-permute-start.33 = (f32[18,8,512]{2,1,0:T(8,128)S(1)}, f32[18,8,512]{2,1,0:T(8,128)S(1)}, u32[]{:S(2)}, u32[]{:S(2)}) collective-permute-start(f32[18,8,512]{2,1,0:T(8,128)S(1)} %bitcast_add_fusion.10), channel_id=1, source_target_pairs={{0,4},{4,8},{8,12},{12,14},{14,10},{10,6},{6,2},{2,0},{1,3},{5,1},... | collective-permute-start | bytes 884744 | tf_op jit(solution)/shard_map/ppermute | solution.py:609
  65.2 9.6 %collective-permute-start.19 = (f32[18,8,512]{2,1,0:T(8,128)S(1)}, f32[18,8,512]{2,1,0:T(8,128)S(1)}, u32[]{:S(2)}, u32[]{:S(2)}) collective-permute-start(f32[18,8,512]{2,1,0:T(8,128)S(1)} %bitcast_add_fusion.16), channel_id=1, source_target_pairs={{0,4},{4,8},{8,12},{12,14},{14,10},{10,6},{6,2},{2,0},{1,3},{5,1},... | collective-permute-start | bytes 884744 | tf_op jit(solution)/shard_map/ppermute | solution.py:609
  68.6 9.6 %collective-permute-start.7 = (f32[19,8,512]{2,1,0:T(8,128)S(1)}, f32[19,8,512]{2,1,0:T(8,128)S(1)}, u32[]{:S(2)}, u32[]{:S(2)}) collective-permute-start(f32[19,8,512]{2,1,0:T(8,128)S(1)} %bitcast_add_fusion.3), channel_id=1, source_target_pairs={{0,4},{4,8},{8,12},{12,14},{14,10},{10,6},{6,2},{2,0},{1,3},{5,1},... | collective-permute-start | bytes 933896 | tf_op jit(solution)/shard_map/ppermute | solution.py:609
  71.7 9.6 %collective-permute-start.34 = (f32[18,8,512]{2,1,0:T(8,128)S(1)}, f32[18,8,512]{2,1,0:T(8,128)S(1)}, u32[]{:S(2)}, u32[]{:S(2)}) collective-permute-start(f32[18,8,512]{2,1,0:T(8,128)S(1)} %bitcast_add_fusion.9), channel_id=1, source_target_pairs={{0,4},{4,8},{8,12},{12,14},{14,10},{10,6},{6,2},{2,0},{1,3},{5,1},... | collective-permute-start | bytes 884744 | tf_op jit(solution)/shard_map/ppermute | solution.py:609
  74.9 14.9 %collective-permute-start.20 = (f32[18,8,512]{2,1,0:T(8,128)S(1)}, f32[18,8,512]{2,1,0:T(8,128)S(1)}, u32[]{:S(2)}, u32[]{:S(2)}) collective-permute-start(f32[18,8,512]{2,1,0:T(8,128)S(1)} %bitcast_add_fusion.15), channel_id=1, source_target_pairs={{0,4},{4,8},{8,12},{12,14},{14,10},{10,6},{6,2},{2,0},{1,3},{5,1},... | collective-permute-start | bytes 884744 | tf_op jit(solution)/shard_map/ppermute | solution.py:609
  78.2 9.9 %collective-permute-start.8 = (f32[19,8,512]{2,1,0:T(8,128)S(1)}, f32[19,8,512]{2,1,0:T(8,128)S(1)}, u32[]{:S(2)}, u32[]{:S(2)}) collective-permute-start(f32[19,8,512]{2,1,0:T(8,128)S(1)} %bitcast_add_fusion.2), channel_id=1, source_target_pairs={{0,4},{4,8},{8,12},{12,14},{14,10},{10,6},{6,2},{2,0},{1,3},{5,1},... | collective-permute-start | bytes 933896 | tf_op jit(solution)/shard_map/ppermute | solution.py:609
  81.4 10.1 %collective-permute-start.35 = (f32[18,8,512]{2,1,0:T(8,128)S(1)}, f32[18,8,512]{2,1,0:T(8,128)S(1)}, u32[]{:S(2)}, u32[]{:S(2)}) collective-permute-start(f32[18,8,512]{2,1,0:T(8,128)S(1)} %bitcast_add_fusion.8), channel_id=1, source_target_pairs={{0,4},{4,8},{8,12},{12,14},{14,10},{10,6},{6,2},{2,0},{1,3},{5,1},... | collective-permute-start | bytes 884744 | tf_op jit(solution)/shard_map/ppermute | solution.py:609
  89.9 8.4 %collective-permute-start.21 = (f32[18,8,512]{2,1,0:T(8,128)S(1)}, f32[18,8,512]{2,1,0:T(8,128)S(1)}, u32[]{:S(2)}, u32[]{:S(2)}) collective-permute-start(f32[18,8,512]{2,1,0:T(8,128)S(1)} %bitcast_add_fusion.14), channel_id=1, source_target_pairs={{0,4},{4,8},{8,12},{12,14},{14,10},{10,6},{6,2},{2,0},{1,3},{5,1},... | collective-permute-start | bytes 884744 | tf_op jit(solution)/shard_map/ppermute | solution.py:609
  91.6 9.9 %collective-permute-start.36 = (f32[18,8,512]{2,1,0:T(8,128)S(1)}, f32[18,8,512]{2,1,0:T(8,128)S(1)}, u32[]{:S(2)}, u32[]{:S(2)}) collective-permute-start(f32[18,8,512]{2,1,0:T(8,128)S(1)} %bitcast_add_fusion.7), channel_id=1, source_target_pairs={{0,4},{4,8},{8,12},{12,14},{14,10},{10,6},{6,2},{2,0},{1,3},{5,1},... | collective-permute-start | bytes 884744 | tf_op jit(solution)/shard_map/ppermute | solution.py:609
  95.2 9.6 %collective-permute-start.10 = (f32[19,8,512]{2,1,0:T(8,128)S(1)}, f32[19,8,512]{2,1,0:T(8,128)S(1)}, u32[]{:S(2)}, u32[]{:S(2)}) collective-permute-start(f32[19,8,512]{2,1,0:T(8,128)S(1)} %bitcast_add_fusion), channel_id=1, source_target_pairs={{0,4},{4,8},{8,12},{12,14},{14,10},{10,6},{6,2},{2,0},{1,3},{5,1},... | collective-permute-start | bytes 933896 | tf_op jit(solution)/shard_map/ppermute | solution.py:609
  98.4 9.6 %collective-permute-start.23 = (f32[18,8,512]{2,1,0:T(8,128)S(1)}, f32[18,8,512]{2,1,0:T(8,128)S(1)}, u32[]{:S(2)}, u32[]{:S(2)}) collective-permute-start(f32[18,8,512]{2,1,0:T(8,128)S(1)} %bitcast_add_fusion.13), channel_id=1, source_target_pairs={{0,4},{4,8},{8,12},{12,14},{14,10},{10,6},{6,2},{2,0},{1,3},{5,1},... | collective-permute-start | bytes 884744 | tf_op jit(solution)/shard_map/ppermute | solution.py:609
  101.5 11.2 %collective-permute-start.37 = (f32[18,8,512]{2,1,0:T(8,128)S(1)}, f32[18,8,512]{2,1,0:T(8,128)S(1)}, u32[]{:S(2)}, u32[]{:S(2)}) collective-permute-start(f32[18,8,512]{2,1,0:T(8,128)S(1)} %bitcast_add_fusion.6), channel_id=1, source_target_pairs={{0,1},{1,0},{2,3},{3,2},{4,5},{5,4},{6,7},{7,6},{8,9},{9,8},{10,11... | collective-permute-start | bytes 884744 | tf_op jit(solution)/shard_map/ppermute | solution.py:587
  101.6 9.5 %collective-permute-start.38 = (f32[18,8,512]{2,1,0:T(8,128)S(1)}, f32[18,8,512]{2,1,0:T(8,128)S(1)}, u32[]{:S(2)}, u32[]{:S(2)}) collective-permute-start(f32[18,8,512]{2,1,0:T(8,128)S(1)} %bitcast_add_fusion.6), channel_id=1, source_target_pairs={{0,4},{4,8},{8,12},{12,14},{14,10},{10,6},{6,2},{2,0},{1,3},{5,1},... | collective-permute-start | bytes 884744 | tf_op jit(solution)/shard_map/ppermute | solution.py:609
  104.9 9.4 %collective-permute-start.11 = (f32[18,8,512]{2,1,0:T(8,128)S(1)}, f32[18,8,512]{2,1,0:T(8,128)S(1)}, u32[]{:S(2)}, u32[]{:S(2)}) collective-permute-start(f32[18,8,512]{2,1,0:T(8,128)S(1)} %slice_add_fusion), channel_id=1, source_target_pairs={{0,4},{4,8},{8,12},{12,14},{14,10},{10,6},{6,2},{2,0},{1,3},{5,1},... | collective-permute-start | bytes 884744 | tf_op jit(solution)/shard_map/ppermute | solution.py:609
  108.0 9.5 %collective-permute-start.25 = (f32[18,8,512]{2,1,0:T(8,128)S(1)}, f32[18,8,512]{2,1,0:T(8,128)S(1)}, u32[]{:S(2)}, u32[]{:S(2)}) collective-permute-start(f32[18,8,512]{2,1,0:T(8,128)S(1)} %collective-permute-done.23), channel_id=1, source_target_pairs={{0,4},{4,8},{8,12},{12,14},{14,10},{10,6},{6,2},{2,0},{1,3},{5,1},... | collective-permute-start | bytes 884744 | tf_op jit(solution)/shard_map/ppermute | solution.py:609
  109.5 8.8 %collective-permute-start.22 = (f32[18,8,512]{2,1,0:T(8,128)S(1)}, f32[18,8,512]{2,1,0:T(8,128)S(1)}, u32[]{:S(2)}, u32[]{:S(2)}) collective-permute-start(f32[18,8,512]{2,1,0:T(8,128)S(1)} %bitcast_add_fusion.13), channel_id=1, source_target_pairs={{0,1},{1,0},{2,3},{3,2},{4,5},{5,4},{6,7},{7,6},{8,9},{9,8},{10,11... | collective-permute-start | bytes 884744 | tf_op jit(solution)/shard_map/ppermute | solution.py:587
  111.1 9.5 %collective-permute-start.40 = (f32[18,8,512]{2,1,0:T(8,128)S(1)}, f32[18,8,512]{2,1,0:T(8,128)S(1)}, u32[]{:S(2)}, u32[]{:S(2)}) collective-permute-start(f32[18,8,512]{2,1,0:T(8,128)S(1)} %collective-permute-done.38), channel_id=1, source_target_pairs={{0,4},{4,8},{8,12},{12,14},{14,10},{10,6},{6,2},{2,0},{1,3},{5,1},... | collective-permute-start | bytes 884744 | tf_op jit(solution)/shard_map/ppermute | solution.py:609
  112.7 9.5 %collective-permute-start.39 = (f32[18,8,512]{2,1,0:T(8,128)S(1)}, f32[18,8,512]{2,1,0:T(8,128)S(1)}, u32[]{:S(2)}, u32[]{:S(2)}) collective-permute-start(f32[18,8,512]{2,1,0:T(8,128)S(1)} %collective-permute-done.38), channel_id=1, source_target_pairs={{0,1},{1,0},{2,3},{3,2},{4,5},{5,4},{6,7},{7,6},{8,9},{9,8},{10,11... | collective-permute-start | bytes 884744 | tf_op jit(solution)/shard_map/ppermute | solution.py:587
  114.3 9.5 %collective-permute-start.12 = (f32[18,8,512]{2,1,0:T(8,128)S(1)}, f32[18,8,512]{2,1,0:T(8,128)S(1)}, u32[]{:S(2)}, u32[]{:S(2)}) collective-permute-start(f32[18,8,512]{2,1,0:T(8,128)S(1)} %collective-permute-done.11), channel_id=1, source_target_pairs={{0,4},{4,8},{8,12},{12,14},{14,10},{10,6},{6,2},{2,0},{1,3},{5,1},... | collective-permute-start | bytes 884744 | tf_op jit(solution)/shard_map/ppermute | solution.py:609
  117.4 7.9 %collective-permute-start.48 = (f32[18,8,512]{2,1,0:T(8,128)S(1)}, f32[18,8,512]{2,1,0:T(8,128)S(1)}, u32[]{:S(2)}, u32[]{:S(2)}) collective-permute-start(f32[18,8,512]{2,1,0:T(8,128)S(1)} %slice_add_fusion), channel_id=1, source_target_pairs={{0,1},{1,0},{2,3},{3,2},{4,5},{5,4},{6,7},{7,6},{8,9},{9,8},{10,11... | collective-permute-start | bytes 884744 | tf_op jit(solution)/shard_map/ppermute | solution.py:587
  118.3 8.6 %collective-permute-start.27 = (f32[18,8,512]{2,1,0:T(8,128)S(1)}, f32[18,8,512]{2,1,0:T(8,128)S(1)}, u32[]{:S(2)}, u32[]{:S(2)}) collective-permute-start(f32[18,8,512]{2,1,0:T(8,128)S(1)} %collective-permute-done.25), channel_id=1, source_target_pairs={{0,4},{4,8},{8,12},{12,14},{14,10},{10,6},{6,2},{2,0},{1,3},{5,1},... | collective-permute-start | bytes 884744 | tf_op jit(solution)/shard_map/ppermute | solution.py:609
  120.6 9.5 %collective-permute-start.42 = (f32[18,8,512]{2,1,0:T(8,128)S(1)}, f32[18,8,512]{2,1,0:T(8,128)S(1)}, u32[]{:S(2)}, u32[]{:S(2)}) collective-permute-start(f32[18,8,512]{2,1,0:T(8,128)S(1)} %collective-permute-done.40), channel_id=1, source_target_pairs={{0,4},{4,8},{8,12},{12,14},{14,10},{10,6},{6,2},{2,0},{1,3},{5,1},... | collective-permute-start | bytes 884744 | tf_op jit(solution)/shard_map/ppermute | solution.py:609
  122.2 7.9 %collective-permute-start.49 = (f32[18,8,512]{2,1,0:T(8,128)S(1)}, f32[18,8,512]{2,1,0:T(8,128)S(1)}, u32[]{:S(2)}, u32[]{:S(2)}) collective-permute-start(f32[18,8,512]{2,1,0:T(8,128)S(1)} %collective-permute-done.11), channel_id=1, source_target_pairs={{0,1},{1,0},{2,3},{3,2},{4,5},{5,4},{6,7},{7,6},{8,9},{9,8},{10,11... | collective-permute-start | bytes 884744 | tf_op jit(solution)/shard_map/ppermute | solution.py:587
  123.8 9.5 %collective-permute-start.13 = (f32[18,8,512]{2,1,0:T(8,128)S(1)}, f32[18,8,512]{2,1,0:T(8,128)S(1)}, u32[]{:S(2)}, u32[]{:S(2)}) collective-permute-start(f32[18,8,512]{2,1,0:T(8,128)S(1)} %collective-permute-done.12), channel_id=1, source_target_pairs={{0,4},{4,8},{8,12},{12,14},{14,10},{10,6},{6,2},{2,0},{1,3},{5,1},... | collective-permute-start | bytes 884744 | tf_op jit(solution)/shard_map/ppermute | solution.py:609
  125.3 7.9 %collective-permute-start.50 = (f32[18,8,512]{2,1,0:T(8,128)S(1)}, f32[18,8,512]{2,1,0:T(8,128)S(1)}, u32[]{:S(2)}, u32[]{:S(2)}) collective-permute-start(f32[18,8,512]{2,1,0:T(8,128)S(1)} %collective-permute-done.12), channel_id=1, source_target_pairs={{0,1},{1,0},{2,3},{3,2},{4,5},{5,4},{6,7},{7,6},{8,9},{9,8},{10,11... | collective-permute-start | bytes 884744 | tf_op jit(solution)/shard_map/ppermute | solution.py:587
  126.9 9.2 %collective-permute-start.24 = (f32[18,8,512]{2,1,0:T(8,128)S(1)}, f32[18,8,512]{2,1,0:T(8,128)S(1)}, u32[]{:S(2)}, u32[]{:S(2)}) collective-permute-start(f32[18,8,512]{2,1,0:T(8,128)S(1)} %collective-permute-done.23), channel_id=1, source_target_pairs={{0,1},{1,0},{2,3},{3,2},{4,5},{5,4},{6,7},{7,6},{8,9},{9,8},{10,11... | collective-permute-start | bytes 884744 | tf_op jit(solution)/shard_map/ppermute | solution.py:587
  137.7 8.6 %collective-permute-start.28 = (f32[18,8,512]{2,1,0:T(8,128)S(1)}, f32[18,8,512]{2,1,0:T(8,128)S(1)}, u32[]{:S(2)}, u32[]{:S(2)}) collective-permute-start(f32[18,8,512]{2,1,0:T(8,128)S(1)} %collective-permute-done.27), channel_id=1, source_target_pairs={{0,1},{1,0},{2,3},{3,2},{4,5},{5,4},{6,7},{7,6},{8,9},{9,8},{10,11... | collective-permute-start | bytes 884744 | tf_op jit(solution)/shard_map/ppermute | solution.py:587
  138.3 8.1 %collective-permute-start.30 = (f32[18,8,512]{2,1,0:T(8,128)S(1)}, f32[18,8,512]{2,1,0:T(8,128)S(1)}, u32[]{:S(2)}, u32[]{:S(2)}) collective-permute-start(f32[18,8,512]{2,1,0:T(8,128)S(1)} %collective-permute-done.29), channel_id=1, source_target_pairs={{0,1},{1,0},{2,3},{3,2},{4,5},{5,4},{6,7},{7,6},{8,9},{9,8},{10,11... | collective-permute-start | bytes 884744 | tf_op jit(solution)/shard_map/ppermute | solution.py:587
  144.7 8.3 %collective-permute-start.62 = (f32[18,8,512]{2,1,0:T(8,128)S(1)}, f32[18,8,512]{2,1,0:T(8,128)S(1)}, u32[]{:S(2)}, u32[]{:S(2)}) collective-permute-start(f32[18,8,512]{2,1,0:T(8,128)S(1)} %collective-permute-done.29), channel_id=1, source_target_pairs={{0,4},{4,8},{8,12},{12,14},{14,10},{10,6},{6,2},{2,0},{1,3},{5,1},... | collective-permute-start | bytes 884744 | tf_op jit(solution)/shard_map/ppermute | solution.py:609
  146.3 8.3 %collective-permute-start.55 = (f32[18,8,512]{2,1,0:T(8,128)S(1)}, f32[18,8,512]{2,1,0:T(8,128)S(1)}, u32[]{:S(2)}, u32[]{:S(2)}) collective-permute-start(f32[18,8,512]{2,1,0:T(8,128)S(1)} %collective-permute-done.13), channel_id=1, source_target_pairs={{0,1},{1,0},{2,3},{3,2},{4,5},{5,4},{6,7},{7,6},{8,9},{9,8},{10,11... | collective-permute-start | bytes 884744 | tf_op jit(solution)/shard_map/ppermute | solution.py:587
  146.3 8.3 %collective-permute-start.56 = (f32[18,8,512]{2,1,0:T(8,128)S(1)}, f32[18,8,512]{2,1,0:T(8,128)S(1)}, u32[]{:S(2)}, u32[]{:S(2)}) collective-permute-start(f32[18,8,512]{2,1,0:T(8,128)S(1)} %collective-permute-done.14), channel_id=1, source_target_pairs={{0,1},{1,0},{2,3},{3,2},{4,5},{5,4},{6,7},{7,6},{8,9},{9,8},{10,11... | collective-permute-start | bytes 884744 | tf_op jit(solution)/shard_map/ppermute | solution.py:587
  146.8 8.3 %collective-permute-start.57 = (f32[18,8,512]{2,1,0:T(8,128)S(1)}, f32[18,8,512]{2,1,0:T(8,128)S(1)}, u32[]{:S(2)}, u32[]{:S(2)}) collective-permute-start(f32[18,8,512]{2,1,0:T(8,128)S(1)} %collective-permute-done.15), channel_id=1, source_target_pairs={{0,1},{1,0},{2,3},{3,2},{4,5},{5,4},{6,7},{7,6},{8,9},{9,8},{10,11... | collective-permute-start | bytes 884744 | tf_op jit(solution)/shard_map/ppermute | solution.py:587
  149.9 8.1 %collective-permute-start.53 = (f32[18,8,512]{2,1,0:T(8,128)S(1)}, f32[18,8,512]{2,1,0:T(8,128)S(1)}, u32[]{:S(2)}, u32[]{:S(2)}) collective-permute-start(f32[18,8,512]{2,1,0:T(8,128)S(1)} %collective-permute-done.52), channel_id=1, source_target_pairs={{0,4},{4,8},{8,12},{12,14},{14,10},{10,6},{6,2},{2,0},{1,3},{5,1},... | collective-permute-start | bytes 884744 | tf_op jit(solution)/shard_map/ppermute | solution.py:609
  155.1 7.8 %collective-permute-start.64 = (f32[18,8,512]{2,1,0:T(8,128)S(1)}, f32[18,8,512]{2,1,0:T(8,128)S(1)}, u32[]{:S(2)}, u32[]{:S(2)}) collective-permute-start(f32[18,8,512]{2,1,0:T(8,128)S(1)} %collective-permute-done.62), channel_id=1, source_target_pairs={{0,4},{4,8},{8,12},{12,14},{14,10},{10,6},{6,2},{2,0},{1,3},{5,1},... | collective-permute-start | bytes 884744 | tf_op jit(solution)/shard_map/ppermute | solution.py:609
  158.0 11.3 %collective-permute-start.58 = (f32[18,8,512]{2,1,0:T(8,128)S(1)}, f32[18,8,512]{2,1,0:T(8,128)S(1)}, u32[]{:S(2)}, u32[]{:S(2)}) collective-permute-start(f32[18,8,512]{2,1,0:T(8,128)S(1)} %collective-permute-done.53), channel_id=1, source_target_pairs={{0,4},{4,8},{8,12},{12,14},{14,10},{10,6},{6,2},{2,0},{1,3},{5,1},... | collective-permute-start | bytes 884744 | tf_op jit(solution)/shard_map/ppermute | solution.py:609
  159.7 9.5 %collective-permute-start.46 = (f32[18,8,512]{2,1,0:T(8,128)S(1)}, f32[18,8,512]{2,1,0:T(8,128)S(1)}, u32[]{:S(2)}, u32[]{:S(2)}) collective-permute-start(f32[18,8,512]{2,1,0:T(8,128)S(1)} %collective-permute-done.44), channel_id=1, source_target_pairs={{0,4},{4,8},{8,12},{12,14},{14,10},{10,6},{6,2},{2,0},{1,3},{5,1},... | collective-permute-start | bytes 884744 | tf_op jit(solution)/shard_map/ppermute | solution.py:609
  163.0 9.4 %collective-permute-start.66 = (f32[18,8,512]{2,1,0:T(8,128)S(1)}, f32[18,8,512]{2,1,0:T(8,128)S(1)}, u32[]{:S(2)}, u32[]{:S(2)}) collective-permute-start(f32[18,8,512]{2,1,0:T(8,128)S(1)} %collective-permute-done.64), channel_id=1, source_target_pairs={{0,4},{4,8},{8,12},{12,14},{14,10},{10,6},{6,2},{2,0},{1,3},{5,1},... | collective-permute-start | bytes 884744 | tf_op jit(solution)/shard_map/ppermute | solution.py:609
  (26 other events, 178.2 us)
